TPU v7x, 32 devices: a whole 2x2x4 slice. The times are simulated.
32 devices in a mesh: row: 8 (over z, y), col: 4 (over x, core).
Axes of the slice: x: 2, y: 2, z: 4, core: 2. Of those that a mesh axis runs over, the one named last changes fastest.
Arguments:
- layer_input: float32 [768, 8192], P('col', 'row'), may hold values from -6 to 6
- ln1_gain: float32 [768], P('col'), may hold values from 0.25 to 1.75
- ln1_bias: float32 [768], P('col'), may hold values from -3 to 3
- w_query: bfloat16 [768, 768], P('row', 'col'), may hold values from -0.21875 to 0.21875
- w_key: bfloat16 [768, 768], P('row', 'col'), may hold values from -0.21875 to 0.21875
- w_value: bfloat16 [768, 768], P('row', 'col'), may hold values from -0.21875 to 0.21875
- b_query: float32 [768], P('col'), may hold values from -3 to 3
- b_value: float32 [768], P('col'), may hold values from -3 to 3
- w_out: bfloat16 [768, 768], P('col', 'row'), may hold values from -2.5 to 2.5
- b_out: float32 [768], P('col'), may hold values from -3 to 3
- ln2_gain: float32 [768], P('col'), may hold values from 0.25 to 1.75
- ln2_bias: float32 [768], P('col'), may hold values from -3 to 3
- w_fc1: bfloat16 [768, 3072], P('row', 'col')
- b_fc1: float32 [3072], P('col'), may hold values from -3 to 3
- w_fc2: bfloat16 [3072, 768], P('col', 'row'), may hold values from -0.109375 to 0.109375
- b_fc2: float32 [768], P('col'), may hold values from -3 to 3
- seq_lengths: int32 [8, 3], P('row'), may hold values from 1 to 1022, as said below
- cotangent: float32 [768, 8192], P('col', 'row'), may hold values from -6 to 6
Outputs:
- output: float32 [768, 8192], P('col', 'row')
- grad_input: float32 [768, 8192], P('col', 'row')
- grad_ln1_gain: float32 [768], P('col')
- grad_ln1_bias: float32 [768], P('col')
- grad_w_query: float32 [768, 768], P('row', 'col')
- grad_w_key: float32 [768, 768], P('row', 'col')
- grad_w_value: float32 [768, 768], P('row', 'col')
- grad_b_query: float32 [768], P('col')
- grad_b_value: float32 [768], P('col')
- grad_w_out: float32 [768, 768], P('col', 'row')
- grad_b_out: float32 [768], P('col')
- grad_ln2_gain: float32 [768], P('col')
- grad_ln2_bias: float32 [768], P('col')
- grad_w_fc1: float32 [768, 3072], P('row', 'col')
- grad_b_fc1: float32 [3072], P('col')
- grad_w_fc2: float32 [3072, 768], P('col', 'row')
- grad_b_fc2: float32 [768], P('col')
Inputs may be any that keep to these rules, and one draw needn't show every extreme that they name: `seq_lengths`: row p lists the lengths of the 3 sequences packed in this order into pack p; they sum to at most 1024, and the remaining positions are padding. In every pack the second sequence starts within the first 256 positions and ends within the last 256 positions.
All inputs are finite; a program needn't handle non-finite values.
Results may differ from a plain program's by a relative error of at most 0.017.
Values may be sent and summed in bfloat16 or wider, within the bound.
A program may use at most 128 MiB of HBM per device.

v0:
```python
import jax
import jax.numpy as jnp
from jax import lax
from jax.sharding import PartitionSpec as P

HEADS = 12
HEAD_DIM = 64


EPS = 1e-05
NEG = -1e30


def to_half(values):
    return values.astype(jnp.bfloat16)


def product(first_op, second_op):
    return jnp.dot(first_op, second_op, preferred_element_type=jnp.float32)


def product_left(first_op, second_op):
    return lax.dot_general(
        first_op, second_op, (((0,), (0,)), ((), ())), preferred_element_type=jnp.float32
    )


def product_right(first_op, second_op):
    return lax.dot_general(
        first_op, second_op, (((1,), (1,)), ((), ())), preferred_element_type=jnp.float32
    )


def column_sum(values):
    return jnp.sum(values.astype(jnp.float32), axis=0)


def smooth_gate(values):
    return jax.nn.gelu(values, approximate=True)


def query_positions(pack_rows):
    col_count = lax.axis_size("col")
    col_index = lax.axis_index("col")
    share_rows = pack_rows // col_count
    return col_index * share_rows + jnp.arange(share_rows, dtype=jnp.int32)


def feature_rows(block_rows):
    return lax.all_gather(block_rows, "col", axis=1, tiled=True)


def feature_sums(partial_value):
    return lax.psum_scatter(partial_value, "col", scatter_dimension=1, tiled=True)


def to_heads(block_rows):
    return lax.all_to_all(block_rows, "col", split_axis=0, concat_axis=1, tiled=True)


def to_features(block_rows):
    spread = lax.all_to_all(block_rows, "col", split_axis=1, concat_axis=0, tiled=True)
    return spread


def norm_forward(block_rows, norm_gain, norm_shift):
    local_width = block_rows.shape[1]
    full_width = local_width * lax.axis_size("col")
    row_sums, row_squares = lax.psum(
        (jnp.sum(block_rows, axis=1), jnp.sum(block_rows * block_rows, axis=1)), "col"
    )
    row_mean = (row_sums / full_width)[:, None]
    variance = (row_squares / full_width)[:, None] - row_mean * row_mean
    row_scale = lax.rsqrt(variance + EPS)
    scaled = (block_rows - row_mean) * row_scale
    normed = feature_rows(to_half(scaled * norm_gain + norm_shift))
    return (normed, scaled, row_scale)


def norm_backward(upstream, scaled, row_scale, norm_gain):
    full_width = upstream.shape[1] * lax.axis_size("col")
    weighted = upstream * norm_gain
    row_sums, row_along = lax.psum(
        (jnp.sum(weighted, axis=1), jnp.sum(weighted * scaled, axis=1)), "col"
    )
    grad_rows = row_scale * (
        weighted - (row_sums / full_width)[:, None] - scaled * (row_along / full_width)[:, None]
    )
    return (grad_rows, jnp.sum(upstream * scaled, axis=0), jnp.sum(upstream, axis=0))


def split_heads(block_rows):
    return block_rows.reshape(block_rows.shape[0], HEADS, HEAD_DIM)


def masked_scores(queries, all_keys, query_pos, segment):
    scores = jnp.einsum(
        "qhd,khd->hqk",
        split_heads(queries),
        split_heads(all_keys),
        preferred_element_type=jnp.float32,
    )
    key_pos = jnp.arange(all_keys.shape[0], dtype=jnp.int32)
    allowed = (segment[query_pos][:, None] == segment[None, :]) & (
        key_pos[None, :] <= query_pos[:, None]
    )
    return jnp.where(allowed[None], scores, NEG)


def attention_forward(queries, all_keys, all_values, query_pos, segment):
    scores = masked_scores(queries, all_keys, query_pos, segment)
    row_top = jnp.max(scores, axis=2, keepdims=True)
    expo_vals = jnp.exp(scores - row_top)
    row_total = jnp.sum(expo_vals, axis=2, keepdims=True)
    attn_probs = to_half(expo_vals / row_total)
    mixed = jnp.einsum(
        "hqk,khd->qhd", attn_probs, split_heads(all_values), preferred_element_type=jnp.float32
    )
    return (mixed.reshape(queries.shape[0], -1), row_top + jnp.log(row_total))


def attention_backward(queries, all_keys, all_values, query_pos, segment, log_total, grad_mixed):
    scores = masked_scores(queries, all_keys, query_pos, segment)
    attn_probs = jnp.exp(scores - log_total)
    grad_heads = split_heads(grad_mixed)
    grad_probs = jnp.einsum(
        "qhd,khd->hqk", grad_heads, split_heads(all_values), preferred_element_type=jnp.float32
    )
    row_inner = jnp.sum(attn_probs * grad_probs, axis=2, keepdims=True)
    grad_scores = to_half(attn_probs * (grad_probs - row_inner))
    grad_queries = jnp.einsum(
        "hqk,khd->qhd", grad_scores, split_heads(all_keys), preferred_element_type=jnp.float32
    )
    grad_keys = jnp.einsum(
        "hqk,qhd->khd", grad_scores, split_heads(queries), preferred_element_type=jnp.float32
    )
    grad_values = jnp.einsum(
        "hqk,qhd->khd", to_half(attn_probs), grad_heads, preferred_element_type=jnp.float32
    )
    key_count = all_keys.shape[0]
    return (
        grad_queries.reshape(queries.shape[0], -1),
        grad_keys.reshape(key_count, -1),
        grad_values.reshape(key_count, -1),
    )


def shards(
    layer_input,
    ln1_gain,
    ln1_bias,
    w_query,
    w_key,
    w_value,
    b_query,
    b_value,
    w_out,
    b_out,
    ln2_gain,
    ln2_bias,
    w_fc1,
    b_fc1,
    w_fc2,
    b_fc2,
    seq_lengths,
    cotangent,
):
    scaling = HEAD_DIM ** (-0.5)
    input_rows = layer_input.T
    cotangent_rows = cotangent.T
    pack_rows = input_rows.shape[0]
    seq_ends = jnp.cumsum(seq_lengths[0])
    places = jnp.arange(pack_rows, dtype=jnp.int32)
    segment = jnp.sum((places[:, None] >= seq_ends[None, :]).astype(jnp.int32), axis=1)
    query_pos = query_positions(pack_rows)
    gathered = (
        lax.all_gather(w_query, "row", axis=0, tiled=True),
        lax.all_gather(w_key, "row", axis=0, tiled=True),
        lax.all_gather(w_value, "row", axis=0, tiled=True),
        lax.all_gather(w_fc1, "row", axis=0, tiled=True),
        lax.all_gather(w_out.T, "row", axis=0, tiled=True),
        lax.all_gather(w_fc2.T, "row", axis=0, tiled=True),
    )
    full_query, full_key, full_value, full_fc1, full_out, full_fc2 = gathered
    normed1, scaled1, scale1 = norm_forward(input_rows, ln1_gain, ln1_bias)
    query_part = to_half((product(normed1, full_query) + b_query) * scaling)
    key_part = to_half(product(normed1, full_key))
    value_part = to_half(product(normed1, full_value) + b_value)
    queries = to_heads(query_part)
    all_keys, all_values = (
        lax.all_gather(key_part, "col", axis=1, tiled=True),
        lax.all_gather(value_part, "col", axis=1, tiled=True),
    )
    attended, log_total = attention_forward(queries, all_keys, all_values, query_pos, segment)
    spread = to_features(to_half(attended))
    middle = input_rows + feature_sums(product_right(spread, full_out)) + b_out
    normed2, scaled2, scale2 = norm_forward(middle, ln2_gain, ln2_bias)
    hidden_pre = product(normed2, full_fc1) + b_fc1
    activated, gate_pull = jax.vjp(smooth_gate, hidden_pre)
    hidden = to_half(activated)
    output = middle + feature_sums(product_right(hidden, full_fc2)) + b_fc2
    grad_mlp = to_half(cotangent_rows)
    grad_mlp_full = feature_rows(grad_mlp)
    grad_hidden = product(grad_mlp_full, full_fc2)
    grad_pre = to_half(gate_pull(grad_hidden)[0])
    grad_fc2_t = product_left(grad_mlp_full, hidden)
    grad_fc1 = product_left(normed2, grad_pre)
    grad_normed2 = feature_sums(product_right(grad_pre, full_fc1))
    back_second, gain2_grad, shift2_grad = norm_backward(grad_normed2, scaled2, scale2, ln2_gain)
    grad_middle = cotangent_rows + back_second
    grad_branch = to_half(grad_middle)
    grad_branch_full = feature_rows(grad_branch)
    grad_out_t = product_left(grad_branch_full, spread)
    grad_spread = to_half(product(grad_branch_full, full_out))
    grad_attended = to_heads(grad_spread)
    grad_q_heads, grad_k_part, grad_v_part = attention_backward(
        queries, all_keys, all_values, query_pos, segment, log_total, grad_attended
    )
    grad_query_raw = to_features(to_half(grad_q_heads)).astype(jnp.float32) * scaling
    grad_query = to_half(grad_query_raw)
    key_total, value_total = (
        lax.psum_scatter(
            grad_k_part.astype(jnp.bfloat16), "col", scatter_dimension=1, tiled=True
        ).astype(jnp.float32),
        lax.psum_scatter(
            grad_v_part.astype(jnp.bfloat16), "col", scatter_dimension=1, tiled=True
        ).astype(jnp.float32),
    )
    grad_key = to_half(key_total)
    grad_value = to_half(value_total)
    grad_normed1 = feature_sums(
        product_right(grad_query, full_query)
        + product_right(grad_key, full_key)
        + product_right(grad_value, full_value)
    )
    back_first, gain1_grad, shift1_grad = norm_backward(grad_normed1, scaled1, scale1, ln1_gain)
    grad_input = grad_middle + back_first
    weight_sums = (
        lax.psum_scatter(
            product_left(normed1, grad_query).astype(jnp.bfloat16),
            "row",
            scatter_dimension=0,
            tiled=True,
        ).astype(jnp.float32),
        lax.psum_scatter(
            product_left(normed1, grad_key).astype(jnp.bfloat16),
            "row",
            scatter_dimension=0,
            tiled=True,
        ).astype(jnp.float32),
        lax.psum_scatter(
            product_left(normed1, grad_value).astype(jnp.bfloat16),
            "row",
            scatter_dimension=0,
            tiled=True,
        ).astype(jnp.float32),
        lax.psum_scatter(
            grad_out_t.astype(jnp.bfloat16), "row", scatter_dimension=0, tiled=True
        ).astype(jnp.float32),
        lax.psum_scatter(
            grad_fc1.astype(jnp.bfloat16), "row", scatter_dimension=0, tiled=True
        ).astype(jnp.float32),
        lax.psum_scatter(
            grad_fc2_t.astype(jnp.bfloat16), "row", scatter_dimension=0, tiled=True
        ).astype(jnp.float32),
    )
    vector_sums = lax.psum(
        (
            gain1_grad,
            shift1_grad,
            column_sum(grad_query_raw),
            column_sum(grad_value),
            column_sum(grad_branch),
            gain2_grad,
            shift2_grad,
            column_sum(grad_pre),
            column_sum(grad_mlp),
        ),
        "row",
    )
    return (
        output.T,
        grad_input.T,
        vector_sums[0],
        vector_sums[1],
        weight_sums[0],
        weight_sums[1],
        weight_sums[2],
        vector_sums[2],
        vector_sums[3],
        weight_sums[3].T,
        vector_sums[4],
        vector_sums[5],
        vector_sums[6],
        weight_sums[4],
        vector_sums[7],
        weight_sums[5].T,
        vector_sums[8],
    )


def solution(mesh):
    in_specs = (
        P("col", "row"),
        P("col"),
        P("col"),
        P("row", "col"),
        P("row", "col"),
        P("row", "col"),
        P("col"),
        P("col"),
        P("col", "row"),
        P("col"),
        P("col"),
        P("col"),
        P("row", "col"),
        P("col"),
        P("col", "row"),
        P("col"),
        P("row", None),
        P("col", "row"),
    )
    out_specs = (
        P("col", "row"),
        P("col", "row"),
        P("col"),
        P("col"),
        P("row", "col"),
        P("row", "col"),
        P("row", "col"),
        P("col"),
        P("col"),
        P("col", "row"),
        P("col"),
        P("col"),
        P("col"),
        P("row", "col"),
        P("col"),
        P("col", "row"),
        P("col"),
    )
    return jax.shard_map(shards, mesh=mesh, in_specs=in_specs, out_specs=out_specs, check_vma=False)
```

profile of v0, /device:TPU:8, one launch (start us, length us, event | category | flops | bytes accessed | tf_op | source)
XLA Modules:
  0.0 993.6 jit_solution(18135864687984033314)
XLA Ops:
  10.5 7.0 all-reduce.4
  17.6 2.1 add_convert_fusion.1
  19.8 28.8 %all_gather.40 = bf16[768,192]{1,0:T(8,128)(2,1)S(1)} all-gather(bf16[96,192]{1,0:T(8,128)(2,1)S(1)} %copy-done.16), channel_id=1, replica_groups=mesh['row'=8,'col'=4] {'row'}, dimensions={0}, use_global_device_ids=true | all-gather | bytes 331776 | tf_op jit(solution)/shard_map/all_gather | solution.py:178
  48.6 2.9 convolution_convert_fusion.9
  51.7 31.2 %all_gather.37 = bf16[768,192]{1,0:T(8,128)(2,1)S(1)} all-gather(bf16[96,192]{1,0:T(8,128)(2,1)S(1)} %copy-done.17), channel_id=1, replica_groups=mesh['row'=8,'col'=4] {'row'}, dimensions={0}, use_global_device_ids=true | all-gather | bytes 331776 | tf_op jit(solution)/shard_map/all_gather | solution.py:179
  85.7 31.0 %all_gather.39 = bf16[768,192]{1,0:T(8,128)(2,1)S(1)} all-gather(bf16[96,192]{1,0:T(8,128)(2,1)S(1)} %copy-done.18), channel_id=1, replica_groups=mesh['row'=8,'col'=4] {'row'}, dimensions={0}, use_global_device_ids=true | all-gather | bytes 331776 | tf_op jit(solution)/shard_map/all_gather | solution.py:177
  118.0 3.5 all-to-all-start
  121.8 7.0 all-to-all-done
  128.9 3.5 select_reduce_fusion
  132.3 4.6 copy-done
  136.9 3.2 fusion
  140.1 7.4 fusion.22
  147.6 3.5 all-to-all-start.1
  151.2 31.0 %all_gather.42 = bf16[768,192]{1,0:T(8,128)(2,1)S(1)} all-gather(bf16[96,192]{1,0:T(8,128)(2,1)S(1)} %bitcast.136), channel_id=1, replica_groups=mesh['row'=8,'col'=4] {'row'}, dimensions={0}, use_global_device_ids=true | all-gather | bytes 331776 | tf_op jit(solution)/shard_map/all_gather | solution.py:181
  182.3 2.3 fusion.38
  185.3 41.4 %reduce-scatter.15.cloned.1.call-done = f32[1024,192]{0,1:T(8,128)} async-done(((f32[1024,768]{0,1:T(8,128)}), f32[1024,192]{0,1:T(8,128)}) %reduce-scatter.15.cloned.1.call-update) | async-done | bytes 786448 | tf_op jit(solution)/shard_map/reduce_scatter | solution.py:54
  228.0 6.1 all-reduce.3
  237.2 18.5 %all-gather.15.cloned.1.call-done = bf16[1024,768]{0,1:T(8,128)(2,1)} async-done(((bf16[1024,192]{0,1:T(8,128)(2,1)}), bf16[1024,768]{0,1:T(8,128)(2,1)}) %all-gather.15.cloned.1.call-update) | async-done | bytes 1572880 | tf_op jit(solution)/shard_map/all_gather | solution.py:50
  255.7 4.9 fusion.36
  260.5 38.0 %all-gather.19.cloned.1.call-done = bf16[768,768]{1,0:T(8,128)(2,1)} async-done(((bf16[96,768]{1,0:T(8,128)(2,1)}), bf16[768,768]{1,0:T(8,128)(2,1)}) %all-gather.19.cloned.1.call-update) | async-done | bytes 1179664 | tf_op jit(solution)/shard_map/all_gather | solution.py:182
  298.5 21.2 %all-gather.21.cloned.1.call-done = bf16[1024,768]{0,1:T(8,128)(2,1)} async-done(((bf16[1024,192]{0,1:T(8,128)(2,1)}), bf16[1024,768]{0,1:T(8,128)(2,1)}) %all-gather.21.cloned.1.call-update) | async-done | bytes 1572880 | tf_op jit(solution)/shard_map/all_gather | solution.py:50
  319.8 6.1 convert_reduce_fusion
  327.1 3.1 fusion.37
  330.3 5.5 fusion.32
  335.8 32.4 %reduce-scatter.19.cloned.1.call-done = f32[1024,192]{0,1:T(8,128)} async-done(((f32[1024,768]{0,1:T(8,128)}), f32[1024,192]{0,1:T(8,128)}) %reduce-scatter.19.cloned.1.call-update) | async-done | bytes 786448 | tf_op jit(solution)/shard_map/reduce_scatter | solution.py:54
  368.2 1.5 multiply_reduce_fusion.1
  369.6 6.1 all-reduce.2
  375.8 32.8 %reduce-scatter.17.cloned.1.call-done = f32[1024,192]{0,1:T(8,128)} async-done(((f32[1024,768]{0,1:T(8,128)}), f32[1024,192]{0,1:T(8,128)}) %reduce-scatter.17.cloned.1.call-update) | async-done | bytes 786448 | tf_op jit(solution)/shard_map/reduce_scatter | solution.py:54
  408.6 3.0 convert_reduce_fusion.2
  411.6 19.8 %all-gather.23.cloned.1.call-done = bf16[1024,768]{0,1:T(8,128)(2,1)} async-done(((bf16[1024,192]{0,1:T(8,128)(2,1)}), bf16[1024,768]{0,1:T(8,128)(2,1)}) %all-gather.23.cloned.1.call-update) | async-done | bytes 1572880 | tf_op jit(solution)/shard_map/all_gather | solution.py:50
  431.4 2.0 convolution_convert_fusion.8
  434.2 3.5 all-to-all-start.2
  437.7 7.3 all-to-all-done.2
  445.0 7.7 fusion.15
  452.9 7.7 multiply_reduce_fusion
  460.6 6.7 multiply_convert_fusion
  467.3 3.0 convolution_convert_fusion
  470.7 4.7 fusion.18
  475.4 1.5 copy.59
  476.9 4.4 convolution_convert_fusion.2
  481.4 5.6 convolution_convert_fusion.7
  487.0 3.5 all-to-all-start.3
  490.6 3.0 convolution_convert_fusion.3
  493.6 4.3 all-to-all-done.3
  498.1 2.8 convolution_convert_fusion.6
  501.0 2.8 convolution_convert_fusion.4
  504.2 2.2 fusion.39
  506.4 5.4 reduce-scatter.21.cloned.1.call-done
  511.8 2.9 convolution_convert_fusion.5
  516.7 2.3 add_add_fusion
  519.0 60.6 %reduce-scatter.37.cloned.1.call-done = bf16[96,768]{1,0:T(8,128)(2,1)} async-done(((bf16[768,768]{1,0:T(8,128)(2,1)}), bf16[96,768]{1,0:T(8,128)(2,1)}) %reduce-scatter.37.cloned.1.call-update) | async-done | bytes 147472
  581.6 64.9 %reduce-scatter.35.cloned.1.call-done = bf16[96,768]{1,0:T(8,128)(2,1)} async-done(((bf16[768,768]{1,0:T(8,128)(2,1)}), bf16[96,768]{1,0:T(8,128)(2,1)}) %reduce-scatter.35.cloned.1.call-update) | async-done | bytes 147472 | tf_op jit(solution)/shard_map/reduce_scatter | solution.py:260
  646.4 1.6 convert_element_type.187
  648.1 62.3 %reduce-scatter.33.cloned.1.call-done = bf16[96,192]{1,0:T(8,128)(2,1)} async-done(((bf16[768,192]{1,0:T(8,128)(2,1)}), bf16[96,192]{1,0:T(8,128)(2,1)}) %reduce-scatter.33.cloned.1.call-update) | async-done | bytes 36880 | tf_op jit(solution)/shard_map/reduce_scatter | solution.py:257
  711.9 62.5 %reduce-scatter.27.cloned.1.call-done = bf16[96,192]{1,0:T(8,128)(2,1)} async-done(((bf16[768,192]{1,0:T(8,128)(2,1)}), bf16[96,192]{1,0:T(8,128)(2,1)}) %reduce-scatter.27.cloned.1.call-update) | async-done | bytes 36880 | tf_op jit(solution)/shard_map/reduce_scatter | solution.py:239
  774.4 1.4 convert_element_type.178
  776.0 62.3 %reduce-scatter.31.cloned.1.call-done = bf16[96,192]{1,0:T(8,128)(2,1)} async-done(((bf16[768,192]{1,0:T(8,128)(2,1)}), bf16[96,192]{1,0:T(8,128)(2,1)}) %reduce-scatter.31.cloned.1.call-update) | async-done | bytes 36880 | tf_op jit(solution)/shard_map/reduce_scatter | solution.py:251
  838.3 1.4 convert_element_type.182
  839.8 62.6 %reduce-scatter.29.cloned.1.call-done = bf16[96,192]{1,0:T(8,128)(2,1)} async-done(((bf16[768,192]{1,0:T(8,128)(2,1)}), bf16[96,192]{1,0:T(8,128)(2,1)}) %reduce-scatter.29.cloned.1.call-update) | async-done | bytes 36880 | tf_op jit(solution)/shard_map/reduce_scatter | solution.py:245
  903.8 38.2 %reduce-scatter.25.cloned.1.call-done = f32[1024,192]{0,1:T(8,128)} async-done(((f32[1024,768]{0,1:T(8,128)}), f32[1024,192]{0,1:T(8,128)}) %reduce-scatter.25.cloned.1.call-update) | async-done | bytes 786448 | tf_op jit(solution)/shard_map/reduce_scatter | solution.py:54
  942.0 1.5 multiply_reduce_fusion.2
  943.5 6.1 all-reduce.1
  949.6 34.4 %all-reduce = (f32[192]{0:T(256)}, f32[192]{0:T(256)}, f32[192]{0:T(256)}, f32[192]{0:T(256)}, f32[192]{0:T(256)}, /*index=5*/f32[192]{0:T(256)}, f32[192]{0:T(256)}, f32[768]{0:T(1024)}, f32[192]{0:T(256)}) all-reduce(f32[192]{0:T(256)S(1)} %get-tuple-element.87, ...), channel_id=1, replica_groups=mesh['row'=8,'col'=4] {'row'}, use_global_device_ids=true, to_apply=%region_28.29 | all-reduce | flops 2304 | bytes 18432 | tf_op jit(solution)/shard_map/psum | solution.py:267
  984.0 2.3 add_bitcast_fusion
  (143 shorter events, 22.9 us)
Async XLA Ops:
  8.0 11.7 %copy-start.16 = (bf16[96,192]{1,0:T(8,128)(2,1)S(1)}, bf16[96,192]{1,0:T(8,128)(2,1)}, u32[]{:S(2)}) copy-start(bf16[96,192]{1,0:T(8,128)(2,1)} %param.22) | copy-start | bytes 110596
  8.0 43.5 %copy-start.30 = (s32[1,3]{1,0:T(1,128)S(1)}, s32[1,3]{1,0:T(1,128)}, u32[]{:S(2)}) copy-start(s32[1,3]{1,0:T(1,128)} %param.34) | copy-start | bytes 40
  8.0 43.7 %copy-start.17 = (bf16[96,192]{1,0:T(8,128)(2,1)S(1)}, bf16[96,192]{1,0:T(8,128)(2,1)}, u32[]{:S(2)}) copy-start(bf16[96,192]{1,0:T(8,128)(2,1)} %param.23) | copy-start | bytes 110596
  8.1 40.5 %all-gather.9.cloned.1.call-start = ((), (), s32[]{:S(2)}) async-start(), calls=%async_computation.16 | async-start | bytes 1966080 | tf_op jit(solution)/shard_map/all_gather | solution.py:50
  9.3 73.6 %copy-start.28 = (f32[192]{0:T(256)S(1)}, f32[192]{0:T(256)}, u32[]{:S(2)}) copy-start(f32[192]{0:T(256)} %param.25) | copy-start | bytes 2308
  19.7 109.1 %all-gather.13.cloned.1.call-start = ((), (), s32[]{:S(2)}) async-start(), calls=%async_computation.18 | async-start | bytes 1966080 | tf_op jit(solution)/shard_map/all_gather | solution.py:191
  48.6 35.6 %copy-start.8 = (bf16[768,192]{1,0:T(8,128)(2,1)}, bf16[768,192]{1,0:T(8,128)(2,1)S(1)}, u32[]{:S(2)}) copy-start(bf16[768,192]{1,0:T(8,128)(2,1)S(1)} %all_gather.40) | copy-start | bytes 884740
  48.6 37.1 %copy-start.18 = (bf16[96,192]{1,0:T(8,128)(2,1)S(1)}, bf16[96,192]{1,0:T(8,128)(2,1)}, u32[]{:S(2)}) copy-start(bf16[96,192]{1,0:T(8,128)(2,1)} %param.21) | copy-start | bytes 110596
  48.6 34.3 %copy-start.25 = (bf16[1024,768]{0,1:T(8,128)(2,1)S(1)}, bf16[1024,768]{0,1:T(8,128)(2,1)}, u32[]{:S(2)}) copy-start(bf16[1024,768]{0,1:T(8,128)(2,1)} %all-gather.9.cloned.1.call-done) | copy-start | bytes 4718596
  51.5 65.2 %copy-start.29 = (f32[192]{0:T(256)S(1)}, f32[192]{0:T(256)}, u32[]{:S(2)}) copy-start(f32[192]{0:T(256)} %param.24) | copy-start | bytes 2308
  51.5 88.6 %all-gather.11.cloned.1.call-start = ((), (), s32[]{:S(2)}) async-start(), calls=%async_computation.17 | async-start | bytes 1966080 | tf_op jit(solution)/shard_map/all_gather | solution.py:192
  116.7 15.6 %copy-start.10 = (bf16[768,192]{1,0:T(8,128)(2,1)}, bf16[768,192]{1,0:T(8,128)(2,1)S(1)}, u32[]{:S(2)}) copy-start(bf16[768,192]{1,0:T(8,128)(2,1)S(1)} %all_gather.39) | copy-start | bytes 884740
  118.0 10.9 %all-to-all-start = ((bf16[4,256,192]{1,2,0:T(8,128)(2,1)}), bf16[4,256,192]{1,2,0:T(8,128)(2,1)S(1)}, u32[]{:S(2)}, u32[]{:S(2)}) async-start(bf16[4,256,192]{1,2,0:T(8,128)(2,1)} %bitcast.118), calls=%async_computation | async-start | bytes 786432 | tf_op jit(solution)/shard_map/all_to_all | solution.py:58
  132.3 4.6 copy-start
  140.1 11.0 %copy-start.19 = (bf16[192,96]{1,0:T(8,128)(2,1)S(1)}, bf16[192,96]{1,0:T(8,128)(2,1)}, u32[]{:S(2)}) copy-start(bf16[192,96]{1,0:T(8,128)(2,1)} %param.26) | copy-start | bytes 110596
  147.6 34.7 %all-to-all-start.1 = ((bf16[256,4,192]{0,2,1:T(8,128)(2,1)}), bf16[256,4,192]{0,2,1:T(8,128)(2,1)S(1)}, u32[]{:S(2)}, u32[]{:S(2)}) async-start(bf16[256,4,192]{0,2,1:T(8,128)(2,1)} %bitcast.9), calls=%async_computation.1 | async-start | bytes 786432 | tf_op jit(solution)/shard_map/all_to_all | solution.py:62
  151.0 75.6 %reduce-scatter.15.cloned.1.call-start = ((), (), s32[]{:S(2)}) async-start(), calls=%async_computation.19 | async-start | bytes 3932160 | tf_op jit(solution)/shard_map/reduce_scatter | solution.py:54
  182.2 2.3 copy-start.14
  182.3 2.3 copy-start.12
  182.3 44.4 %copy-start.2 = (f32[192,1024]{1,0:T(8,128)S(1)}, f32[192,1024]{1,0:T(8,128)}, u32[]{:S(2)}) copy-start(f32[192,1024]{1,0:T(8,128)} %param.18) | copy-start | bytes 2359300
  182.3 44.4 %copy-start.22 = (f32[192]{0:T(256)S(1)}, f32[192]{0:T(256)}, u32[]{:S(2)}) copy-start(f32[192]{0:T(256)} %param.27) | copy-start | bytes 2308
  184.6 49.6 %copy-start.21 = (f32[192]{0:T(256)S(1)}, f32[192]{0:T(256)}, u32[]{:S(2)}) copy-start(f32[192]{0:T(256)} %param.28) | copy-start | bytes 2308
  184.6 49.6 %copy-start.23 = (f32[192]{0:T(256)S(1)}, f32[192]{0:T(256)}, u32[]{:S(2)}) copy-start(f32[192]{0:T(256)} %param.29) | copy-start | bytes 2308
  184.6 51.2 %copy-start.5 = (f32[192,1024]{1,0:T(8,128)S(1)}, f32[192,1024]{1,0:T(8,128)}, u32[]{:S(2)}) copy-start(f32[192,1024]{1,0:T(8,128)} %param.35) | copy-start | bytes 2359300
  184.6 52.6 %all-gather.17.cloned.1.call-start = ((), (), s32[]{:S(2)}) async-start(), calls=%async_computation.21 | async-start | bytes 1327104 | tf_op jit(solution)/shard_map/all_gather | solution.py:180
  185.2 70.5 %all-gather.15.cloned.1.call-start = ((), (), s32[]{:S(2)}) async-start(), calls=%async_computation.20 | async-start | bytes 1966080 | tf_op jit(solution)/shard_map/all_gather | solution.py:50
  235.2 63.4 %all-gather.19.cloned.1.call-start = ((), (), s32[]{:S(2)}) async-start(), calls=%async_computation.22 | async-start | bytes 1327104 | tf_op jit(solution)/shard_map/all_gather | solution.py:182
  235.7 84.0 %all-gather.21.cloned.1.call-start = ((), (), s32[]{:S(2)}) async-start(), calls=%async_computation.24 | async-start | bytes 1966080 | tf_op jit(solution)/shard_map/all_gather | solution.py:50
  236.6 83.2 %copy-start.27 = (f32[768]{0:T(1024)S(1)}, f32[768]{0:T(1024)}, u32[]{:S(2)}) copy-start(f32[768]{0:T(1024)} %param.31) | copy-start | bytes 9220
  236.6 131.5 %reduce-scatter.19.cloned.1.call-start = ((), (), s32[]{:S(2)}) async-start(), calls=%async_computation.25 | async-start | bytes 3932160 | tf_op jit(solution)/shard_map/reduce_scatter | solution.py:54
  319.8 7.3 copy-start.26
  325.9 1.2 copy-start.31
  330.2 78.3 %reduce-scatter.17.cloned.1.call-start = ((), (), s32[]{:S(2)}) async-start(), calls=%async_computation.23 | async-start | bytes 3932160 | tf_op jit(solution)/shard_map/reduce_scatter | solution.py:54
  335.7 72.8 %copy-start.24 = (f32[192]{0:T(256)S(1)}, f32[192]{0:T(256)}, u32[]{:S(2)}) copy-start(f32[192]{0:T(256)} %param.33) | copy-start | bytes 2308
  335.8 95.6 %all-gather.23.cloned.1.call-start = ((), (), s32[]{:S(2)}) async-start(), calls=%async_computation.26 | async-start | bytes 1966080 | tf_op jit(solution)/shard_map/all_gather | solution.py:50
  434.2 10.9 %all-to-all-start.2 = ((bf16[4,256,192]{1,2,0:T(8,128)(2,1)}), bf16[4,256,192]{1,2,0:T(8,128)(2,1)S(1)}, u32[]{:S(2)}, u32[]{:S(2)}) async-start(bf16[4,256,192]{1,2,0:T(8,128)(2,1)} %bitcast.117), calls=%async_computation.5 | async-start | bytes 786432 | tf_op jit(solution)/shard_map/all_to_all | solution.py:58
  437.6 63.4 %reduce-scatter.23.cloned.1.call-start = ((), (), s32[]{:S(2)}) async-start(), calls=%async_computation.28 | async-start | bytes 1966080 | tf_op jit(solution)/shard_map/reduce_scatter | solution.py:225
  452.7 59.1 %reduce-scatter.21.cloned.1.call-start = ((), (), s32[]{:S(2)}) async-start(), calls=%async_computation.27 | async-start | bytes 1966080 | tf_op jit(solution)/shard_map/reduce_scatter | solution.py:222
  467.3 3.3 copy-start.1
  470.7 108.9 %reduce-scatter.37.cloned.1.call-start = ((), (), s32[]{:S(2)}) async-start(), calls=%async_computation.35 | async-start | bytes 1327104
  476.9 4.5 copy-start.4
  476.9 169.5 %reduce-scatter.35.cloned.1.call-start = ((), (), s32[]{:S(2)}) async-start(), calls=%async_computation.34 | async-start | bytes 1327104 | tf_op jit(solution)/shard_map/reduce_scatter | solution.py:260
  481.4 9.2 copy-start.13
  487.0 10.9 %all-to-all-start.3 = ((bf16[256,4,192]{0,2,1:T(8,128)(2,1)}), bf16[256,4,192]{0,2,1:T(8,128)(2,1)S(1)}, u32[]{:S(2)}, u32[]{:S(2)}) async-start(bf16[256,4,192]{0,2,1:T(8,128)(2,1)} %bitcast.18), calls=%async_computation.6 | async-start | bytes 786432 | tf_op jit(solution)/shard_map/all_to_all | solution.py:62
  490.5 219.9 %reduce-scatter.33.cloned.1.call-start = ((), (), s32[]{:S(2)}) async-start(), calls=%async_computation.33 | async-start | bytes 442368 | tf_op jit(solution)/shard_map/reduce_scatter | solution.py:257
  493.5 280.9 %reduce-scatter.27.cloned.1.call-start = ((), (), s32[]{:S(2)}) async-start(), calls=%async_computation.30 | async-start | bytes 442368 | tf_op jit(solution)/shard_map/reduce_scatter | solution.py:239
  498.1 6.0 copy-start.11
  501.0 337.4 %reduce-scatter.31.cloned.1.call-start = ((), (), s32[]{:S(2)}) async-start(), calls=%async_computation.32 | async-start | bytes 442368 | tf_op jit(solution)/shard_map/reduce_scatter | solution.py:251
  503.9 10.9 %copy-start.9 = (bf16[768,192]{1,0:T(8,128)(2,1)S(1)}, bf16[768,192]{1,0:T(8,128)(2,1)}, u32[]{:S(2)}) copy-start(bf16[768,192]{1,0:T(8,128)(2,1)} %copy-done.8) | copy-start | bytes 884740
  503.9 398.5 %reduce-scatter.29.cloned.1.call-start = ((), (), s32[]{:S(2)}) async-start(), calls=%async_computation.31 | async-start | bytes 442368 | tf_op jit(solution)/shard_map/reduce_scatter | solution.py:245
  506.4 9.0 copy-start.7
  511.8 3.0 copy-start.15
  514.7 427.3 %reduce-scatter.25.cloned.1.call-start = ((), (), s32[]{:S(2)}) async-start(), calls=%async_computation.29 | async-start | bytes 3932160 | tf_op jit(solution)/shard_map/reduce_scatter | solution.py:54
  514.8 1.9 copy-start.3
  519.0 423.0 %copy-start.20 = (f32[192]{0:T(256)S(1)}, f32[192]{0:T(256)}, u32[]{:S(2)}) copy-start(f32[192]{0:T(256)} %param.19) | copy-start | bytes 2308
  519.0 465.0 %copy-start.6 = (f32[1024,192]{0,1:T(8,128)S(1)}, f32[1024,192]{0,1:T(8,128)}, u32[]{:S(2)}) copy-start(f32[1024,192]{0,1:T(8,128)} %get-tuple-element.118) | copy-start | bytes 2359300
Sparse Core Ops, SparseCore 0:
  19.8 19.8 all-gather.8
  51.6 22.1 all-gather.12
  84.3 22.1 all-gather.10
  184.7 41.8 reduce-scatter.14
  411.7 19.6 all-gather.22
  452.8 28.2 reduce-scatter.22
  483.6 28.1 reduce-scatter.20
  515.6 63.9 reduce-scatter.36
  583.4 63.0 reduce-scatter.34
  649.9 60.4 reduce-scatter.32
  714.0 60.3 reduce-scatter.26
  777.9 60.3 reduce-scatter.30
  841.9 60.3 reduce-scatter.28
  904.9 37.0 reduce-scatter.24
Sparse Core Ops, SparseCore 1:
  187.3 44.4 all-gather.16
  235.3 20.4 all-gather.14
  258.0 40.5 all-gather.18
  300.8 19.0 all-gather.20
  330.3 37.8 reduce-scatter.18
  370.7 37.8 reduce-scatter.16
where the time goes:
time: 1010 us; the launch traced here: 994 us
  waiting for transfers between devices  643 us (64%)
  blocking collectives  182 us (18%)
  matrix products  88.9 us (9%)
  other arithmetic  33.5 us (3%)
  between operations  16.3 us (2%)
  starting transfers between devices  15.5 us (2%)
  local copies, waits for them, and re-layouts  14.7 us (1%)
    reduce_scatter x4, waiting for transfers between devices, feature_sums(): lax.psum_scatter(partial_value, 'col', scatter_dimension=1, tiled=True)  145 us
    reduce_scatter x1, waiting for transfers between devices, shards(): lax.psum_scatter(grad_fc1.astype(jnp.bfloat16), 'row', scatter_dimension=...  64.9 us
    reduce_scatter x1, waiting for transfers between devices, shards(): lax.psum_scatter(product_left(normed1, grad_key).astype(jnp.bfloat16), 'r...  62.6 us
    reduce_scatter x1, waiting for transfers between devices, shards(): lax.psum_scatter(product_left(normed1, grad_query).astype(jnp.bfloat16),...  62.5 us
    reduce_scatter x1, waiting for transfers between devices, shards(): lax.psum_scatter(product_left(normed1, grad_value).astype(jnp.bfloat16),...  62.3 us
    reduce_scatter x1, waiting for transfers between devices, shards(): lax.psum_scatter(grad_out_t.astype(jnp.bfloat16), 'row', scatter_dimensio...  62.3 us
    unnamed x21, waiting for transfers between devices  61.9 us
    all_gather x4, waiting for transfers between devices, feature_rows(): return lax.all_gather(block_rows, 'col', axis=1, tiled=True)  59.6 us
  transfers between devices with their start and end apart: 24, of which 18 were waited for; matrix products, arithmetic and copies ran while one was open for 9% of the time, Pallas kernels for 0%

commit v1 on v0

--- a/solution.py
+++ b/solution.py
@@ -1,6 +1,10 @@
+import functools
+
 import jax
 import jax.numpy as jnp
 from jax import lax
+from jax.experimental import pallas as pl
+from jax.experimental.pallas import tpu as pltpu
 from jax.sharding import PartitionSpec as P
 
 HEADS = 12
@@ -299,6 +303,807 @@
     )
 
 
+VMEM_LIMIT = 56 * 1024 * 1024
+MESH_IDS = pl.DeviceIdType.MESH
+
+
+def left_product(first_op, second_op, **extra):
+    return lax.dot_general(
+        first_op, second_op, (((0,), (0,)), ((), ())), preferred_element_type=jnp.float32, **extra
+    )
+
+
+def right_product(first_op, second_op, **extra):
+    return lax.dot_general(
+        first_op, second_op, (((1,), (1,)), ((), ())), preferred_element_type=jnp.float32, **extra
+    )
+
+
+def remote(source, target, send_sem, recv_sem, device):
+    return pltpu.make_async_remote_copy(
+        src_ref=source,
+        dst_ref=target,
+        send_sem=send_sem,
+        recv_sem=recv_sem,
+        device_id=device,
+        device_id_type=MESH_IDS,
+    )
+
+
+class Place:
+    def __init__(self):
+        self.col = lax.axis_index("col")
+        self.row = lax.axis_index("row")
+        self.core_peer = self.col + 1 - 2 * lax.rem(self.col, 2)
+        self.chip_peer = lax.rem(self.col + 2, 4)
+        self.far_peer = lax.rem(self.core_peer + 2, 4)
+        self.z = self.row // 2
+        self.y = lax.rem(self.row, 2)
+        self.y_peer = self.row + 1 - 2 * self.y
+
+
+def greet(place, rows_too):
+    barrier = pltpu.get_barrier_semaphore()
+    count = 3
+    for step in range(1, 4):
+        peer = lax.rem(place.col + step, 4)
+        pl.semaphore_signal(barrier, inc=1, device_id={"col": peer}, device_id_type=MESH_IDS)
+    if rows_too:
+        count += 7
+        for step in range(1, 8):
+            peer = lax.rem(place.row + step, 8)
+            pl.semaphore_signal(barrier, inc=1, device_id={"row": peer}, device_id_type=MESH_IDS)
+    pl.semaphore_wait(barrier, count)
+
+
+class ColGather:
+    def __init__(self, place, buf, send, recv):
+        self.place, self.buf, self.send, self.recv = place, buf, send, recv
+        self.size = buf.shape[0] // 4
+
+    def block(self, index):
+        return self.buf.at[pl.ds(pl.multiple_of(index * self.size, self.size), self.size)]
+
+    def start(self):
+        own = self.block(self.place.col)
+        self.chip = remote(own, own, self.send.at[0], self.recv.at[0], {"col": self.place.chip_peer})
+        self.core = remote(own, own, self.send.at[1], self.recv.at[1], {"col": self.place.core_peer})
+        self.chip.start()
+        self.core.start()
+
+    def forward(self):
+        self.chip.wait_recv()
+        got = self.block(self.place.chip_peer)
+        self.onward = remote(got, got, self.send.at[2], self.recv.at[2], {"col": self.place.core_peer})
+        self.onward.start()
+
+    def finish(self):
+        self.chip.wait_send()
+        self.core.wait()
+        self.onward.wait()
+
+
+class ColScatter:
+    def __init__(self, place, part, slots, stage, send, recv):
+        self.place, self.part, self.slots, self.stage = place, part, slots, stage
+        self.send, self.recv = send, recv
+        self.size = part.shape[0] // 4
+
+    def block(self, index):
+        return self.part.at[pl.ds(pl.multiple_of(index * self.size, self.size), self.size)]
+
+    def start(self):
+        place = self.place
+        peer = {"col": place.core_peer}
+        self.far = remote(
+            self.block(place.far_peer), self.slots.at[0], self.send.at[0], self.recv.at[0], peer
+        )
+        self.near = remote(
+            self.block(place.core_peer), self.slots.at[1], self.send.at[1], self.recv.at[1], peer
+        )
+        self.far.start()
+        self.near.start()
+
+    def forward(self):
+        self.far.wait_recv()
+        mixed = self.block(self.place.chip_peer)[...].astype(jnp.float32) + self.slots[0].astype(
+            jnp.float32
+        )
+        self.stage[...] = mixed.astype(self.stage.dtype)
+        self.cross = remote(
+            self.stage,
+            self.slots.at[2],
+            self.send.at[2],
+            self.recv.at[2],
+            {"col": self.place.chip_peer},
+        )
+        self.cross.start()
+
+    def finish(self):
+        self.far.wait_send()
+        self.near.wait()
+        self.cross.wait()
+        own = self.block(self.place.col)[...].astype(jnp.float32)
+        return own + self.slots[1].astype(jnp.float32) + self.slots[2].astype(jnp.float32)
+
+
+def exchange_sums(place, first, second, stat, send, recv):
+    stat[place.col, 0:1, :] = first
+    stat[place.col, 1:2, :] = second
+    copies = []
+    for step in range(1, 4):
+        peer = lax.rem(place.col + step, 4)
+        copy = remote(
+            stat.at[place.col],
+            stat.at[place.col],
+            send.at[step - 1],
+            recv.at[step - 1],
+            {"col": peer},
+        )
+        copy.start()
+        copies.append(copy)
+    for copy in copies:
+        copy.wait()
+    total = stat[0] + stat[1] + stat[2] + stat[3]
+    return total[0:1], total[1:2]
+
+
+def norm_stats(place, values, width, stat, send, recv):
+    sums, squares = exchange_sums(
+        place,
+        jnp.sum(values, axis=0, keepdims=True),
+        jnp.sum(values * values, axis=0, keepdims=True),
+        stat,
+        send,
+        recv,
+    )
+    mean = sums / width
+    scale = lax.rsqrt(squares / width - mean * mean + EPS)
+    return mean, scale
+
+
+def norm_back(place, upstream, scaled, scale, gain, width, stat, send, recv):
+    weighted = upstream * gain
+    sums, along = exchange_sums(
+        place,
+        jnp.sum(weighted, axis=0, keepdims=True),
+        jnp.sum(weighted * scaled, axis=0, keepdims=True),
+        stat,
+        send,
+        recv,
+    )
+    return scale * (weighted - sums / width - scaled * (along / width))
+
+
+def token_sum(values):
+    ones = jnp.ones((8, values.shape[1]), jnp.float32)
+    return right_product(ones, values, precision=lax.Precision.HIGHEST)[0:1]
+
+
+class LineGather:
+    def __init__(self, place, buf, columns, size, stride, offset, send, recv):
+        self.place, self.buf, self.columns, self.size = place, buf, columns, size
+        self.stride, self.offset, self.send, self.recv = stride, offset, send, recv
+
+    def copy(self, hop, way):
+        source = self.place.z - way * hop
+        start = pl.multiple_of(jnp.clip(source, 0, 3) * self.stride + self.offset, 16)
+        block = self.buf.at[pl.ds(start, self.size), self.columns]
+        slot = 4 * (1 if way < 0 else 0)
+        target = jnp.clip(self.place.row + 2 * way, 0, 7)
+        return remote(
+            block, block, self.send.at[slot + hop], self.recv.at[slot + hop + 1], {"row": target}
+        )
+
+    def arrived(self, hop, way):
+        slot = 4 * (1 if way < 0 else 0)
+        start = pl.multiple_of(
+            jnp.clip(self.place.z - way * hop, 0, 3) * self.stride + self.offset, 16
+        )
+        block = self.buf.at[pl.ds(start, self.size), self.columns]
+        pltpu.make_async_copy(block, block, self.recv.at[slot + hop]).wait()
+
+    def has(self, hop, way):
+        return self.place.z >= hop if way > 0 else self.place.z + hop <= 3
+
+    def sends(self, hop, way):
+        more = self.place.z < 3 if way > 0 else self.place.z > 0
+        return jnp.logical_and(self.has(hop, way), more)
+
+    def start(self):
+        for way in (1, -1):
+
+            @pl.when(self.sends(0, way))
+            def _():
+                self.copy(0, way).start()
+
+    def step(self, hop):
+        for way in (1, -1):
+
+            @pl.when(self.has(hop, way))
+            def _():
+                self.arrived(hop, way)
+
+            if hop < 3:
+
+                @pl.when(self.sends(hop, way))
+                def _():
+                    self.copy(hop, way).start()
+
+    def finish(self):
+        for hop in range(3):
+            for way in (1, -1):
+
+                @pl.when(self.sends(hop, way))
+                def _():
+                    self.copy(hop, way).wait_send()
+
+
+class LineScatter:
+    def __init__(self, place, block, right, left, send, recv):
+        self.place, self.block, self.right, self.left = place, block, right, left
+        self.send, self.recv = send, recv
+
+    def copy(self, target_z, way):
+        slots = self.right if way > 0 else self.left
+        base = 0 if way > 0 else 4
+        device = {"row": jnp.clip(self.place.row + 2 * way, 0, 7)}
+        return remote(
+            slots.at[target_z],
+            slots.at[target_z],
+            self.send.at[base + target_z],
+            self.recv.at[base + target_z],
+            device,
+        )
+
+    def step(self, index):
+        z = self.place.z
+        for way, target_z in ((1, 3 - index), (-1, index)):
+            slots = self.right if way > 0 else self.left
+            relays = z < target_z if way > 0 else z > target_z
+            edge = z == 0 if way > 0 else z == 3
+            inner = z > 0 if way > 0 else z < 3
+
+            @pl.when(jnp.logical_and(relays, edge))
+            def _():
+                slots[target_z] = self.block(target_z)[...]
+
+            @pl.when(jnp.logical_and(relays, inner))
+            def _():
+                self.copy(target_z, way).wait_recv()
+                mixed = slots[target_z].astype(jnp.float32) + self.block(target_z)[...].astype(
+                    jnp.float32
+                )
+                slots[target_z] = mixed.astype(slots.dtype)
+
+            @pl.when(relays)
+            def _():
+                self.copy(target_z, way).start()
+
+    def finish(self, total):
+        z = self.place.z
+        for target_z in range(4):
+
+            @pl.when(z == target_z)
+            def _():
+                total[...] = self.block(target_z)[...].astype(jnp.float32)
+                if target_z > 0:
+                    self.copy(target_z, 1).wait_recv()
+                    total[...] += self.right[target_z].astype(jnp.float32)
+                if target_z < 3:
+                    self.copy(target_z, -1).wait_recv()
+                    total[...] += self.left[target_z].astype(jnp.float32)
+
+            if target_z > 0:
+
+                @pl.when(z < target_z)
+                def _():
+                    self.copy(target_z, 1).wait_send()
+
+            if target_z < 3:
+
+                @pl.when(z > target_z)
+                def _():
+                    self.copy(target_z, -1).wait_send()
+
+
+def enter_kernel(
+    x_ref, cot_ref, gain_ref, shift_ref, w_ref,
+    h_ref, gm_ref, stats_ref, full_ref,
+    stat, sums_send, sums_recv, h_send, h_recv, gm_send, gm_recv,
+    near_send, near_recv, far_send, far_recv, y_send, y_recv,
+):
+    place = Place()
+    greet(place, True)
+    size = x_ref.shape[0]
+    rows = w_ref.shape[0]
+    half = w_ref.shape[1] // 2
+    first, second = pl.ds(0, half), pl.ds(half, half)
+    own_row = pl.multiple_of(place.row * rows, rows)
+    full_ref[pl.ds(own_row, rows), :] = w_ref[...]
+    own_second = full_ref.at[pl.ds(own_row, rows), second]
+    y_peer = {"row": place.y_peer}
+    pair = remote(own_second, own_second, y_send.at[4], y_recv.at[4], y_peer)
+    pair.start()
+    line_first = LineGather(
+        place, full_ref, first, rows, 2 * rows, place.y * rows, near_send, near_recv
+    )
+    line_first.start()
+    own = pl.ds(pl.multiple_of(place.col * size, size), size)
+    gm_ref[own, :] = cot_ref[...].astype(gm_ref.dtype)
+    values = x_ref[...]
+    mean, scale = norm_stats(place, values, 4.0 * size, stat, sums_send, sums_recv)
+    stats_ref[0:1, :] = mean
+    stats_ref[1:2, :] = scale
+    h_ref[own, :] = ((values - mean) * scale * gain_ref[...] + shift_ref[...]).astype(h_ref.dtype)
+    h_gather = ColGather(place, h_ref, h_send, h_recv)
+    h_gather.start()
+    gm_gather = ColGather(place, gm_ref, gm_send, gm_recv)
+    gm_gather.start()
+    pair.wait()
+    line_second = LineGather(
+        place, full_ref, second, 2 * rows, 2 * rows, 0, far_send, far_recv
+    )
+    line_second.start()
+
+    def across(source, slot):
+        start = pl.multiple_of(source * 2 * rows + place.y * rows, rows)
+        block = full_ref.at[pl.ds(start, rows), first]
+        return remote(block, block, y_send.at[slot], y_recv.at[slot], y_peer)
+
+    across(place.z, 5).start()
+    line_first.step(1)
+    h_gather.forward()
+    line_second.step(1)
+    line_first.step(2)
+    gm_gather.forward()
+    line_second.step(2)
+    line_first.step(3)
+    for source in range(4):
+
+        @pl.when(place.z != source)
+        def _():
+            across(source, source).start()
+
+    line_second.step(3)
+    h_gather.finish()
+    gm_gather.finish()
+    across(place.z, 5).wait()
+    for source in range(4):
+
+        @pl.when(place.z != source)
+        def _():
+            across(source, source).wait()
+
+    line_first.finish()
+    line_second.finish()
+
+
+def middle_kernel(
+    part_ref, x_ref, bias_ref, gain_ref, shift_ref,
+    mid_ref, h_ref, stats_ref,
+    slots, stage, stat, rs_send, rs_recv, sums_send, sums_recv, h_send, h_recv,
+):
+    place = Place()
+    greet(place, False)
+    size = x_ref.shape[0]
+    scatter = ColScatter(place, part_ref, slots, stage, rs_send, rs_recv)
+    scatter.start()
+    scatter.forward()
+    values = scatter.finish() + x_ref[...] + bias_ref[...]
+    mid_ref[...] = values
+    mean, scale = norm_stats(place, values, 4.0 * size, stat, sums_send, sums_recv)
+    stats_ref[0:1, :] = mean
+    stats_ref[1:2, :] = scale
+    own = pl.ds(pl.multiple_of(place.col * size, size), size)
+    h_ref[own, :] = ((values - mean) * scale * gain_ref[...] + shift_ref[...]).astype(h_ref.dtype)
+    gather = ColGather(place, h_ref, h_send, h_recv)
+    gather.start()
+    gather.forward()
+    gather.finish()
+
+
+def turn_kernel(
+    out_part_ref, grad_part_ref, mid_ref, cot_ref, stats_ref, gain_ref, bias_ref,
+    out_ref, gx_ref, ga_ref, vec_ref,
+    slots, stage, out_slots, out_stage, stat,
+    rs_send, rs_recv, out_send, out_recv, sums_send, sums_recv, ga_send, ga_recv,
+):
+    place = Place()
+    greet(place, False)
+    size = mid_ref.shape[0]
+    scatter = ColScatter(place, grad_part_ref, slots, stage, rs_send, rs_recv)
+    scatter.start()
+    out_scatter = ColScatter(place, out_part_ref, out_slots, out_stage, out_send, out_recv)
+    out_scatter.start()
+    scatter.forward()
+    mean, scale = stats_ref[0:1, :], stats_ref[1:2, :]
+    upstream = scatter.finish()
+    scaled = (mid_ref[...] - mean) * scale
+    back = norm_back(
+        place, upstream, scaled, scale, gain_ref[...], 4.0 * size, stat, sums_send, sums_recv
+    )
+    gx = cot_ref[...] + back
+    gx_ref[...] = gx
+    own = pl.ds(pl.multiple_of(place.col * size, size), size)
+    ga_ref[own, :] = gx.astype(ga_ref.dtype)
+    gather = ColGather(place, ga_ref, ga_send, ga_recv)
+    gather.start()
+    out_scatter.forward()
+    vec_ref[0:1, :] = token_sum(upstream * scaled)
+    vec_ref[1:2, :] = token_sum(upstream)
+    gather.forward()
+    out_ref[...] = out_scatter.finish() + mid_ref[...] + bias_ref[...]
+    gather.finish()
+
+
+def leave_kernel(
+    part_ref, x_ref, stats_ref, gain_ref, gx_ref, grads_ref, vec_ref,
+    gin_ref, sums_ref, vecs_ref,
+    slots, stage, stat, rs_send, rs_recv, sums_send, sums_recv,
+    vec_slots, vec_send, vec_recv,
+    y_slots, right_a, left_a, right_b, left_b, total_b, y_stage, y_last,
+    y_send, y_recv, near_send, near_recv, far_send, far_recv,
+):
+    place = Place()
+    greet(place, True)
+    size = x_ref.shape[0]
+    rows = grads_ref.shape[0] // 8
+    half = grads_ref.shape[1] // 2
+    first, second = pl.ds(0, half), pl.ds(half, half)
+    y_peer = {"row": place.y_peer}
+    scatter = ColScatter(place, part_ref, slots, stage, rs_send, rs_recv)
+    scatter.start()
+
+    def across(target_z):
+        start = pl.multiple_of(target_z * 2 * rows + (1 - place.y) * rows, rows)
+        return remote(
+            grads_ref.at[pl.ds(start, rows), first],
+            y_slots.at[target_z],
+            y_send.at[target_z],
+            y_recv.at[target_z],
+            y_peer,
+        )
+
+    for target_z in (3, 0, 2, 1):
+        across(target_z).start()
+    line_b = LineScatter(
+        place,
+        lambda k: grads_ref.at[pl.ds(k * 2 * rows, 2 * rows), second],
+        right_b, left_b, far_send, far_recv,
+    )
+    line_b.step(0)
+    scatter.forward()
+    for target_z in (3, 0, 2, 1):
+        across(target_z).wait()
+        start = pl.multiple_of(target_z * 2 * rows + place.y * rows, rows)
+        mixed = y_slots[target_z].astype(jnp.float32) + grads_ref[
+            pl.ds(start, rows), first
+        ].astype(jnp.float32)
+        y_slots[target_z] = mixed.astype(y_slots.dtype)
+    line_b.step(1)
+    line_a = LineScatter(
+        place, lambda k: y_slots.at[k], right_a, left_a, near_send, near_recv
+    )
+    line_a.step(0)
+    line_b.step(2)
+    line_a.step(1)
+    mean, scale = stats_ref[0:1, :], stats_ref[1:2, :]
+    upstream = scatter.finish()
+    scaled = (x_ref[...] - mean) * scale
+    vec_slots[place.row] = vec_ref[...]
+    vec_slots[place.row, 10:11, 0:size] = token_sum(upstream * scaled)
+    vec_slots[place.row, 11:12, 0:size] = token_sum(upstream)
+    vec_copies = []
+    for step in range(1, 8):
+        peer = lax.rem(place.row + step, 8)
+        copy = remote(
+            vec_slots.at[place.row],
+            vec_slots.at[place.row],
+            vec_send.at[step - 1],
+            vec_recv.at[step - 1],
+            {"row": peer},
+        )
+        copy.start()
+        vec_copies.append(copy)
+    back = norm_back(
+        place, upstream, scaled, scale, gain_ref[...], 4.0 * size, stat, sums_send, sums_recv
+    )
+    gin_ref[...] = gx_ref[...] + back
+    line_a.step(2)
+    line_b.finish(total_b)
+    theirs = pl.ds(pl.multiple_of((1 - place.y) * rows, rows), rows)
+    y_stage[...] = total_b[theirs, :].astype(y_stage.dtype)
+    last = remote(y_stage, y_last, y_send.at[4], y_recv.at[4], y_peer)
+    last.start()
+    line_a.finish(sums_ref.at[:, first])
+    for copy in vec_copies:
+        copy.wait()
+    total = vec_slots[0]
+    for index in range(1, 8):
+        total = total + vec_slots[index]
+    vecs_ref[...] = total
+    last.wait()
+    ours = pl.ds(pl.multiple_of(place.y * rows, rows), rows)
+    sums_ref[:, second] = total_b[ours, :] + y_last[...].astype(jnp.float32)
+
+
+def communicate(kernel, number, shapes, scratch, *operands):
+    return pl.pallas_call(
+        kernel,
+        out_shape=[jax.ShapeDtypeStruct(*shape) for shape in shapes],
+        in_specs=[pl.BlockSpec(memory_space=pltpu.VMEM)] * len(operands),
+        out_specs=[pl.BlockSpec(memory_space=pltpu.VMEM)] * len(shapes),
+        scratch_shapes=scratch,
+        compiler_params=pltpu.CompilerParams(
+            collective_id=number, has_side_effects=True, vmem_limit_bytes=VMEM_LIMIT
+        ),
+    )(*operands)
+
+
+def sems(*counts):
+    pairs = []
+    for count in counts:
+        pairs += [pltpu.SemaphoreType.DMA((count,)), pltpu.SemaphoreType.DMA((count,))]
+    return pairs
+
+
+def allowed_pairs(keys, start, width, key_seg, query_seg):
+    key_pos = lax.broadcasted_iota(jnp.int32, (keys, width), 0)
+    query_pos = lax.broadcasted_iota(jnp.int32, (keys, width), 1) + start
+    return (key_seg == query_seg) & (key_pos <= query_pos)
+
+
+def attend_kernel(q_ref, k_ref, v_ref, key_seg_ref, query_seg_ref, o_ref, log_ref):
+    tokens = q_ref.shape[1]
+    width = tokens // 4
+    for start in range(0, tokens, width):
+        keys = start + width
+        mine = pl.ds(start, width)
+        scores = left_product(k_ref[:, 0:keys], q_ref[:, mine])
+        allowed = allowed_pairs(
+            keys, start, width, key_seg_ref[0:keys, :], query_seg_ref[:, mine]
+        )
+        scores = jnp.where(allowed, scores, NEG)
+        top = jnp.max(scores, axis=0, keepdims=True)
+        expo = jnp.exp(scores - top)
+        total = jnp.sum(expo, axis=0, keepdims=True)
+        probs = (expo * (1.0 / total)).astype(jnp.bfloat16)
+        o_ref[:, mine] = product(v_ref[:, 0:keys], probs).astype(o_ref.dtype)
+        log_ref[0, :, mine] = top + jnp.log(total)
+
+
+def attend_back_kernel(
+    q_ref, k_ref, v_ref, go_ref, log_ref, key_seg_ref, query_seg_ref,
+    gq_ref, gk_ref, gv_ref, gk_sum, gv_sum,
+):
+    tokens = q_ref.shape[1]
+    width = tokens // 4
+    gk_sum[...] = jnp.zeros_like(gk_sum)
+    gv_sum[...] = jnp.zeros_like(gv_sum)
+    for start in range(0, tokens, width):
+        keys = start + width
+        mine = pl.ds(start, width)
+        queries, upstream = q_ref[:, mine], go_ref[:, mine]
+        scores = left_product(k_ref[:, 0:keys], queries)
+        allowed = allowed_pairs(
+            keys, start, width, key_seg_ref[0:keys, :], query_seg_ref[:, mine]
+        )
+        probs = jnp.exp(jnp.where(allowed, scores, NEG) - log_ref[0, :, mine])
+        grad_probs = left_product(v_ref[:, 0:keys], upstream)
+        inner = jnp.sum(probs * grad_probs, axis=0, keepdims=True)
+        grad_scores = (probs * (grad_probs - inner)).astype(jnp.bfloat16)
+        grad_q = product(k_ref[:, 0:keys], grad_scores).astype(jnp.bfloat16)
+        gq_ref[:, mine] = (grad_q.astype(jnp.float32) * HEAD_DIM ** (-0.5)).astype(gq_ref.dtype)
+        gk_sum[:, 0:keys] += right_product(queries, grad_scores)
+        gv_sum[:, 0:keys] += right_product(upstream, probs.astype(jnp.bfloat16))
+    gk_ref[...] = gk_sum[...].astype(gk_ref.dtype)
+    gv_ref[...] = gv_sum[...].astype(gv_ref.dtype)
+
+
+def head_spec(tokens, offset):
+    return pl.BlockSpec((HEAD_DIM, tokens), lambda head: (head + offset, 0))
+
+
+def whole_spec(shape):
+    return pl.BlockSpec(shape, lambda head: (0,) * len(shape))
+
+
+def local_params():
+    return pltpu.CompilerParams(vmem_limit_bytes=VMEM_LIMIT)
+
+
+def attend(qkv, key_seg, query_seg):
+    size, tokens = qkv.shape[0] // 3, qkv.shape[1]
+    heads = size // HEAD_DIM
+    log_spec = pl.BlockSpec((1, 1, tokens), lambda head: (head, 0, 0))
+    return pl.pallas_call(
+        attend_kernel,
+        grid=(heads,),
+        in_specs=[head_spec(tokens, part * heads) for part in range(3)]
+        + [whole_spec((tokens, 1)), whole_spec((1, tokens))],
+        out_specs=[head_spec(tokens, 0), log_spec],
+        out_shape=[
+            jax.ShapeDtypeStruct((size, tokens), jnp.bfloat16),
+            jax.ShapeDtypeStruct((heads, 1, tokens), jnp.float32),
+        ],
+        compiler_params=local_params(),
+    )(qkv, qkv, qkv, key_seg, query_seg)
+
+
+def attend_back(qkv, grad_mixed, log_total, key_seg, query_seg):
+    size, tokens = qkv.shape[0] // 3, qkv.shape[1]
+    heads = size // HEAD_DIM
+    log_spec = pl.BlockSpec((1, 1, tokens), lambda head: (head, 0, 0))
+    return pl.pallas_call(
+        attend_back_kernel,
+        grid=(heads,),
+        in_specs=[head_spec(tokens, part * heads) for part in range(3)]
+        + [head_spec(tokens, 0), log_spec, whole_spec((tokens, 1)), whole_spec((1, tokens))],
+        out_specs=[head_spec(tokens, 0)] * 3,
+        out_shape=[jax.ShapeDtypeStruct((size, tokens), jnp.bfloat16)] * 3,
+        scratch_shapes=[pltpu.VMEM((HEAD_DIM, tokens), jnp.float32)] * 2,
+        compiler_params=local_params(),
+    )(qkv, qkv, qkv, grad_mixed, log_total, key_seg, query_seg)
+
+
+def fast_shards(
+    layer_input,
+    ln1_gain,
+    ln1_bias,
+    w_query,
+    w_key,
+    w_value,
+    b_query,
+    b_value,
+    w_out,
+    b_out,
+    ln2_gain,
+    ln2_bias,
+    w_fc1,
+    b_fc1,
+    w_fc2,
+    b_fc2,
+    seq_lengths,
+    cotangent,
+):
+    half, wide = jnp.bfloat16, jnp.float32
+    size, tokens = layer_input.shape
+    full = 4 * size
+    rows, hidden_size = w_fc1.shape
+    width = 4 * size + 2 * hidden_size
+    scaling = HEAD_DIM ** (-0.5)
+    seq_ends = jnp.cumsum(seq_lengths[0])
+    places = jnp.arange(tokens, dtype=jnp.int32)
+    segment = jnp.sum((places[:, None] >= seq_ends[None, :]).astype(jnp.int32), axis=1)
+    key_seg, query_seg = segment[:, None], segment[None, :]
+    packed = jnp.concatenate([w_query, w_key, w_value, w_out.T, w_fc1, w_fc2.T], axis=1)
+    stat = pltpu.VMEM((4, 8, tokens), wide)
+    slots = pltpu.VMEM((3, size, tokens), half)
+    stage = pltpu.VMEM((size, tokens), half)
+
+    normed1, grad_mlp, stats1, weights = communicate(
+        enter_kernel,
+        1,
+        [((full, tokens), half), ((full, tokens), half), ((8, tokens), wide), ((8 * rows, width), half)],
+        [stat] + sems(3, 3, 3, 8, 8, 6),
+        layer_input,
+        cotangent,
+        ln1_gain[:, None],
+        ln1_bias[:, None],
+        packed,
+    )
+    w_qkv, w_up = weights[:, : 3 * size], weights[:, 3 * size : 4 * size]
+    w_first = weights[:, 4 * size : 4 * size + hidden_size]
+    w_second = weights[:, 4 * size + hidden_size :]
+    qkv_bias = jnp.concatenate([b_query, jnp.zeros_like(b_query), b_value])[:, None]
+    qkv_scale = jnp.where(jnp.arange(3 * size) < size, scaling, 1.0)[:, None]
+    qkv = to_half((left_product(w_qkv, normed1) + qkv_bias) * qkv_scale)
+    mixed, log_total = attend(qkv, key_seg, query_seg)
+    middle, normed2, stats2 = communicate(
+        middle_kernel,
+        2,
+        [((size, tokens), wide), ((full, tokens), half), ((8, tokens), wide)],
+        [slots, stage, stat] + sems(3, 3, 3),
+        to_half(product(w_up, mixed)),
+        layer_input,
+        b_out[:, None],
+        ln2_gain[:, None],
+        ln2_bias[:, None],
+    )
+    hidden_pre = left_product(w_first, normed2) + b_fc1[:, None]
+    activated, gate_pull = jax.vjp(smooth_gate, hidden_pre)
+    hidden = to_half(activated)
+    grad_pre = to_half(gate_pull(left_product(w_second, grad_mlp))[0])
+    output, grad_middle, grad_branch, norm2_sums = communicate(
+        turn_kernel,
+        3,
+        [((size, tokens), wide), ((size, tokens), wide), ((full, tokens), half), ((8, size), wide)],
+        [slots, stage, slots, stage, stat] + sems(3, 3, 3, 3),
+        to_half(product(w_second, hidden)),
+        to_half(product(w_first, grad_pre)),
+        middle,
+        cotangent,
+        stats2,
+        ln2_gain[:, None],
+        b_fc2[:, None],
+    )
+    grad_mixed = to_half(left_product(w_up, grad_branch))
+    grad_q, grad_k, grad_v = attend_back(qkv, grad_mixed, log_total, key_seg, query_seg)
+    grad_qkv = jnp.concatenate([grad_q, grad_k, grad_v], axis=0)
+    grads = jnp.concatenate(
+        [
+            to_half(right_product(normed1, grad_qkv)),
+            to_half(right_product(grad_branch, mixed)),
+            to_half(right_product(normed2, grad_pre)),
+            to_half(right_product(grad_mlp, hidden)),
+        ],
+        axis=1,
+    )
+
+    def along(values):
+        return jnp.sum(values.astype(wide), axis=1)
+
+    vectors = jnp.concatenate(
+        [
+            along(grad_q)[None],
+            along(grad_v)[None],
+            along(to_half(grad_middle))[None],
+            norm2_sums[0:2],
+            along(to_half(cotangent))[None],
+            along(grad_pre).reshape(hidden_size // size, size),
+            jnp.zeros((6, size), wide),
+        ],
+        axis=0,
+    )
+    vectors = jnp.pad(vectors, ((0, 0), (0, 256 - size)))
+    line_half = width // 2
+    grad_input, sums, vector_sums = communicate(
+        leave_kernel,
+        4,
+        [((size, tokens), wide), ((rows, width), wide), (vectors.shape, wide)],
+        [slots, stage, stat]
+        + sems(3, 3)
+        + [pltpu.VMEM((8,) + vectors.shape, wide)]
+        + sems(7)
+        + [pltpu.VMEM((4, rows, line_half), half)] * 3
+        + [pltpu.VMEM((4, 2 * rows, line_half), half)] * 2
+        + [
+            pltpu.VMEM((2 * rows, line_half), wide),
+            pltpu.VMEM((rows, line_half), half),
+            pltpu.VMEM((rows, line_half), half),
+        ]
+        + sems(5, 8, 8),
+        to_half(product(w_qkv, grad_qkv)),
+        layer_input,
+        stats1,
+        ln1_gain[:, None],
+        grad_middle,
+        grads,
+        vectors,
+    )
+    vector_sums = vector_sums[:, :size]
+    return (
+        output,
+        grad_input,
+        vector_sums[10],
+        vector_sums[11],
+        sums[:, :size],
+        sums[:, size : 2 * size],
+        sums[:, 2 * size : 3 * size],
+        vector_sums[0],
+        vector_sums[1],
+        sums[:, 3 * size : 4 * size].T,
+        vector_sums[2],
+        vector_sums[3],
+        vector_sums[4],
+        sums[:, 4 * size : 4 * size + hidden_size],
+        vector_sums[6:10].reshape(-1),
+        sums[:, 4 * size + hidden_size :].T,
+        vector_sums[5],
+    )
+
+
 def solution(mesh):
     in_specs = (
         P("col", "row"),
@@ -339,4 +1144,6 @@
         P("col", "row"),
         P("col"),
     )
-    return jax.shard_map(shards, mesh=mesh, in_specs=in_specs, out_specs=out_specs, check_vma=False)
+    fits = mesh.shape["col"] == 4 and mesh.shape["row"] == 8
+    body = fast_shards if fits else shards
+    return jax.shard_map(body, mesh=mesh, in_specs=in_specs, out_specs=out_specs, check_vma=False)

time: 1010 us -> 296 us (0.29); the launches traced: 994 us -> 294 us
  waiting for transfers between devices: 643 us -> 0 us
  Pallas kernels: 0 us -> 220 us
  blocking collectives: 182 us -> 0 us
  matrix products: 88.9 us -> 35.8 us
  other arithmetic: 33.5 us -> 5.43 us
  local copies, waits for them, and re-layouts: 14.7 us -> 31.8 us
  starting transfers between devices: 15.5 us -> 0 us
  between operations: 16.3 us -> 0.97 us
    reduce_scatter x11 -> x0, waiting for transfers between devices: 465 us -> none  [the longest x4 145 us: feature_sums(): lax.psum_scatter(partial_value, 'col', scatter_dimension=1, tiled=True)]
    pallas_call x0 -> x6, Pallas kernels: none -> 220 us  [the longest x4 201 us: communicate(): pl.pallas_call(kernel, out_shape=[jax.ShapeDtypeStruct(*shape) for shape...]
    all_gather x4 -> x0, blocking collectives: 122 us -> none  [the longest x1 31.2 us: shards(): lax.all_gather(w_value, 'row', axis=0, tiled=True)]
    all_gather x8 -> x0, waiting for transfers between devices: 97.6 us -> none  [the longest x4 59.6 us: feature_rows(): return lax.all_gather(block_rows, 'col', axis=1, tiled=True)]
    unnamed x21 -> x0, waiting for transfers between devices: 61.9 us -> none
    psum x5 -> x0, blocking collectives: 59.7 us -> none  [the longest x1 34.4 us: shards(): lax.psum((gain1_grad, shift1_grad, column_sum(grad_query_raw), column_sum...]
    dot_general x18 -> x8, matrix products: 71.3 us -> 21.2 us  [the longest x4 13.9 us: left_product(): lax.dot_general(first_op, second_op, (((0,), (0,)), ((), ())), preferred_...]
    all_to_all x4 -> x0, waiting for transfers between devices: 18.7 us -> none  [the longest x2 14.4 us: to_heads(): lax.all_to_all(block_rows, 'col', split_axis=0, concat_axis=1, tiled=True)]
  transfers between devices with their start and end apart: 24 -> 0, of which waited for: 18 -> 0; matrix products, arithmetic and copies ran while one was open for 9% -> 0% of each run, Pallas kernels for 0% -> 0%
where the time goes in v1:
time: 296 us; the launch traced here: 294 us
  Pallas kernels  220 us (74%)
  matrix products  35.8 us (12%)
  local copies, waits for them, and re-layouts  31.8 us (11%)
  other arithmetic  5.43 us (2%)
    pallas_call x4, Pallas kernels, communicate(): pl.pallas_call(kernel, out_shape=[jax.ShapeDtypeStruct(*shape) for shape...  201 us
    dot_general x4, matrix products, product(): return jnp.dot(first_op, second_op, preferred_element_type=jnp.float32)  14.6 us
    dot_general x4, matrix products, left_product(): lax.dot_general(first_op, second_op, (((0,), (0,)), ((), ())), preferred_...  13.9 us
    pallas_call x1, Pallas kernels, attend_back(): pl.pallas_call(attend_back_kernel, grid=(heads,), in_specs=[head_spec(tok...  10.4 us
    pallas_call x1, Pallas kernels, attend(): pl.pallas_call(attend_kernel, grid=(heads,), in_specs=[head_spec(tokens,...  9.06 us
    dot_general x4, matrix products, right_product(): lax.dot_general(first_op, second_op, (((1,), (1,)), ((), ())), preferred_...  7.26 us
    concatenate x1, local copies, waits for them, and re-layouts, fast_shards(): jnp.concatenate([to_half(right_product(normed1, grad_qkv)), to_half(right...  6.02 us

profile of v1, /device:TPU:8, one launch (start us, length us, event | category | flops | bytes accessed | tf_op | source)
XLA Modules:
  0.0 294.1 jit_solution(17137814159087510209)
XLA Ops:
  0.7 0.0 copy-start.7
  0.7 0.0 copy-start.6
  0.7 0.9 reduce-window.8
  1.5 1.3 convert_reduce_fusion.1
  2.8 0.1 convert_reduce_fusion.5
  2.9 0.0 copy-start.8
  2.9 0.8 pad_maximum_fusion
  3.7 0.9 copy.73
  4.6 1.4 copy.74.gain_ref
  6.0 1.4 copy.78.gain_ref
  7.5 1.4 copy.75.shift_ref
  8.9 1.4 copy.77.bias_ref
  10.3 1.4 copy.79.shift_ref
  11.8 1.4 copy.81.bias_ref
  13.2 0.0 copy-done.7
  13.2 0.0 copy-done.6
  13.2 1.7 concatenate.15.w_ref
  15.0 1.0 copy.76.key_seg_ref
  16.0 53.0 %shard_map.305 = (bf16[768,1024]{1,0:T(8,128)(2,1)}, bf16[768,1024]{1,0:T(8,128)(2,1)}, f32[8,1024]{1,0:T(8,128)}, bf16[768,2304]{1,0:T(8,128)(2,1)}) custom-call(f32[192,1024]{1,0:T(8,128)} %x_ref.5, f32[192,1024]{1,0:T(8,128)} %cot_ref.3, f32[192,1]{1,0:T(8,128)} %copy.74.gain_ref, f32[192,1]{1,0:T(8,128)} %copy.75.shift_ref, ...), custom_call_target="tpu_custom_call" | custom-call | tf_op jit(solution)/shard_map/pallas_call | solution.py:832
  69.0 0.0 copy-done.8
  69.0 3.9 %multiply_convert_fusion.1.q_ref.k_ref.v_ref = bf16[576,1024]{1,0:T(8,128)(2,1)} fusion(bf16[768,1024]{1,0:T(8,128)(2,1)} %get-tuple-element.37, f32[576]{0:T(1024)S(1)} %get-tuple-element.142, f32[576]{0:T(1024)S(1)} %get-tuple-element.141, bf16[768,2304]{1,0:T(8,128)(2,1)} %get-tuple-element.36), kind=kOutput, calls=%fused_computation.11 | convolution fusion | flops 907739136 | bytes 3740160 | tf_op jit(solution)/shard_map/dot_general | solution.py:311
  72.9 9.1 %shard_map.306 = (bf16[192,1024]{1,0:T(8,128)(2,1)}, f32[3,1,1024]{2,1,0:T(1,128)}) custom-call(bf16[576,1024]{1,0:T(8,128)(2,1)} %multiply_convert_fusion.1.q_ref.k_ref.v_ref, bf16[576,1024]{1,0:T(8,128)(2,1)} %multiply_convert_fusion.1.q_ref.k_ref.v_ref, bf16[576,1024]{1,0:T(8,128)(2,1)} %multiply_convert_fusion.1.q_ref.k_ref.v_ref, ...), custom_call_target="tpu_custom_call" | custom-call | tf_op jit(solution)/shard_map/pallas_call | solution.py:920
  82.0 0.0 copy-done.9
  82.0 2.8 convolution_convert_fusion.3.part_ref
  84.8 31.6 %shard_map.307 = (f32[192,1024]{1,0:T(8,128)}, bf16[768,1024]{1,0:T(8,128)(2,1)}, f32[8,1024]{1,0:T(8,128)}) custom-call(bf16[768,1024]{1,0:T(8,128)(2,1)} %convolution_convert_fusion.3.part_ref, f32[192,1024]{1,0:T(8,128)} %x_ref.5, f32[192,1]{1,0:T(8,128)} %copy.77.bias_ref, f32[192,1]{1,0:T(8,128)} %copy.78.gain_ref, f32[192,1]{1,0:T(8,128)} %copy.79.shift_ref), custom_call_target="tpu_custom_call" | custom-call | tf_op jit(solution)/shard_map/pallas_call | solution.py:832
  116.4 0.0 copy-done.14
  116.4 0.0 copy-start.11
  116.4 3.8 %multiply_convert_fusion = (bf16[768,1024]{1,0:T(8,128)(2,1)S(1)}, f32[768,1024]{1,0:T(8,128)S(1)}) fusion(f32[768]{0:T(1024)S(1)} %copy-done.14, bf16[768,1024]{1,0:T(8,128)(2,1)} %get-tuple-element.39, bf16[768,2304]{1,0:T(8,128)(2,1)S(1)} %copy-done.9), kind=kOutput, calls=%fused_computation.10 | convolution fusion | flops 1215823872 | bytes 7475200 | tf_op jit(solution)/shard_map/dot_general | solution.py:311
  120.2 0.0 copy-done.11
  120.2 3.9 %convert_reduce_fusion = (f32[768]{0:T(1024)S(1)}, bf16[768,1024]{1,0:T(8,128)(2,1)S(1)}) fusion(f32[768,1024]{1,0:T(8,128)S(1)} %get-tuple-element.138, f32[768]{0:T(1024)S(1)} %copy-done.14, bf16[768,1024]{1,0:T(8,128)(2,1)S(1)} %copy-done.11, bf16[768,2304]{1,0:T(8,128)(2,1)S(1)} %copy-done.9), kind=kOutput, calls=%fused_computation.9 | convolution fusion | flops 1226046720 | bytes 7478272 | tf_op jit(solution)/shard_map/dot_general | solution.py:311
  124.1 0.0 copy-start.15
  124.1 0.0 copy-start.12
  124.1 1.4 convolution_convert_fusion.4
  125.6 0.5 copy-done.12
  126.1 2.5 convolution_convert_fusion.5
  128.6 0.1 reshape.73
  128.7 4.0 %convolution_convert_fusion.2.out_part_ref = bf16[768,1024]{1,0:T(8,128)(2,1)} fusion(bf16[768,1024]{1,0:T(8,128)(2,1)S(1)} %get-tuple-element.137, bf16[768,2304]{1,0:T(8,128)(2,1)} %get-tuple-element.36), kind=kOutput, calls=%fused_computation.14 | convolution fusion | flops 1208745984 | bytes 4325376 | tf_op jit(solution)/shard_map/dot_general | solution.py:23
  132.6 3.8 %convolution_convert_fusion.1.grad_part_ref = bf16[768,1024]{1,0:T(8,128)(2,1)} fusion(bf16[768,1024]{1,0:T(8,128)(2,1)S(1)} %copy-done.16, bf16[768,2304]{1,0:T(8,128)(2,1)} %get-tuple-element.36), kind=kOutput, calls=%fused_computation.13 | convolution fusion | flops 1208745984 | bytes 4325376 | tf_op jit(solution)/shard_map/dot_general | solution.py:23
  136.5 39.9 %shard_map.308 = (f32[192,1024]{1,0:T(8,128)}, f32[192,1024]{1,0:T(8,128)}, bf16[768,1024]{1,0:T(8,128)(2,1)}, f32[8,192]{1,0:T(8,128)}) custom-call(bf16[768,1024]{1,0:T(8,128)(2,1)} %convolution_convert_fusion.2.out_part_ref, bf16[768,1024]{1,0:T(8,128)(2,1)} %convolution_convert_fusion.1.grad_part_ref, f32[192,1024]{1,0:T(8,128)} %get-tuple-element.41.mid_ref, ...), custom_call_target="tpu_custom_call" | custom-call | tf_op jit(solution)/shard_map/pallas_call | solution.py:832
  176.4 2.2 convolution_convert_fusion.8
  178.7 0.0 copy-done
  178.7 0.1 convert_reduce_fusion.2
  178.8 0.7 slice.74
  179.5 0.2 copy.86
  179.7 2.4 convolution_convert_fusion.7.go_ref
  182.1 10.4 %shard_map.309 = (bf16[192,1024]{1,0:T(8,128)(2,1)}, bf16[192,1024]{1,0:T(8,128)(2,1)}, bf16[192,1024]{1,0:T(8,128)(2,1)}) custom-call(bf16[576,1024]{1,0:T(8,128)(2,1)} %multiply_convert_fusion.1.q_ref.k_ref.v_ref, bf16[576,1024]{1,0:T(8,128)(2,1)} %multiply_convert_fusion.1.q_ref.k_ref.v_ref, bf16[576,1024]{1,0:T(8,128)(2,1)} %multiply_convert_fusion.1.q_ref.k_ref.v_ref, ...), custom_call_target="tpu_custom_call" | custom-call | tf_op jit(solution)/shard_map/pallas_call | solution.py:938
  192.5 1.2 convert_reduce_fusion.4
  193.7 1.1 convert_reduce_fusion.3
  194.8 0.1 concatenate.19
  195.0 0.6 pad.4.vec_ref
  195.6 1.0 constant_dynamic-update-slice_fusion.2
  196.7 3.9 %convolution_convert_fusion.part_ref = bf16[768,1024]{1,0:T(8,128)(2,1)} fusion(bf16[576,1024]{1,0:T(8,128)(2,1)S(1)} %constant_dynamic-update-slice_fusion, bf16[768,2304]{1,0:T(8,128)(2,1)} %get-tuple-element.36), kind=kOutput, calls=%fused_computation.12 | convolution fusion | flops 906756096 | bytes 3735552 | tf_op jit(solution)/shard_map/dot_general | solution.py:23
  200.6 1.1 convolution_convert_fusion.6
  201.8 0.9 copy.85
  202.6 6.0 %concatenate.18.grads_ref = bf16[768,2304]{1,0:T(8,128)(2,1)} concatenate(bf16[768,576]{1,0:T(8,128)(2,1)S(1)} %copy.85, bf16[768,192]{1,0:T(8,128)(2,1)S(1)} %copy.86, bf16[768,768]{1,0:T(8,128)(2,1)} %convolution_convert_fusion.5, bf16[768,768]{1,0:T(8,128)(2,1)S(1)} %convolution_convert_fusion.4), dimensions={1} | concatenate | bytes 7077888 | tf_op jit(solution)/shard_map/concatenate | solution.py:1034
  208.7 76.1 %shard_map.310 = (f32[192,1024]{1,0:T(8,128)}, f32[96,2304]{1,0:T(8,128)}, f32[16,256]{1,0:T(8,128)}) custom-call(bf16[768,1024]{1,0:T(8,128)(2,1)} %convolution_convert_fusion.part_ref, f32[192,1024]{1,0:T(8,128)} %x_ref.5, f32[8,1024]{1,0:T(8,128)} %get-tuple-element.49.stats_ref, f32[192,1]{1,0:T(8,128)} %copy.74.gain_ref, ...), custom_call_target="tpu_custom_call" | custom-call | tf_op jit(solution)/shard_map/pallas_call | solution.py:832
  284.8 0.8 slice.87
  285.6 1.5 fusion.20
  287.1 0.7 reshape.74
  287.7 1.9 slice_bitcast_fusion.1
  289.6 2.0 slice_bitcast_fusion
  291.6 0.7 copy.88
  292.3 0.9 copy.95
  293.2 0.9 copy.96
  (24 shorter events, 0.1 us)
Async XLA Ops:
  0.7 12.6 %copy-start.7 = (bf16[768,96]{0,1:T(8,128)(2,1)S(1)}, bf16[768,96]{0,1:T(8,128)(2,1)}, u32[]{:S(2)}) copy-start(bf16[768,96]{0,1:T(8,128)(2,1)} %param.32) | copy-start | bytes 442372
  0.7 12.6 %copy-start.6 = (bf16[96,768]{1,0:T(8,128)(2,1)S(1)}, bf16[96,768]{1,0:T(8,128)(2,1)}, u32[]{:S(2)}) copy-start(bf16[96,768]{1,0:T(8,128)(2,1)} %param.30) | copy-start | bytes 442372
  2.9 66.1 %copy-start.8 = (s32[1024]{0:T(1024)}, s32[1024]{0:T(1024)S(1)}, u32[]{:S(2)}) copy-start(s32[1024]{0:T(1024)S(1)} %convert_reduce_fusion.5) | copy-start | bytes 12292
  72.9 9.1 %copy-start.9 = (bf16[768,2304]{1,0:T(8,128)(2,1)S(1)}, bf16[768,2304]{1,0:T(8,128)(2,1)}, u32[]{:S(2)}) copy-start(bf16[768,2304]{1,0:T(8,128)(2,1)} %get-tuple-element.36) | copy-start | bytes 10616836
  84.8 31.6 %copy-start.14 = (f32[768]{0:T(1024)S(1)}, f32[768]{0:T(1024)}, u32[]{:S(2)}) copy-start(f32[768]{0:T(1024)} %param.31) | copy-start | bytes 9220
  116.4 3.8 %copy-start.11 = (bf16[768,1024]{1,0:T(8,128)(2,1)S(1)}, bf16[768,1024]{1,0:T(8,128)(2,1)}, u32[]{:S(2)}) copy-start(bf16[768,1024]{1,0:T(8,128)(2,1)} %get-tuple-element.40) | copy-start | bytes 4718596
  124.1 1.5 copy-start.15
  124.1 2.0 copy-start.12
  128.7 4.0 %copy-start.16 = (bf16[768,1024]{1,0:T(8,128)(2,1)S(1)}, bf16[768,1024]{1,0:T(8,128)(2,1)}, u32[]{:S(2)}) copy-start(bf16[768,1024]{1,0:T(8,128)(2,1)} %copy-done.15) | copy-start | bytes 4718596
  136.5 40.0 %copy-start.4 = (bf16[192,1024]{1,0:T(8,128)(2,1)S(1)}, bf16[192,1024]{1,0:T(8,128)(2,1)}, u32[]{:S(2)}) copy-start(bf16[192,1024]{1,0:T(8,128)(2,1)} %get-tuple-element.38) | copy-start | bytes 1179652
  176.4 2.3 copy-start
  176.4 3.3 %copy-start.13 = (bf16[768,1024]{1,0:T(8,128)(2,1)S(1)}, bf16[768,1024]{1,0:T(8,128)(2,1)}, u32[]{:S(2)}) copy-start(bf16[768,1024]{1,0:T(8,128)(2,1)} %get-tuple-element.44) | copy-start | bytes 4718596
  192.5 4.1 %copy-start.5 = (bf16[192,1024]{1,0:T(8,128)(2,1)S(1)}, bf16[192,1024]{1,0:T(8,128)(2,1)}, u32[]{:S(2)}) copy-start(bf16[192,1024]{1,0:T(8,128)(2,1)} %get-tuple-element.47) | copy-start | bytes 1179652
  192.5 4.2 %copy-start.1 = (bf16[192,1024]{1,0:T(8,128)(2,1)S(1)}, bf16[192,1024]{1,0:T(8,128)(2,1)}, u32[]{:S(2)}) copy-start(bf16[192,1024]{1,0:T(8,128)(2,1)} %get-tuple-element.48) | copy-start | bytes 1179652
  196.7 3.9 %copy-start.10 = (bf16[768,1024]{1,0:T(8,128)(2,1)S(1)}, bf16[768,1024]{1,0:T(8,128)(2,1)}, u32[]{:S(2)}) copy-start(bf16[768,1024]{1,0:T(8,128)(2,1)} %get-tuple-element.37) | copy-start | bytes 4718596
  284.8 7.6 %copy-start.2 = (f32[192,1024]{1,0:T(8,128)S(1)}, f32[192,1024]{1,0:T(8,128)}, u32[]{:S(2)}) copy-start(f32[192,1024]{1,0:T(8,128)} %get-tuple-element.160) | copy-start | bytes 2359300
  289.6 3.6 %copy-start.3 = (f32[192,1024]{1,0:T(8,128)S(1)}, f32[192,1024]{1,0:T(8,128)}, u32[]{:S(2)}) copy-start(f32[192,1024]{1,0:T(8,128)} %get-tuple-element.161) | copy-start | bytes 2359300

commit v2 on v1

--- a/solution.py
+++ b/solution.py
@@ -357,24 +357,30 @@
 
 
 class ColGather:
-    def __init__(self, place, buf, send, recv):
-        self.place, self.buf, self.send, self.recv = place, buf, send, recv
+    def __init__(self, place, buf, columns, send, recv, base):
+        self.place, self.buf, self.columns = place, buf, columns
+        self.send, self.recv, self.base = send, recv, base
         self.size = buf.shape[0] // 4
 
     def block(self, index):
-        return self.buf.at[pl.ds(pl.multiple_of(index * self.size, self.size), self.size)]
+        rows = pl.ds(pl.multiple_of(index * self.size, self.size), self.size)
+        return self.buf.at[rows, self.columns]
+
+    def move(self, slot, source, device):
+        slot += self.base
+        return remote(source, source, self.send.at[slot], self.recv.at[slot], {"col": device})
 
     def start(self):
         own = self.block(self.place.col)
-        self.chip = remote(own, own, self.send.at[0], self.recv.at[0], {"col": self.place.chip_peer})
-        self.core = remote(own, own, self.send.at[1], self.recv.at[1], {"col": self.place.core_peer})
+        self.chip = self.move(0, own, self.place.chip_peer)
+        self.core = self.move(1, own, self.place.core_peer)
         self.chip.start()
         self.core.start()
 
     def forward(self):
         self.chip.wait_recv()
         got = self.block(self.place.chip_peer)
-        self.onward = remote(got, got, self.send.at[2], self.recv.at[2], {"col": self.place.core_peer})
+        self.onward = self.move(2, got, self.place.core_peer)
         self.onward.start()
 
     def finish(self):
@@ -384,39 +390,40 @@
 
 
 class ColScatter:
-    def __init__(self, place, part, slots, stage, send, recv):
-        self.place, self.part, self.slots, self.stage = place, part, slots, stage
-        self.send, self.recv = send, recv
+    def __init__(self, place, part, slots, stage, columns, send, recv, base):
+        self.place, self.part, self.columns = place, part, columns
+        self.slots, self.stage = slots, stage
+        self.send, self.recv, self.base = send, recv, base
         self.size = part.shape[0] // 4
 
     def block(self, index):
-        return self.part.at[pl.ds(pl.multiple_of(index * self.size, self.size), self.size)]
+        rows = pl.ds(pl.multiple_of(index * self.size, self.size), self.size)
+        return self.part.at[rows, self.columns]
+
+    def slot(self, index):
+        return self.slots.at[index, :, self.columns]
+
+    def move(self, slot, source, device):
+        sem = slot + self.base
+        return remote(
+            source, self.slot(slot), self.send.at[sem], self.recv.at[sem], {"col": device}
+        )
 
     def start(self):
         place = self.place
-        peer = {"col": place.core_peer}
-        self.far = remote(
-            self.block(place.far_peer), self.slots.at[0], self.send.at[0], self.recv.at[0], peer
-        )
-        self.near = remote(
-            self.block(place.core_peer), self.slots.at[1], self.send.at[1], self.recv.at[1], peer
-        )
+        self.far = self.move(0, self.block(place.far_peer), place.core_peer)
         self.far.start()
+        self.near = self.move(1, self.block(place.core_peer), place.core_peer)
         self.near.start()
 
     def forward(self):
         self.far.wait_recv()
-        mixed = self.block(self.place.chip_peer)[...].astype(jnp.float32) + self.slots[0].astype(
-            jnp.float32
-        )
-        self.stage[...] = mixed.astype(self.stage.dtype)
-        self.cross = remote(
-            self.stage,
-            self.slots.at[2],
-            self.send.at[2],
-            self.recv.at[2],
-            {"col": self.place.chip_peer},
-        )
+        mixed = self.block(self.place.chip_peer)[...].astype(jnp.float32) + self.slot(0)[
+            ...
+        ].astype(jnp.float32)
+        staged = self.stage.at[:, self.columns]
+        staged[...] = mixed.astype(self.stage.dtype)
+        self.cross = self.move(2, staged, self.place.chip_peer)
         self.cross.start()
 
     def finish(self):
@@ -424,55 +431,59 @@
         self.near.wait()
         self.cross.wait()
         own = self.block(self.place.col)[...].astype(jnp.float32)
-        return own + self.slots[1].astype(jnp.float32) + self.slots[2].astype(jnp.float32)
-
-
-def exchange_sums(place, first, second, stat, send, recv):
-    stat[place.col, 0:1, :] = first
-    stat[place.col, 1:2, :] = second
-    copies = []
-    for step in range(1, 4):
-        peer = lax.rem(place.col + step, 4)
-        copy = remote(
-            stat.at[place.col],
-            stat.at[place.col],
-            send.at[step - 1],
-            recv.at[step - 1],
-            {"col": peer},
-        )
-        copy.start()
-        copies.append(copy)
-    for copy in copies:
-        copy.wait()
-    total = stat[0] + stat[1] + stat[2] + stat[3]
-    return total[0:1], total[1:2]
-
-
-def norm_stats(place, values, width, stat, send, recv):
-    sums, squares = exchange_sums(
+        return own + self.slot(1)[...].astype(jnp.float32) + self.slot(2)[...].astype(jnp.float32)
+
+
+class ColSums:
+    def __init__(self, place, first, second, stat, columns, send, recv, base):
+        self.stat, self.columns = stat, columns
+        stat[place.col, 0:1, columns] = first
+        stat[place.col, 1:2, columns] = second
+        own = stat.at[place.col, :, columns]
+        self.copies = []
+        for step in range(1, 4):
+            peer = lax.rem(place.col + step, 4)
+            sem = base + step - 1
+            copy = remote(own, own, send.at[sem], recv.at[sem], {"col": peer})
+            copy.start()
+            self.copies.append(copy)
+
+    def finish(self):
+        for copy in self.copies:
+            copy.wait()
+        part = [self.stat[index, :, self.columns] for index in range(4)]
+        total = part[0] + part[1] + part[2] + part[3]
+        return total[0:1], total[1:2]
+
+
+def begin_stats(place, values, *rest):
+    return ColSums(
         place,
         jnp.sum(values, axis=0, keepdims=True),
         jnp.sum(values * values, axis=0, keepdims=True),
-        stat,
-        send,
-        recv,
-    )
-    mean = sums / width
-    scale = lax.rsqrt(squares / width - mean * mean + EPS)
-    return mean, scale
-
-
-def norm_back(place, upstream, scaled, scale, gain, width, stat, send, recv):
+        *rest,
+    )
+
+
+def end_stats(sums, width):
+    total, squares = sums.finish()
+    mean = total / width
+    return mean, lax.rsqrt(squares / width - mean * mean + EPS)
+
+
+def begin_back(place, upstream, scaled, gain, *rest):
     weighted = upstream * gain
-    sums, along = exchange_sums(
+    return ColSums(
         place,
         jnp.sum(weighted, axis=0, keepdims=True),
         jnp.sum(weighted * scaled, axis=0, keepdims=True),
-        stat,
-        send,
-        recv,
-    )
-    return scale * (weighted - sums / width - scaled * (along / width))
+        *rest,
+    )
+
+
+def end_back(sums, upstream, scaled, scale, gain, width):
+    total, along = sums.finish()
+    return scale * (upstream * gain - total / width - scaled * (along / width))
 
 
 def token_sum(values):
@@ -481,9 +492,10 @@
 
 
 class LineGather:
-    def __init__(self, place, buf, columns, size, stride, offset, send, recv):
+    def __init__(self, place, buf, columns, size, stride, offset, send, recv, onward=None):
         self.place, self.buf, self.columns, self.size = place, buf, columns, size
         self.stride, self.offset, self.send, self.recv = stride, offset, send, recv
+        self.onward = onward
 
     def copy(self, hop, way):
         source = self.place.z - way * hop
@@ -523,6 +535,8 @@
             @pl.when(self.has(hop, way))
             def _():
                 self.arrived(hop, way)
+                if self.onward is not None:
+                    self.onward(hop, way).start()
 
             if hop < 3:
 
@@ -531,6 +545,14 @@
                     self.copy(hop, way).start()
 
     def finish(self):
+        if self.onward is not None:
+            for hop in range(1, 4):
+                for way in (1, -1):
+
+                    @pl.when(self.has(hop, way))
+                    def _():
+                        self.onward(hop, way).wait()
+
         for hop in range(3):
             for way in (1, -1):
 
@@ -607,190 +629,354 @@
                     self.copy(target_z, -1).wait_send()
 
 
+def row_gather_scratch():
+    return sems(8, 8, 8)
+
+
+class RowGather:
+    def __init__(self, place, first, second, rows, send_a, recv_a, send_b, recv_b, y_send, y_recv):
+        self.place, self.rows = place, rows
+        self.first, self.first_columns = first
+        self.second, self.second_columns = second
+        self.y_send, self.y_recv = y_send, y_recv
+        self.line_a = LineGather(
+            place, self.first, self.first_columns, rows, 2 * rows, place.y * rows,
+            send_a, recv_a, self.onward,
+        )
+        self.line_b = LineGather(
+            place, self.second, self.second_columns, 2 * rows, 2 * rows, 0, send_b, recv_b
+        )
+
+    def across(self, buf, columns, source_z, slot):
+        start = pl.multiple_of(source_z * 2 * self.rows + self.place.y * self.rows, self.rows)
+        block = buf.at[pl.ds(start, self.rows), columns]
+        peer = {"row": self.place.y_peer}
+        return remote(block, block, self.y_send.at[slot], self.y_recv.at[slot], peer)
+
+    def onward(self, hop, way):
+        source = jnp.clip(self.place.z - way * hop, 0, 3)
+        slot = hop if way > 0 else hop + 3
+        return self.across(self.first, self.first_columns, source, slot)
+
+    def start(self):
+        self.pair = self.across(self.second, self.second_columns, self.place.z, 7)
+        self.pair.start()
+        self.line_a.start()
+
+    def second_start(self):
+        self.pair.wait()
+        self.line_b.start()
+        self.mine = self.onward(0, 1)
+        self.mine.start()
+
+    def step(self, hop):
+        self.line_a.step(hop)
+        self.line_b.step(hop)
+
+    def finish(self):
+        self.mine.wait()
+        self.line_a.finish()
+        self.line_b.finish()
+
+
+def row_scatter_scratch(rows, columns, half, wide):
+    return (
+        [pltpu.VMEM((4, rows, columns), half)] * 3
+        + [pltpu.VMEM((4, 2 * rows, columns), half)] * 2
+        + [
+            pltpu.VMEM((2 * rows, columns), wide),
+            pltpu.VMEM((rows, columns), half),
+            pltpu.VMEM((rows, columns), half),
+        ]
+        + sems(5, 8, 8)
+    )
+
+
+class RowScatter:
+    def __init__(
+        self, place, first, second, rows, slots, right_a, left_a, right_b, left_b,
+        total, stage, last, y_send, y_recv, send_a, recv_a, send_b, recv_b,
+    ):
+        self.place, self.rows, self.slots = place, rows, slots
+        self.first, self.first_columns = first
+        self.second, self.second_columns = second
+        self.total, self.stage, self.last = total, stage, last
+        self.y_send, self.y_recv = y_send, y_recv
+        self.line_a = LineScatter(place, lambda k: slots.at[k], right_a, left_a, send_a, recv_a)
+        self.line_b = LineScatter(
+            place,
+            lambda k: self.second.at[pl.ds(k * 2 * rows, 2 * rows), self.second_columns],
+            right_b, left_b, send_b, recv_b,
+        )
+
+    def block(self, target_z, target_y):
+        start = pl.multiple_of(target_z * 2 * self.rows + target_y * self.rows, self.rows)
+        return self.first.at[pl.ds(start, self.rows), self.first_columns]
+
+    def start(self):
+        self.copies = {}
+        for target_z in (3, 0, 2, 1):
+            self.copies[target_z] = remote(
+                self.block(target_z, 1 - self.place.y),
+                self.slots.at[target_z],
+                self.y_send.at[target_z],
+                self.y_recv.at[target_z],
+                {"row": self.place.y_peer},
+            )
+            self.copies[target_z].start()
+        self.line_b.step(0)
+
+    def mix(self, target_z):
+        self.copies[target_z].wait()
+        mixed = self.slots[target_z].astype(jnp.float32) + self.block(target_z, self.place.y)[
+            ...
+        ].astype(jnp.float32)
+        self.slots[target_z] = mixed.astype(self.slots.dtype)
+
+    def second_start(self):
+        self.mix(3)
+        self.mix(0)
+        self.line_a.step(0)
+        self.mix(2)
+        self.mix(1)
+
+    def third(self):
+        self.line_b.step(1)
+        self.line_a.step(1)
+
+    def fourth(self):
+        self.line_b.step(2)
+        self.line_a.step(2)
+
+    def fifth(self):
+        rows = self.rows
+        self.line_b.finish(self.total)
+        theirs = pl.ds(pl.multiple_of((1 - self.place.y) * rows, rows), rows)
+        self.stage[...] = self.total[theirs, :].astype(self.stage.dtype)
+        self.final = remote(
+            self.stage, self.last, self.y_send.at[4], self.y_recv.at[4], {"row": self.place.y_peer}
+        )
+        self.final.start()
+
+    def finish(self, first_out, second_out):
+        rows = self.rows
+        self.line_a.finish(first_out)
+        self.final.wait()
+        ours = pl.ds(pl.multiple_of(self.place.y * rows, rows), rows)
+        second_out[...] = self.total[ours, :] + self.last[...].astype(jnp.float32)
+
+
+CHUNKS = 2
+
+
+def chunks_of(tokens):
+    width = tokens // CHUNKS
+    return [pl.ds(index * width, width) for index in range(CHUNKS)]
+
+
+GAIN1, SHIFT1, BIAS_OUT, GAIN2, SHIFT2, BIAS_FC2 = range(6)
+
+
 def enter_kernel(
-    x_ref, cot_ref, gain_ref, shift_ref, w_ref,
+    x_ref, cot_ref, par_ref, w_ref,
     h_ref, gm_ref, stats_ref, full_ref,
-    stat, sums_send, sums_recv, h_send, h_recv, gm_send, gm_recv,
-    near_send, near_recv, far_send, far_recv, y_send, y_recv,
+    stat, sums_send, sums_recv, h_send, h_recv, gm_send, gm_recv, *row_scratch,
 ):
     place = Place()
     greet(place, True)
     size = x_ref.shape[0]
     rows = w_ref.shape[0]
     half = w_ref.shape[1] // 2
-    first, second = pl.ds(0, half), pl.ds(half, half)
-    own_row = pl.multiple_of(place.row * rows, rows)
-    full_ref[pl.ds(own_row, rows), :] = w_ref[...]
-    own_second = full_ref.at[pl.ds(own_row, rows), second]
-    y_peer = {"row": place.y_peer}
-    pair = remote(own_second, own_second, y_send.at[4], y_recv.at[4], y_peer)
-    pair.start()
-    line_first = LineGather(
-        place, full_ref, first, rows, 2 * rows, place.y * rows, near_send, near_recv
-    )
-    line_first.start()
+    chunks = chunks_of(x_ref.shape[1])
     own = pl.ds(pl.multiple_of(place.col * size, size), size)
+    full_ref[pl.ds(pl.multiple_of(place.row * rows, rows), rows), :] = w_ref[...]
+    gather = RowGather(
+        place, (full_ref, pl.ds(0, half)), (full_ref, pl.ds(half, half)), rows, *row_scratch
+    )
+    gather.start()
+    sums = [
+        begin_stats(place, x_ref[:, cols], stat, cols, sums_send, sums_recv, 3 * index)
+        for index, cols in enumerate(chunks)
+    ]
     gm_ref[own, :] = cot_ref[...].astype(gm_ref.dtype)
-    values = x_ref[...]
-    mean, scale = norm_stats(place, values, 4.0 * size, stat, sums_send, sums_recv)
-    stats_ref[0:1, :] = mean
-    stats_ref[1:2, :] = scale
-    h_ref[own, :] = ((values - mean) * scale * gain_ref[...] + shift_ref[...]).astype(h_ref.dtype)
-    h_gather = ColGather(place, h_ref, h_send, h_recv)
-    h_gather.start()
-    gm_gather = ColGather(place, gm_ref, gm_send, gm_recv)
-    gm_gather.start()
-    pair.wait()
-    line_second = LineGather(
-        place, full_ref, second, 2 * rows, 2 * rows, 0, far_send, far_recv
-    )
-    line_second.start()
-
-    def across(source, slot):
-        start = pl.multiple_of(source * 2 * rows + place.y * rows, rows)
-        block = full_ref.at[pl.ds(start, rows), first]
-        return remote(block, block, y_send.at[slot], y_recv.at[slot], y_peer)
-
-    across(place.z, 5).start()
-    line_first.step(1)
-    h_gather.forward()
-    line_second.step(1)
-    line_first.step(2)
-    gm_gather.forward()
-    line_second.step(2)
-    line_first.step(3)
-    for source in range(4):
-
-        @pl.when(place.z != source)
-        def _():
-            across(source, source).start()
-
-    line_second.step(3)
-    h_gather.finish()
-    gm_gather.finish()
-    across(place.z, 5).wait()
-    for source in range(4):
-
-        @pl.when(place.z != source)
-        def _():
-            across(source, source).wait()
-
-    line_first.finish()
-    line_second.finish()
+    gathers = []
+    for index, cols in enumerate(chunks):
+        mean, scale = end_stats(sums[index], 4.0 * size)
+        stats_ref[0:1, cols] = mean
+        stats_ref[1:2, cols] = scale
+        normed = (x_ref[:, cols] - mean) * scale * par_ref[:, GAIN1 : GAIN1 + 1]
+        h_ref[own, cols] = (normed + par_ref[:, SHIFT1 : SHIFT1 + 1]).astype(h_ref.dtype)
+        gathers.append(ColGather(place, h_ref, cols, h_send, h_recv, 3 * index))
+        gathers[-1].start()
+    for index, cols in enumerate(chunks):
+        gathers.append(ColGather(place, gm_ref, cols, gm_send, gm_recv, 3 * index))
+        gathers[-1].start()
+    gather.second_start()
+    gather.step(1)
+    gathers[0].forward()
+    gather.step(2)
+    gathers[1].forward()
+    gather.step(3)
+    for item in gathers[2:]:
+        item.forward()
+    for item in gathers:
+        item.finish()
+    gather.finish()
 
 
 def middle_kernel(
-    part_ref, x_ref, bias_ref, gain_ref, shift_ref,
-    mid_ref, h_ref, stats_ref,
-    slots, stage, stat, rs_send, rs_recv, sums_send, sums_recv, h_send, h_recv,
-):
-    place = Place()
-    greet(place, False)
-    size = x_ref.shape[0]
-    scatter = ColScatter(place, part_ref, slots, stage, rs_send, rs_recv)
-    scatter.start()
-    scatter.forward()
-    values = scatter.finish() + x_ref[...] + bias_ref[...]
-    mid_ref[...] = values
-    mean, scale = norm_stats(place, values, 4.0 * size, stat, sums_send, sums_recv)
-    stats_ref[0:1, :] = mean
-    stats_ref[1:2, :] = scale
-    own = pl.ds(pl.multiple_of(place.col * size, size), size)
-    h_ref[own, :] = ((values - mean) * scale * gain_ref[...] + shift_ref[...]).astype(h_ref.dtype)
-    gather = ColGather(place, h_ref, h_send, h_recv)
-    gather.start()
-    gather.forward()
-    gather.finish()
-
-
-def turn_kernel(
-    out_part_ref, grad_part_ref, mid_ref, cot_ref, stats_ref, gain_ref, bias_ref,
-    out_ref, gx_ref, ga_ref, vec_ref,
-    slots, stage, out_slots, out_stage, stat,
-    rs_send, rs_recv, out_send, out_recv, sums_send, sums_recv, ga_send, ga_recv,
-):
-    place = Place()
-    greet(place, False)
-    size = mid_ref.shape[0]
-    scatter = ColScatter(place, grad_part_ref, slots, stage, rs_send, rs_recv)
-    scatter.start()
-    out_scatter = ColScatter(place, out_part_ref, out_slots, out_stage, out_send, out_recv)
-    out_scatter.start()
-    scatter.forward()
-    mean, scale = stats_ref[0:1, :], stats_ref[1:2, :]
-    upstream = scatter.finish()
-    scaled = (mid_ref[...] - mean) * scale
-    back = norm_back(
-        place, upstream, scaled, scale, gain_ref[...], 4.0 * size, stat, sums_send, sums_recv
-    )
-    gx = cot_ref[...] + back
-    gx_ref[...] = gx
-    own = pl.ds(pl.multiple_of(place.col * size, size), size)
-    ga_ref[own, :] = gx.astype(ga_ref.dtype)
-    gather = ColGather(place, ga_ref, ga_send, ga_recv)
-    gather.start()
-    out_scatter.forward()
-    vec_ref[0:1, :] = token_sum(upstream * scaled)
-    vec_ref[1:2, :] = token_sum(upstream)
-    gather.forward()
-    out_ref[...] = out_scatter.finish() + mid_ref[...] + bias_ref[...]
-    gather.finish()
-
-
-def leave_kernel(
-    part_ref, x_ref, stats_ref, gain_ref, gx_ref, grads_ref, vec_ref,
-    gin_ref, sums_ref, vecs_ref,
-    slots, stage, stat, rs_send, rs_recv, sums_send, sums_recv,
-    vec_slots, vec_send, vec_recv,
-    y_slots, right_a, left_a, right_b, left_b, total_b, y_stage, y_last,
-    y_send, y_recv, near_send, near_recv, far_send, far_recv,
+    part_ref, x_ref, par_ref, first_ref, second_ref,
+    mid_ref, h_ref, stats_ref, full_first, full_second,
+    slots, stage, stat, rs_send, rs_recv, sums_send, sums_recv, h_send, h_recv, *row_scratch,
 ):
     place = Place()
     greet(place, True)
     size = x_ref.shape[0]
-    rows = grads_ref.shape[0] // 8
+    rows, columns = first_ref.shape
+    chunks = chunks_of(x_ref.shape[1])
+    own = pl.ds(pl.multiple_of(place.col * size, size), size)
+    scatters = [
+        ColScatter(place, part_ref, slots, stage, cols, rs_send, rs_recv, 3 * index)
+        for index, cols in enumerate(chunks)
+    ]
+    for item in scatters:
+        item.start()
+    own_rows = pl.ds(pl.multiple_of(place.row * rows, rows), rows)
+    full_first[own_rows, :] = first_ref[...]
+    full_second[own_rows, :] = second_ref[...]
+    everything = pl.ds(0, columns)
+    gather = RowGather(
+        place, (full_first, everything), (full_second, everything), rows, *row_scratch
+    )
+    gather.start()
+    for item in scatters:
+        item.forward()
+    gather.second_start()
+    sums, gathers = [], []
+
+    def begin(index):
+        cols = chunks[index]
+        values = scatters[index].finish() + x_ref[:, cols] + par_ref[:, BIAS_OUT : BIAS_OUT + 1]
+        mid_ref[:, cols] = values
+        sums.append(begin_stats(place, values, stat, cols, sums_send, sums_recv, 3 * index))
+
+    def end(index):
+        cols = chunks[index]
+        mean, scale = end_stats(sums[index], 4.0 * size)
+        stats_ref[0:1, cols] = mean
+        stats_ref[1:2, cols] = scale
+        normed = (mid_ref[:, cols] - mean) * scale * par_ref[:, GAIN2 : GAIN2 + 1]
+        h_ref[own, cols] = (normed + par_ref[:, SHIFT2 : SHIFT2 + 1]).astype(h_ref.dtype)
+        gathers.append(ColGather(place, h_ref, cols, h_send, h_recv, 3 * index))
+        gathers[-1].start()
+
+    begin(0)
+    end(0)
+    gather.step(1)
+    begin(1)
+    end(1)
+    gathers[0].forward()
+    gather.step(2)
+    gathers[1].forward()
+    gather.step(3)
+    for item in gathers:
+        item.finish()
+    gather.finish()
+
+
+def turn_kernel(
+    part_ref, mid_ref, cot_ref, stats_ref, par_ref, first_ref, second_ref,
+    gx_ref, ga_ref, vec_ref, first_out, second_out,
+    up_keep, slots, stage, stat, rs_send, rs_recv, sums_send, sums_recv, ga_send, ga_recv,
+    *row_scratch,
+):
+    place = Place()
+    greet(place, True)
+    size = mid_ref.shape[0]
+    rows = first_out.shape[0]
+    everything = pl.ds(0, first_ref.shape[1])
+    chunks = chunks_of(mid_ref.shape[1])
+    own = pl.ds(pl.multiple_of(place.col * size, size), size)
+    gain = par_ref[:, GAIN2 : GAIN2 + 1]
+    scatters = [
+        ColScatter(place, part_ref, slots, stage, cols, rs_send, rs_recv, 3 * index)
+        for index, cols in enumerate(chunks)
+    ]
+    for item in scatters:
+        item.start()
+    summer = RowScatter(
+        place, (first_ref, everything), (second_ref, everything), rows, *row_scratch
+    )
+    summer.start()
+    for item in scatters:
+        item.forward()
+    summer.second_start()
+    gathers = []
+
+    def scaled(cols):
+        return (mid_ref[:, cols] - stats_ref[0:1, cols]) * stats_ref[1:2, cols]
+
+    def turn(index):
+        cols = chunks[index]
+        upstream = scatters[index].finish()
+        up_keep[:, cols] = upstream
+        xhat = scaled(cols)
+        sums = begin_back(
+            place, upstream, xhat, gain, stat, cols, sums_send, sums_recv, 3 * index
+        )
+        back = end_back(sums, upstream, xhat, stats_ref[1:2, cols], gain, 4.0 * size)
+        gx = cot_ref[:, cols] + back
+        gx_ref[:, cols] = gx
+        ga_ref[own, cols] = gx.astype(ga_ref.dtype)
+        gathers.append(ColGather(place, ga_ref, cols, ga_send, ga_recv, 3 * index))
+        gathers[-1].start()
+
+    turn(0)
+    summer.third()
+    turn(1)
+    summer.fourth()
+    gathers[0].forward()
+    summer.fifth()
+    gathers[1].forward()
+    vec_ref[0:1, :] = token_sum(up_keep[...] * scaled(pl.ds(0, mid_ref.shape[1])))
+    vec_ref[1:2, :] = token_sum(up_keep[...])
+    for item in gathers:
+        item.finish()
+    summer.finish(first_out, second_out)
+
+
+def leave_kernel(
+    part_ref, out_part_ref, x_ref, mid_ref, stats_ref, par_ref, gx_ref, grads_ref, vec_ref,
+    gin_ref, out_ref, first_out, second_out, vecs_ref,
+    slots, stage, out_slots, out_stage, stat,
+    rs_send, rs_recv, out_send, out_recv, sums_send, sums_recv,
+    vec_slots, vec_send, vec_recv, *row_scratch,
+):
+    place = Place()
+    greet(place, True)
+    size = x_ref.shape[0]
+    rows = first_out.shape[0]
     half = grads_ref.shape[1] // 2
-    first, second = pl.ds(0, half), pl.ds(half, half)
-    y_peer = {"row": place.y_peer}
-    scatter = ColScatter(place, part_ref, slots, stage, rs_send, rs_recv)
+    everything = pl.ds(0, x_ref.shape[1])
+    gain = par_ref[:, GAIN1 : GAIN1 + 1]
+    scatter = ColScatter(place, part_ref, slots, stage, everything, rs_send, rs_recv, 0)
     scatter.start()
-
-    def across(target_z):
-        start = pl.multiple_of(target_z * 2 * rows + (1 - place.y) * rows, rows)
-        return remote(
-            grads_ref.at[pl.ds(start, rows), first],
-            y_slots.at[target_z],
-            y_send.at[target_z],
-            y_recv.at[target_z],
-            y_peer,
-        )
-
-    for target_z in (3, 0, 2, 1):
-        across(target_z).start()
-    line_b = LineScatter(
-        place,
-        lambda k: grads_ref.at[pl.ds(k * 2 * rows, 2 * rows), second],
-        right_b, left_b, far_send, far_recv,
-    )
-    line_b.step(0)
+    summer = RowScatter(
+        place, (grads_ref, pl.ds(0, half)), (grads_ref, pl.ds(half, half)), rows, *row_scratch
+    )
+    summer.start()
+    out_scatter = ColScatter(
+        place, out_part_ref, out_slots, out_stage, everything, out_send, out_recv, 0
+    )
+    out_scatter.start()
     scatter.forward()
-    for target_z in (3, 0, 2, 1):
-        across(target_z).wait()
-        start = pl.multiple_of(target_z * 2 * rows + place.y * rows, rows)
-        mixed = y_slots[target_z].astype(jnp.float32) + grads_ref[
-            pl.ds(start, rows), first
-        ].astype(jnp.float32)
-        y_slots[target_z] = mixed.astype(y_slots.dtype)
-    line_b.step(1)
-    line_a = LineScatter(
-        place, lambda k: y_slots.at[k], right_a, left_a, near_send, near_recv
-    )
-    line_a.step(0)
-    line_b.step(2)
-    line_a.step(1)
-    mean, scale = stats_ref[0:1, :], stats_ref[1:2, :]
+    out_scatter.forward()
+    summer.second_start()
+    summer.third()
+    scale = stats_ref[1:2, :]
     upstream = scatter.finish()
-    scaled = (x_ref[...] - mean) * scale
+    scaled = (x_ref[...] - stats_ref[0:1, :]) * scale
+    sums = begin_back(place, upstream, scaled, gain, stat, everything, sums_send, sums_recv, 0)
     vec_slots[place.row] = vec_ref[...]
     vec_slots[place.row, 10:11, 0:size] = token_sum(upstream * scaled)
     vec_slots[place.row, 11:12, 0:size] = token_sum(upstream)
@@ -806,26 +992,17 @@
         )
         copy.start()
         vec_copies.append(copy)
-    back = norm_back(
-        place, upstream, scaled, scale, gain_ref[...], 4.0 * size, stat, sums_send, sums_recv
-    )
-    gin_ref[...] = gx_ref[...] + back
-    line_a.step(2)
-    line_b.finish(total_b)
-    theirs = pl.ds(pl.multiple_of((1 - place.y) * rows, rows), rows)
-    y_stage[...] = total_b[theirs, :].astype(y_stage.dtype)
-    last = remote(y_stage, y_last, y_send.at[4], y_recv.at[4], y_peer)
-    last.start()
-    line_a.finish(sums_ref.at[:, first])
+    summer.fourth()
+    gin_ref[...] = gx_ref[...] + end_back(sums, upstream, scaled, scale, gain, 4.0 * size)
+    summer.fifth()
+    out_ref[...] = out_scatter.finish() + mid_ref[...] + par_ref[:, BIAS_FC2 : BIAS_FC2 + 1]
+    summer.finish(first_out, second_out)
     for copy in vec_copies:
         copy.wait()
     total = vec_slots[0]
     for index in range(1, 8):
         total = total + vec_slots[index]
     vecs_ref[...] = total
-    last.wait()
-    ours = pl.ds(pl.multiple_of(place.y * rows, rows), rows)
-    sums_ref[:, second] = total_b[ours, :] + y_last[...].astype(jnp.float32)
 
 
 def communicate(kernel, number, shapes, scratch, *operands):
@@ -973,60 +1150,66 @@
     rows, hidden_size = w_fc1.shape
     width = 4 * size + 2 * hidden_size
     scaling = HEAD_DIM ** (-0.5)
-    seq_ends = jnp.cumsum(seq_lengths[0])
     places = jnp.arange(tokens, dtype=jnp.int32)
-    segment = jnp.sum((places[:, None] >= seq_ends[None, :]).astype(jnp.int32), axis=1)
+    ends = [seq_lengths[0, 0]]
+    for index in range(1, 3):
+        ends.append(ends[-1] + seq_lengths[0, index])
+    segment = sum((places >= end).astype(jnp.int32) for end in ends)
     key_seg, query_seg = segment[:, None], segment[None, :]
-    packed = jnp.concatenate([w_query, w_key, w_value, w_out.T, w_fc1, w_fc2.T], axis=1)
+    packed = jnp.concatenate([w_query, w_key, w_value, w_out.T], axis=1)
+    params = jnp.stack([ln1_gain, ln1_bias, b_out, ln2_gain, ln2_bias, b_fc2], axis=1)
     stat = pltpu.VMEM((4, 8, tokens), wide)
     slots = pltpu.VMEM((3, size, tokens), half)
     stage = pltpu.VMEM((size, tokens), half)
+    own_f32 = ((size, tokens), wide)
+    all_half = ((full, tokens), half)
+    stats_shape = ((8, tokens), wide)
+    each = 3 * CHUNKS
 
     normed1, grad_mlp, stats1, weights = communicate(
         enter_kernel,
         1,
-        [((full, tokens), half), ((full, tokens), half), ((8, tokens), wide), ((8 * rows, width), half)],
-        [stat] + sems(3, 3, 3, 8, 8, 6),
+        [all_half, all_half, stats_shape, ((full, full), half)],
+        [stat] + sems(each, each, each) + row_gather_scratch(),
         layer_input,
         cotangent,
-        ln1_gain[:, None],
-        ln1_bias[:, None],
+        params,
         packed,
     )
-    w_qkv, w_up = weights[:, : 3 * size], weights[:, 3 * size : 4 * size]
-    w_first = weights[:, 4 * size : 4 * size + hidden_size]
-    w_second = weights[:, 4 * size + hidden_size :]
+    w_qkv, w_up = weights[:, : 3 * size], weights[:, 3 * size :]
     qkv_bias = jnp.concatenate([b_query, jnp.zeros_like(b_query), b_value])[:, None]
     qkv_scale = jnp.where(jnp.arange(3 * size) < size, scaling, 1.0)[:, None]
     qkv = to_half((left_product(w_qkv, normed1) + qkv_bias) * qkv_scale)
     mixed, log_total = attend(qkv, key_seg, query_seg)
-    middle, normed2, stats2 = communicate(
+    middle, normed2, stats2, w_first, w_second = communicate(
         middle_kernel,
         2,
-        [((size, tokens), wide), ((full, tokens), half), ((8, tokens), wide)],
-        [slots, stage, stat] + sems(3, 3, 3),
+        [own_f32, all_half, stats_shape] + [((8 * rows, hidden_size), half)] * 2,
+        [slots, stage, stat] + sems(each, each, each) + row_gather_scratch(),
         to_half(product(w_up, mixed)),
         layer_input,
-        b_out[:, None],
-        ln2_gain[:, None],
-        ln2_bias[:, None],
+        params,
+        w_fc1,
+        w_fc2.T,
     )
     hidden_pre = left_product(w_first, normed2) + b_fc1[:, None]
     activated, gate_pull = jax.vjp(smooth_gate, hidden_pre)
     hidden = to_half(activated)
     grad_pre = to_half(gate_pull(left_product(w_second, grad_mlp))[0])
-    output, grad_middle, grad_branch, norm2_sums = communicate(
+    grad_middle, grad_branch, norm2_sums, sum_first, sum_second = communicate(
         turn_kernel,
         3,
-        [((size, tokens), wide), ((size, tokens), wide), ((full, tokens), half), ((8, size), wide)],
-        [slots, stage, slots, stage, stat] + sems(3, 3, 3, 3),
-        to_half(product(w_second, hidden)),
+        [own_f32, all_half, ((8, size), wide)] + [((rows, hidden_size), wide)] * 2,
+        [pltpu.VMEM((size, tokens), wide), slots, stage, stat]
+        + sems(each, each, each)
+        + row_scatter_scratch(rows, hidden_size, half, wide),
         to_half(product(w_first, grad_pre)),
         middle,
         cotangent,
         stats2,
-        ln2_gain[:, None],
-        b_fc2[:, None],
+        params,
+        to_half(right_product(normed2, grad_pre)),
+        to_half(right_product(grad_mlp, hidden)),
     )
     grad_mixed = to_half(left_product(w_up, grad_branch))
     grad_q, grad_k, grad_v = attend_back(qkv, grad_mixed, log_total, key_seg, query_seg)
@@ -1035,8 +1218,6 @@
         [
             to_half(right_product(normed1, grad_qkv)),
             to_half(right_product(grad_branch, mixed)),
-            to_half(right_product(normed2, grad_pre)),
-            to_half(right_product(grad_mlp, hidden)),
         ],
         axis=1,
     )
@@ -1057,27 +1238,21 @@
         axis=0,
     )
     vectors = jnp.pad(vectors, ((0, 0), (0, 256 - size)))
-    line_half = width // 2
-    grad_input, sums, vector_sums = communicate(
+    grad_input, output, sum_qk, sum_vo, vector_sums = communicate(
         leave_kernel,
         4,
-        [((size, tokens), wide), ((rows, width), wide), (vectors.shape, wide)],
-        [slots, stage, stat]
-        + sems(3, 3)
+        [own_f32, own_f32] + [((rows, full // 2), wide)] * 2 + [(vectors.shape, wide)],
+        [slots, stage, slots, stage, stat]
+        + sems(3, 3, 3)
         + [pltpu.VMEM((8,) + vectors.shape, wide)]
         + sems(7)
-        + [pltpu.VMEM((4, rows, line_half), half)] * 3
-        + [pltpu.VMEM((4, 2 * rows, line_half), half)] * 2
-        + [
-            pltpu.VMEM((2 * rows, line_half), wide),
-            pltpu.VMEM((rows, line_half), half),
-            pltpu.VMEM((rows, line_half), half),
-        ]
-        + sems(5, 8, 8),
+        + row_scatter_scratch(rows, full // 2, half, wide),
         to_half(product(w_qkv, grad_qkv)),
+        to_half(product(w_second, hidden)),
         layer_input,
+        middle,
         stats1,
-        ln1_gain[:, None],
+        params,
         grad_middle,
         grads,
         vectors,
@@ -1088,18 +1263,18 @@
         grad_input,
         vector_sums[10],
         vector_sums[11],
-        sums[:, :size],
-        sums[:, size : 2 * size],
-        sums[:, 2 * size : 3 * size],
+        sum_qk[:, :size],
+        sum_qk[:, size:],
+        sum_vo[:, :size],
         vector_sums[0],
         vector_sums[1],
-        sums[:, 3 * size : 4 * size].T,
+        sum_vo[:, size:].T,
         vector_sums[2],
         vector_sums[3],
         vector_sums[4],
-        sums[:, 4 * size : 4 * size + hidden_size],
+        sum_first,
         vector_sums[6:10].reshape(-1),
-        sums[:, 4 * size + hidden_size :].T,
+        sum_second.T,
         vector_sums[5],
     )
 

time: 296 us -> 254 us (0.86)
  Pallas kernels: 220 us -> 188 us
  local copies, waits for them, and re-layouts: 31.8 us -> 19.7 us
    pallas_call x4, Pallas kernels: 201 us -> 169 us  [communicate(): pl.pallas_call(kernel, out_shape=[jax.ShapeDtypeStruct(*shape) for shape...]
    broadcast_in_dim x7 -> x0, local copies, waits for them, and re-layouts: 9.67 us -> none  [the longest x1 1.44 us: fast_shards(): ln1_gain[:, None]]
    concatenate x2 -> x0, local copies, waits for them, and re-layouts: 7.75 us -> none  [the longest x1 6.02 us: fast_shards(): jnp.concatenate([to_half(right_product(normed1, grad_qkv)), to_half(right...]
    dot_general x4, matrix products: 14.6 us -> 10.5 us  [product(): return jnp.dot(first_op, second_op, preferred_element_type=jnp.float32)]
    unnamed x40 -> x52, local copies, waits for them, and re-layouts: 5.02 us -> 8.2 us
    slice x0 -> x2, local copies, waits for them, and re-layouts: none -> 3.06 us  [the longest x1 1.7 us: fast_shards(): sum_qk[:, size:]]
where the time goes in v2:
time: 254 us; the launch traced here: 253 us
  Pallas kernels  188 us (74%)
  matrix products  34 us (13%)
  local copies, waits for them, and re-layouts  19.7 us (8%)
  other arithmetic  8.38 us (3%)
  between operations  2.92 us (1%)
    pallas_call x4, Pallas kernels, communicate(): pl.pallas_call(kernel, out_shape=[jax.ShapeDtypeStruct(*shape) for shape...  169 us
    dot_general x4, matrix products, left_product(): lax.dot_general(first_op, second_op, (((0,), (0,)), ((), ())), preferred_...  13.9 us
    dot_general x4, matrix products, product(): return jnp.dot(first_op, second_op, preferred_element_type=jnp.float32)  10.5 us
    pallas_call x1, Pallas kernels, attend_back(): pl.pallas_call(attend_back_kernel, grid=(heads,), in_specs=[head_spec(tok...  10.4 us
    dot_general x4, matrix products, right_product(): lax.dot_general(first_op, second_op, (((1,), (1,)), ((), ())), preferred_...  9.55 us
    pallas_call x1, Pallas kernels, attend(): pl.pallas_call(attend_kernel, grid=(heads,), in_specs=[head_spec(tokens,...  9.19 us
    unnamed x52, local copies, waits for them, and re-layouts  8.2 us

profile of v2, /device:TPU:8, one launch (start us, length us, event | category | flops | bytes accessed | tf_op | source)
XLA Modules:
  0.0 253.2 jit_solution(9350281249307634258)
XLA Ops:
  0.7 0.0 copy-start.14
  0.7 0.0 copy-start.13
  0.7 1.4 fusion.17
  4.0 1.6 convert_add_fusion.key_seg_ref
  5.6 1.3 fusion.12.query_seg_ref
  6.8 0.8 stack.27
  7.6 0.8 copy.58.par_ref
  8.4 0.9 copy.57
  9.3 1.6 pad_maximum_fusion.1.w_ref
  10.9 30.8 %shard_map.305 = (bf16[768,1024]{1,0:T(8,128)(2,1)}, bf16[768,1024]{1,0:T(8,128)(2,1)}, f32[8,1024]{1,0:T(8,128)}, bf16[768,768]{1,0:T(8,128)(2,1)}) custom-call(f32[192,1024]{1,0:T(8,128)} %x_ref.5, f32[192,1024]{1,0:T(8,128)} %cot_ref.3, f32[192,6]{1,0:T(8,128)} %copy.58.par_ref, bf16[96,768]{1,0:T(8,128)(2,1)} %pad_maximum_fusion.1.w_ref), custom_call_target="tpu_custom_call" | custom-call | tf_op jit(solution)/shard_map/pallas_call | solution.py:1009
  41.8 0.0 copy-done.14
  41.8 0.0 copy-done.13
  41.8 0.1 pad_maximum_fusion.2
  41.8 3.9 %multiply_convert_fusion.1.q_ref.k_ref.v_ref = bf16[576,1024]{1,0:T(8,128)(2,1)} fusion(bf16[768,1024]{1,0:T(8,128)(2,1)} %get-tuple-element.42, f32[576]{0:T(1024)S(1)} %get-tuple-element.152, f32[576]{0:T(1024)S(1)} %get-tuple-element.151, bf16[768,768]{1,0:T(8,128)(2,1)} %get-tuple-element.41), kind=kOutput, calls=%fused_computation.11 | convolution fusion | flops 907739136 | bytes 3740160 | tf_op jit(solution)/shard_map/dot_general | solution.py:311
  45.8 9.2 %shard_map.306 = (bf16[192,1024]{1,0:T(8,128)(2,1)}, f32[3,1,1024]{2,1,0:T(1,128)}) custom-call(bf16[576,1024]{1,0:T(8,128)(2,1)} %multiply_convert_fusion.1.q_ref.k_ref.v_ref, bf16[576,1024]{1,0:T(8,128)(2,1)} %multiply_convert_fusion.1.q_ref.k_ref.v_ref, bf16[576,1024]{1,0:T(8,128)(2,1)} %multiply_convert_fusion.1.q_ref.k_ref.v_ref, ...), custom_call_target="tpu_custom_call" | custom-call | tf_op jit(solution)/shard_map/pallas_call | solution.py:1097
  55.0 0.0 copy-done.9
  55.0 2.8 %convolution_convert_fusion.3.part_ref = bf16[768,1024]{1,0:T(8,128)(2,1)} fusion(bf16[192,1024]{1,0:T(8,128)(2,1)} %get-tuple-element.43, bf16[768,768]{1,0:T(8,128)(2,1)S(1)} %copy-done.9), kind=kOutput, calls=%fused_computation.15 | convolution fusion | flops 302776320 | bytes 2359296 | tf_op jit(solution)/shard_map/dot_general | solution.py:23
  57.8 38.7 %shard_map.307 = (f32[192,1024]{1,0:T(8,128)}, bf16[768,1024]{1,0:T(8,128)(2,1)}, f32[8,1024]{1,0:T(8,128)}, bf16[768,768]{1,0:T(8,128)(2,1)}, bf16[768,768]{1,0:T(8,128)(2,1)}) custom-call(bf16[768,1024]{1,0:T(8,128)(2,1)} %convolution_convert_fusion.3.part_ref, f32[192,1024]{1,0:T(8,128)} %x_ref.5, f32[192,6]{1,0:T(8,128)} %copy.58.par_ref, ...), custom_call_target="tpu_custom_call" | custom-call | tf_op jit(solution)/shard_map/pallas_call | solution.py:1009
  96.5 0.0 copy-start.15
  96.5 0.0 copy-start.17
  96.5 0.0 copy-start.19
  96.5 3.3 %fusion.18 = f32[768,1024]{1,0:T(8,128)S(1)} fusion(bf16[768,768]{1,0:T(8,128)(2,1)} %get-tuple-element.44, bf16[768,1024]{1,0:T(8,128)(2,1)} %get-tuple-element.47), kind=kOutput, calls=%fused_computation.50 | convolution fusion | flops 1207959552 | bytes 5898240 | tf_op jit(solution)/shard_map/dot_general | solution.py:311
  99.8 0.0 copy-done.15
  99.8 0.0 copy-done.17
  99.8 0.0 copy-done.19
  99.9 3.9 %convert_reduce_fusion = (f32[768]{0:T(1024)S(1)}, bf16[768,1024]{1,0:T(8,128)(2,1)S(1)}, bf16[768,1024]{1,0:T(8,128)(2,1)S(1)}) fusion(f32[768,1024]{1,0:T(8,128)S(1)} %fusion.18, f32[768]{0:T(1024)S(1)} %copy-done.19, bf16[768,768]{1,0:T(8,128)(2,1)S(1)} %copy-done.17, bf16[768,1024]{1,0:T(8,128)(2,1)S(1)} %copy-done.15), kind=kOutput, calls=%fused_computation.9 | convolution fusion | flops 1227619584 | bytes 9050112 | tf_op jit(solution)/shard_map/dot_general | solution.py:311
  103.8 2.5 convolution_convert_fusion.4.second_ref
  106.3 0.0 copy-done.16
  106.3 2.5 convolution_convert_fusion.5.first_ref
  108.7 2.6 %convolution_convert_fusion.2.part_ref = bf16[768,1024]{1,0:T(8,128)(2,1)} fusion(bf16[768,768]{1,0:T(8,128)(2,1)S(1)} %copy-done.18, bf16[768,1024]{1,0:T(8,128)(2,1)S(1)} %get-tuple-element.134), kind=kOutput, calls=%fused_computation.14 | convolution fusion | flops 1208745984 | bytes 4325376 | tf_op jit(solution)/shard_map/dot_general | solution.py:23
  111.3 57.3 %shard_map.308 = (f32[192,1024]{1,0:T(8,128)}, bf16[768,1024]{1,0:T(8,128)(2,1)}, f32[8,192]{1,0:T(8,128)}, f32[96,768]{1,0:T(8,128)}, f32[96,768]{1,0:T(8,128)}) custom-call(bf16[768,1024]{1,0:T(8,128)(2,1)} %convolution_convert_fusion.2.part_ref, f32[192,1024]{1,0:T(8,128)} %get-tuple-element.48.mid_ref, f32[192,1024]{1,0:T(8,128)} %cot_ref.3, ...), custom_call_target="tpu_custom_call" | custom-call | tf_op jit(solution)/shard_map/pallas_call | solution.py:1009
  168.6 2.7 %convolution_convert_fusion.7.go_ref = bf16[192,1024]{1,0:T(8,128)(2,1)} fusion(bf16[768,1024]{1,0:T(8,128)(2,1)} %get-tuple-element.50, bf16[768,768]{1,0:T(8,128)(2,1)S(1)} %copy-done.9), kind=kOutput, calls=%fused_computation.19 | convolution fusion | flops 302186496 | bytes 2359296 | tf_op jit(solution)/shard_map/dot_general | solution.py:311
  171.3 10.4 %shard_map.309 = (bf16[192,1024]{1,0:T(8,128)(2,1)}, bf16[192,1024]{1,0:T(8,128)(2,1)}, bf16[192,1024]{1,0:T(8,128)(2,1)}) custom-call(bf16[576,1024]{1,0:T(8,128)(2,1)} %multiply_convert_fusion.1.q_ref.k_ref.v_ref, bf16[576,1024]{1,0:T(8,128)(2,1)} %multiply_convert_fusion.1.q_ref.k_ref.v_ref, bf16[576,1024]{1,0:T(8,128)(2,1)} %multiply_convert_fusion.1.q_ref.k_ref.v_ref, ...), custom_call_target="tpu_custom_call" | custom-call | tf_op jit(solution)/shard_map/pallas_call | solution.py:1115
  181.8 1.2 convert_reduce_fusion.4
  183.0 1.1 convert_reduce_fusion.3
  184.2 0.7 slice.72
  184.9 0.1 convert_reduce_fusion.2
  185.0 0.1 reshape.115
  185.1 0.1 convert_reduce_fusion.1
  185.2 0.1 concatenate.19
  185.3 0.6 pad.4.vec_ref
  186.1 1.0 copy-done.11
  187.1 2.5 %convolution_convert_fusion.6 = bf16[768,576]{0,1:T(8,128)(2,1)S(1)} fusion(bf16[768,1024]{1,0:T(8,128)(2,1)} %get-tuple-element.42, bf16[576,1024]{1,0:T(8,128)(2,1)S(1)} %constant_dynamic-update-slice_fusion), kind=kOutput, calls=%fused_computation.18 | convolution fusion | flops 906412032 | bytes 3637248 | tf_op jit(solution)/shard_map/dot_general | solution.py:317
  189.7 0.0 copy-start.5
  189.7 0.6 copy.62
  190.3 0.3 copy-done.5
  190.7 2.1 convolution_convert_fusion.8
  192.7 0.2 copy.63
  192.9 1.2 pad_maximum_fusion.grads_ref
  194.2 0.6 copy-done.21
  194.8 2.6 %convolution_convert_fusion.1.out_part_ref = bf16[768,1024]{1,0:T(8,128)(2,1)} fusion(bf16[768,768]{1,0:T(8,128)(2,1)S(1)} %copy-done.17, bf16[768,1024]{1,0:T(8,128)(2,1)S(1)} %copy-done.21), kind=kOutput, calls=%fused_computation.13 | convolution fusion | flops 1208745984 | bytes 4325376 | tf_op jit(solution)/shard_map/dot_general | solution.py:23
  197.3 0.0 copy-done.12
  197.3 2.5 convolution_convert_fusion.part_ref
  199.9 41.8 %shard_map.310 = (f32[192,1024]{1,0:T(8,128)}, f32[192,1024]{1,0:T(8,128)}, f32[96,384]{1,0:T(8,128)}, f32[96,384]{1,0:T(8,128)}, f32[16,256]{1,0:T(8,128)}) custom-call(bf16[768,1024]{1,0:T(8,128)(2,1)} %convolution_convert_fusion.part_ref, bf16[768,1024]{1,0:T(8,128)(2,1)} %convolution_convert_fusion.1.out_part_ref, f32[192,1024]{1,0:T(8,128)} %x_ref.5, ...), custom_call_target="tpu_custom_call" | custom-call | tf_op jit(solution)/shard_map/pallas_call | solution.py:1009
  241.7 1.7 slice_bitcast_fusion
  243.3 0.7 copy.65
  244.1 1.7 fusion.15
  245.8 1.5 fusion.16
  247.3 0.7 slice.84
  248.0 0.7 reshape.116
  248.7 2.1 copy.73
  250.8 0.9 copy.74
  251.7 0.7 copy.75
  252.4 0.7 copy.76
  (32 shorter events, 0.1 us)
Async XLA Ops:
  0.7 41.1 %copy-start.14 = (f32[192]{0:T(256)S(1)}, f32[192]{0:T(256)}, u32[]{:S(2)}) copy-start(f32[192]{0:T(256)} %param.24) | copy-start | bytes 2308
  0.7 41.1 %copy-start.13 = (f32[192]{0:T(256)S(1)}, f32[192]{0:T(256)}, u32[]{:S(2)}) copy-start(f32[192]{0:T(256)} %param.25) | copy-start | bytes 2308
  45.8 9.2 %copy-start.9 = (bf16[768,768]{1,0:T(8,128)(2,1)S(1)}, bf16[768,768]{1,0:T(8,128)(2,1)}, u32[]{:S(2)}) copy-start(bf16[768,768]{1,0:T(8,128)(2,1)} %get-tuple-element.41) | copy-start | bytes 3538948
  96.5 3.4 %copy-start.15 = (bf16[768,1024]{1,0:T(8,128)(2,1)S(1)}, bf16[768,1024]{1,0:T(8,128)(2,1)}, u32[]{:S(2)}) copy-start(bf16[768,1024]{1,0:T(8,128)(2,1)} %get-tuple-element.46) | copy-start | bytes 4718596
  96.5 3.4 %copy-start.17 = (bf16[768,768]{1,0:T(8,128)(2,1)S(1)}, bf16[768,768]{1,0:T(8,128)(2,1)}, u32[]{:S(2)}) copy-start(bf16[768,768]{1,0:T(8,128)(2,1)} %get-tuple-element.45) | copy-start | bytes 3538948
  96.5 3.4 %copy-start.19 = (f32[768]{0:T(1024)S(1)}, f32[768]{0:T(1024)}, u32[]{:S(2)}) copy-start(f32[768]{0:T(1024)} %param.31) | copy-start | bytes 9220
  103.8 2.5 copy-start.20
  103.8 2.5 copy-start.16
  106.3 2.5 copy-start.18
  171.3 13.5 %copy-start.1 = (f32[192,1024]{1,0:T(8,128)S(1)}, f32[192,1024]{1,0:T(8,128)}, u32[]{:S(2)}) copy-start(f32[192,1024]{1,0:T(8,128)} %get-tuple-element.56.gx_ref) | copy-start | bytes 2359300
  181.8 3.3 %copy-start = (f32[192,1024]{1,0:T(8,128)S(1)}, f32[192,1024]{1,0:T(8,128)}, u32[]{:S(2)}) copy-start(f32[192,1024]{1,0:T(8,128)} %cot_ref.3) | copy-start | bytes 2359300
  181.8 4.2 %copy-start.3 = (bf16[192,1024]{1,0:T(8,128)(2,1)S(1)}, bf16[192,1024]{1,0:T(8,128)(2,1)}, u32[]{:S(2)}) copy-start(bf16[192,1024]{1,0:T(8,128)(2,1)} %get-tuple-element.52) | copy-start | bytes 1179652
  181.8 4.2 %copy-start.6 = (bf16[192,1024]{1,0:T(8,128)(2,1)S(1)}, bf16[192,1024]{1,0:T(8,128)(2,1)}, u32[]{:S(2)}) copy-start(bf16[192,1024]{1,0:T(8,128)(2,1)} %get-tuple-element.53) | copy-start | bytes 1179652
  184.9 1.2 copy-start.2
  186.1 1.0 copy-start.11
  189.7 1.0 copy-start.5
  192.9 1.8 copy-start.21
  194.8 2.6 %copy-start.10 = (bf16[768,768]{1,0:T(8,128)(2,1)S(1)}, bf16[768,768]{1,0:T(8,128)(2,1)}, u32[]{:S(2)}) copy-start(bf16[768,768]{1,0:T(8,128)(2,1)} %get-tuple-element.41) | copy-start | bytes 3538948
  194.8 2.6 %copy-start.12 = (bf16[576,1024]{1,0:T(8,128)(2,1)S(1)}, bf16[576,1024]{1,0:T(8,128)(2,1)}, u32[]{:S(2)}) copy-start(bf16[576,1024]{1,0:T(8,128)(2,1)} %copy-done.11) | copy-start | bytes 3538948
  241.7 9.2 %copy-start.4 = (f32[192,1024]{1,0:T(8,128)S(1)}, f32[192,1024]{1,0:T(8,128)}, u32[]{:S(2)}) copy-start(f32[192,1024]{1,0:T(8,128)} %get-tuple-element.171) | copy-start | bytes 2359300
  248.7 3.0 %copy-start.8 = (f32[96,768]{1,0:T(8,128)S(1)}, f32[96,768]{1,0:T(8,128)}, u32[]{:S(2)}) copy-start(f32[96,768]{1,0:T(8,128)} %get-tuple-element.183) | copy-start | bytes 884740
  248.7 3.8 %copy-start.7 = (f32[96,768]{1,0:T(8,128)S(1)}, f32[96,768]{1,0:T(8,128)}, u32[]{:S(2)}) copy-start(f32[96,768]{1,0:T(8,128)} %get-tuple-element.64) | copy-start | bytes 884740

commit v3 on v2

--- a/solution.py
+++ b/solution.py
@@ -778,18 +778,20 @@
 
 
 def enter_kernel(
-    x_ref, cot_ref, par_ref, w_ref,
-    h_ref, gm_ref, stats_ref, full_ref,
-    stat, sums_send, sums_recv, h_send, h_recv, gm_send, gm_recv, *row_scratch,
+    x_ref, par_ref, wq_ref, wk_ref, wv_ref, wo_ref,
+    h_ref, stats_ref, full_ref,
+    stat, sums_send, sums_recv, h_send, h_recv, *row_scratch,
 ):
     place = Place()
     greet(place, True)
     size = x_ref.shape[0]
-    rows = w_ref.shape[0]
-    half = w_ref.shape[1] // 2
+    rows = wq_ref.shape[0]
+    half = 2 * size
     chunks = chunks_of(x_ref.shape[1])
     own = pl.ds(pl.multiple_of(place.col * size, size), size)
-    full_ref[pl.ds(pl.multiple_of(place.row * rows, rows), rows), :] = w_ref[...]
+    own_rows = pl.ds(pl.multiple_of(place.row * rows, rows), rows)
+    for index, ref in enumerate((wq_ref, wk_ref, wv_ref, wo_ref)):
+        full_ref[own_rows, index * size : (index + 1) * size] = ref[...]
     gather = RowGather(
         place, (full_ref, pl.ds(0, half)), (full_ref, pl.ds(half, half)), rows, *row_scratch
     )
@@ -798,7 +800,6 @@
         begin_stats(place, x_ref[:, cols], stat, cols, sums_send, sums_recv, 3 * index)
         for index, cols in enumerate(chunks)
     ]
-    gm_ref[own, :] = cot_ref[...].astype(gm_ref.dtype)
     gathers = []
     for index, cols in enumerate(chunks):
         mean, scale = end_stats(sums[index], 4.0 * size)
@@ -808,26 +809,22 @@
         h_ref[own, cols] = (normed + par_ref[:, SHIFT1 : SHIFT1 + 1]).astype(h_ref.dtype)
         gathers.append(ColGather(place, h_ref, cols, h_send, h_recv, 3 * index))
         gathers[-1].start()
-    for index, cols in enumerate(chunks):
-        gathers.append(ColGather(place, gm_ref, cols, gm_send, gm_recv, 3 * index))
-        gathers[-1].start()
     gather.second_start()
     gather.step(1)
     gathers[0].forward()
     gather.step(2)
     gathers[1].forward()
     gather.step(3)
-    for item in gathers[2:]:
-        item.forward()
     for item in gathers:
         item.finish()
     gather.finish()
 
 
 def middle_kernel(
-    part_ref, x_ref, par_ref, first_ref, second_ref,
-    mid_ref, h_ref, stats_ref, full_first, full_second,
-    slots, stage, stat, rs_send, rs_recv, sums_send, sums_recv, h_send, h_recv, *row_scratch,
+    part_ref, x_ref, cot_ref, par_ref, first_ref, second_ref,
+    mid_ref, h_ref, gm_ref, stats_ref, full_first, full_second,
+    slots, stage, stat, rs_send, rs_recv, sums_send, sums_recv, h_send, h_recv,
+    gm_send, gm_recv, *row_scratch,
 ):
     place = Place()
     greet(place, True)
@@ -851,6 +848,7 @@
     gather.start()
     for item in scatters:
         item.forward()
+    gm_ref[own, :] = cot_ref[...].astype(gm_ref.dtype)
     gather.second_start()
     sums, gathers = [], []
 
@@ -875,19 +873,23 @@
     gather.step(1)
     begin(1)
     end(1)
+    everywhere = pl.ds(0, x_ref.shape[1])
+    gathers.append(ColGather(place, gm_ref, everywhere, gm_send, gm_recv, 0))
+    gathers[2].start()
     gathers[0].forward()
     gather.step(2)
     gathers[1].forward()
     gather.step(3)
+    gathers[2].forward()
     for item in gathers:
         item.finish()
     gather.finish()
 
 
 def turn_kernel(
-    part_ref, mid_ref, cot_ref, stats_ref, par_ref, first_ref, second_ref,
-    gx_ref, ga_ref, vec_ref, first_out, second_out,
-    up_keep, slots, stage, stat, rs_send, rs_recv, sums_send, sums_recv, ga_send, ga_recv,
+    part_ref, out_part_ref, mid_ref, cot_ref, stats_ref, par_ref, first_ref, second_ref,
+    gx_ref, ga_ref, out_ref, vec_ref, first_out, second_out,
+    up_keep, slots, stage, out_slots, out_stage, stat, rs_send, rs_recv, out_send, out_recv, sums_send, sums_recv, ga_send, ga_recv,
     *row_scratch,
 ):
     place = Place()
@@ -908,6 +910,10 @@
         place, (first_ref, everything), (second_ref, everything), rows, *row_scratch
     )
     summer.start()
+    out_scatter = ColScatter(
+        place, out_part_ref, out_slots, out_stage, pl.ds(0, mid_ref.shape[1]), out_send, out_recv, 0
+    )
+    out_scatter.start()
     for item in scatters:
         item.forward()
     summer.second_start()
@@ -934,6 +940,7 @@
     turn(0)
     summer.third()
     turn(1)
+    out_scatter.forward()
     summer.fourth()
     gathers[0].forward()
     summer.fifth()
@@ -942,14 +949,14 @@
     vec_ref[1:2, :] = token_sum(up_keep[...])
     for item in gathers:
         item.finish()
+    out_ref[...] = out_scatter.finish() + mid_ref[...] + par_ref[:, BIAS_FC2 : BIAS_FC2 + 1]
     summer.finish(first_out, second_out)
 
 
 def leave_kernel(
-    part_ref, out_part_ref, x_ref, mid_ref, stats_ref, par_ref, gx_ref, grads_ref, vec_ref,
-    gin_ref, out_ref, first_out, second_out, vecs_ref,
-    slots, stage, out_slots, out_stage, stat,
-    rs_send, rs_recv, out_send, out_recv, sums_send, sums_recv,
+    part_ref, x_ref, stats_ref, par_ref, gx_ref, grads_ref, vec_ref,
+    gin_ref, first_out, second_out, vecs_ref,
+    slots, stage, stat, rs_send, rs_recv, sums_send, sums_recv,
     vec_slots, vec_send, vec_recv, *row_scratch,
 ):
     place = Place()
@@ -965,14 +972,8 @@
         place, (grads_ref, pl.ds(0, half)), (grads_ref, pl.ds(half, half)), rows, *row_scratch
     )
     summer.start()
-    out_scatter = ColScatter(
-        place, out_part_ref, out_slots, out_stage, everything, out_send, out_recv, 0
-    )
-    out_scatter.start()
     scatter.forward()
-    out_scatter.forward()
     summer.second_start()
-    summer.third()
     scale = stats_ref[1:2, :]
     upstream = scatter.finish()
     scaled = (x_ref[...] - stats_ref[0:1, :]) * scale
@@ -992,10 +993,10 @@
         )
         copy.start()
         vec_copies.append(copy)
+    summer.third()
+    gin_ref[...] = gx_ref[...] + end_back(sums, upstream, scaled, scale, gain, 4.0 * size)
     summer.fourth()
-    gin_ref[...] = gx_ref[...] + end_back(sums, upstream, scaled, scale, gain, 4.0 * size)
     summer.fifth()
-    out_ref[...] = out_scatter.finish() + mid_ref[...] + par_ref[:, BIAS_FC2 : BIAS_FC2 + 1]
     summer.finish(first_out, second_out)
     for copy in vec_copies:
         copy.wait()
@@ -1025,22 +1026,26 @@
     return pairs
 
 
-def allowed_pairs(keys, start, width, key_seg, query_seg):
-    key_pos = lax.broadcasted_iota(jnp.int32, (keys, width), 0)
-    query_pos = lax.broadcasted_iota(jnp.int32, (keys, width), 1) + start
+def allowed_pairs(keys, start, width, len_ref):
+    key_pos = lax.broadcasted_iota(jnp.int32, (keys, 1), 0)
+    query_pos = lax.broadcasted_iota(jnp.int32, (1, width), 1) + start
+    key_seg, query_seg = jnp.zeros_like(key_pos), jnp.zeros_like(query_pos)
+    end = 0
+    for index in range(len_ref.shape[1]):
+        end += len_ref[0, index]
+        key_seg += jnp.where(key_pos >= end, 1, 0)
+        query_seg += jnp.where(query_pos >= end, 1, 0)
     return (key_seg == query_seg) & (key_pos <= query_pos)
 
 
-def attend_kernel(q_ref, k_ref, v_ref, key_seg_ref, query_seg_ref, o_ref, log_ref):
+def attend_kernel(q_ref, k_ref, v_ref, len_ref, o_ref, log_ref):
     tokens = q_ref.shape[1]
     width = tokens // 4
     for start in range(0, tokens, width):
         keys = start + width
         mine = pl.ds(start, width)
         scores = left_product(k_ref[:, 0:keys], q_ref[:, mine])
-        allowed = allowed_pairs(
-            keys, start, width, key_seg_ref[0:keys, :], query_seg_ref[:, mine]
-        )
+        allowed = allowed_pairs(keys, start, width, len_ref)
         scores = jnp.where(allowed, scores, NEG)
         top = jnp.max(scores, axis=0, keepdims=True)
         expo = jnp.exp(scores - top)
@@ -1051,7 +1056,7 @@
 
 
 def attend_back_kernel(
-    q_ref, k_ref, v_ref, go_ref, log_ref, key_seg_ref, query_seg_ref,
+    q_ref, k_ref, v_ref, go_ref, log_ref, len_ref,
     gq_ref, gk_ref, gv_ref, gk_sum, gv_sum,
 ):
     tokens = q_ref.shape[1]
@@ -1063,9 +1068,7 @@
         mine = pl.ds(start, width)
         queries, upstream = q_ref[:, mine], go_ref[:, mine]
         scores = left_product(k_ref[:, 0:keys], queries)
-        allowed = allowed_pairs(
-            keys, start, width, key_seg_ref[0:keys, :], query_seg_ref[:, mine]
-        )
+        allowed = allowed_pairs(keys, start, width, len_ref)
         probs = jnp.exp(jnp.where(allowed, scores, NEG) - log_ref[0, :, mine])
         grad_probs = left_product(v_ref[:, 0:keys], upstream)
         inner = jnp.sum(probs * grad_probs, axis=0, keepdims=True)
@@ -1082,15 +1085,15 @@
     return pl.BlockSpec((HEAD_DIM, tokens), lambda head: (head + offset, 0))
 
 
-def whole_spec(shape):
-    return pl.BlockSpec(shape, lambda head: (0,) * len(shape))
+def len_spec():
+    return pl.BlockSpec(memory_space=pltpu.SMEM)
 
 
 def local_params():
     return pltpu.CompilerParams(vmem_limit_bytes=VMEM_LIMIT)
 
 
-def attend(qkv, key_seg, query_seg):
+def attend(qkv, lengths):
     size, tokens = qkv.shape[0] // 3, qkv.shape[1]
     heads = size // HEAD_DIM
     log_spec = pl.BlockSpec((1, 1, tokens), lambda head: (head, 0, 0))
@@ -1098,17 +1101,17 @@
         attend_kernel,
         grid=(heads,),
         in_specs=[head_spec(tokens, part * heads) for part in range(3)]
-        + [whole_spec((tokens, 1)), whole_spec((1, tokens))],
+        + [len_spec()],
         out_specs=[head_spec(tokens, 0), log_spec],
         out_shape=[
             jax.ShapeDtypeStruct((size, tokens), jnp.bfloat16),
             jax.ShapeDtypeStruct((heads, 1, tokens), jnp.float32),
         ],
         compiler_params=local_params(),
-    )(qkv, qkv, qkv, key_seg, query_seg)
-
-
-def attend_back(qkv, grad_mixed, log_total, key_seg, query_seg):
+    )(qkv, qkv, qkv, lengths)
+
+
+def attend_back(qkv, grad_mixed, log_total, lengths):
     size, tokens = qkv.shape[0] // 3, qkv.shape[1]
     heads = size // HEAD_DIM
     log_spec = pl.BlockSpec((1, 1, tokens), lambda head: (head, 0, 0))
@@ -1116,12 +1119,12 @@
         attend_back_kernel,
         grid=(heads,),
         in_specs=[head_spec(tokens, part * heads) for part in range(3)]
-        + [head_spec(tokens, 0), log_spec, whole_spec((tokens, 1)), whole_spec((1, tokens))],
+        + [head_spec(tokens, 0), log_spec, len_spec()],
         out_specs=[head_spec(tokens, 0)] * 3,
         out_shape=[jax.ShapeDtypeStruct((size, tokens), jnp.bfloat16)] * 3,
         scratch_shapes=[pltpu.VMEM((HEAD_DIM, tokens), jnp.float32)] * 2,
         compiler_params=local_params(),
-    )(qkv, qkv, qkv, grad_mixed, log_total, key_seg, query_seg)
+    )(qkv, qkv, qkv, grad_mixed, log_total, lengths)
 
 
 def fast_shards(
@@ -1150,13 +1153,6 @@
     rows, hidden_size = w_fc1.shape
     width = 4 * size + 2 * hidden_size
     scaling = HEAD_DIM ** (-0.5)
-    places = jnp.arange(tokens, dtype=jnp.int32)
-    ends = [seq_lengths[0, 0]]
-    for index in range(1, 3):
-        ends.append(ends[-1] + seq_lengths[0, index])
-    segment = sum((places >= end).astype(jnp.int32) for end in ends)
-    key_seg, query_seg = segment[:, None], segment[None, :]
-    packed = jnp.concatenate([w_query, w_key, w_value, w_out.T], axis=1)
     params = jnp.stack([ln1_gain, ln1_bias, b_out, ln2_gain, ln2_bias, b_fc2], axis=1)
     stat = pltpu.VMEM((4, 8, tokens), wide)
     slots = pltpu.VMEM((3, size, tokens), half)
@@ -1166,28 +1162,31 @@
     stats_shape = ((8, tokens), wide)
     each = 3 * CHUNKS
 
-    normed1, grad_mlp, stats1, weights = communicate(
+    normed1, stats1, weights = communicate(
         enter_kernel,
         1,
-        [all_half, all_half, stats_shape, ((full, full), half)],
-        [stat] + sems(each, each, each) + row_gather_scratch(),
+        [all_half, stats_shape, ((full, full), half)],
+        [stat] + sems(each, each) + row_gather_scratch(),
         layer_input,
-        cotangent,
         params,
-        packed,
+        w_query,
+        w_key,
+        w_value,
+        w_out.T,
     )
     w_qkv, w_up = weights[:, : 3 * size], weights[:, 3 * size :]
     qkv_bias = jnp.concatenate([b_query, jnp.zeros_like(b_query), b_value])[:, None]
     qkv_scale = jnp.where(jnp.arange(3 * size) < size, scaling, 1.0)[:, None]
     qkv = to_half((left_product(w_qkv, normed1) + qkv_bias) * qkv_scale)
-    mixed, log_total = attend(qkv, key_seg, query_seg)
-    middle, normed2, stats2, w_first, w_second = communicate(
+    mixed, log_total = attend(qkv, seq_lengths)
+    middle, normed2, grad_mlp, stats2, w_first, w_second = communicate(
         middle_kernel,
         2,
-        [own_f32, all_half, stats_shape] + [((8 * rows, hidden_size), half)] * 2,
-        [slots, stage, stat] + sems(each, each, each) + row_gather_scratch(),
+        [own_f32, all_half, all_half, stats_shape] + [((8 * rows, hidden_size), half)] * 2,
+        [slots, stage, stat] + sems(each, each, each, 3) + row_gather_scratch(),
         to_half(product(w_up, mixed)),
         layer_input,
+        cotangent,
         params,
         w_fc1,
         w_fc2.T,
@@ -1196,14 +1195,15 @@
     activated, gate_pull = jax.vjp(smooth_gate, hidden_pre)
     hidden = to_half(activated)
     grad_pre = to_half(gate_pull(left_product(w_second, grad_mlp))[0])
-    grad_middle, grad_branch, norm2_sums, sum_first, sum_second = communicate(
+    grad_middle, grad_branch, output, norm2_sums, sum_first, sum_second = communicate(
         turn_kernel,
         3,
-        [own_f32, all_half, ((8, size), wide)] + [((rows, hidden_size), wide)] * 2,
-        [pltpu.VMEM((size, tokens), wide), slots, stage, stat]
-        + sems(each, each, each)
+        [own_f32, all_half, own_f32, ((8, size), wide)] + [((rows, hidden_size), wide)] * 2,
+        [pltpu.VMEM((size, tokens), wide), slots, stage, slots, stage, stat]
+        + sems(each, 3, each, each)
         + row_scatter_scratch(rows, hidden_size, half, wide),
         to_half(product(w_first, grad_pre)),
+        to_half(product(w_second, hidden)),
         middle,
         cotangent,
         stats2,
@@ -1212,7 +1212,7 @@
         to_half(right_product(grad_mlp, hidden)),
     )
     grad_mixed = to_half(left_product(w_up, grad_branch))
-    grad_q, grad_k, grad_v = attend_back(qkv, grad_mixed, log_total, key_seg, query_seg)
+    grad_q, grad_k, grad_v = attend_back(qkv, grad_mixed, log_total, seq_lengths)
     grad_qkv = jnp.concatenate([grad_q, grad_k, grad_v], axis=0)
     grads = jnp.concatenate(
         [
@@ -1238,19 +1238,17 @@
         axis=0,
     )
     vectors = jnp.pad(vectors, ((0, 0), (0, 256 - size)))
-    grad_input, output, sum_qk, sum_vo, vector_sums = communicate(
+    grad_input, sum_qk, sum_vo, vector_sums = communicate(
         leave_kernel,
         4,
-        [own_f32, own_f32] + [((rows, full // 2), wide)] * 2 + [(vectors.shape, wide)],
-        [slots, stage, slots, stage, stat]
-        + sems(3, 3, 3)
+        [own_f32] + [((rows, full // 2), wide)] * 2 + [(vectors.shape, wide)],
+        [slots, stage, stat]
+        + sems(3, 3)
         + [pltpu.VMEM((8,) + vectors.shape, wide)]
         + sems(7)
         + row_scatter_scratch(rows, full // 2, half, wide),
         to_half(product(w_qkv, grad_qkv)),
-        to_half(product(w_second, hidden)),
         layer_input,
-        middle,
         stats1,
         params,
         grad_middle,

time: 254 us -> 247 us (0.972)
  other arithmetic: 8.38 us -> 4.61 us
    add x2 -> x0, other arithmetic: 2.85 us -> none  [fast_shards(): segment = sum(((places >= end).astype(jnp.int32) for end in ends))]
    unnamed x52 -> x46, local copies, waits for them, and re-layouts: 8.2 us -> 7.61 us
where the time goes in v3:
time: 247 us; the launch traced here: 246 us
  Pallas kernels  189 us (77%)
  matrix products  33.9 us (14%)
  local copies, waits for them, and re-layouts  17.8 us (7%)
  other arithmetic  4.61 us (2%)
    pallas_call x4, Pallas kernels, communicate(): pl.pallas_call(kernel, out_shape=[jax.ShapeDtypeStruct(*shape) for shape...  170 us
    dot_general x4, matrix products, left_product(): lax.dot_general(first_op, second_op, (((0,), (0,)), ((), ())), preferred_...  13.9 us
    pallas_call x1, Pallas kernels, attend_back(): pl.pallas_call(attend_back_kernel, grid=(heads,), in_specs=[head_spec(tok...  10.5 us
    dot_general x4, matrix products, product(): return jnp.dot(first_op, second_op, preferred_element_type=jnp.float32)  10.4 us
    dot_general x4, matrix products, right_product(): lax.dot_general(first_op, second_op, (((1,), (1,)), ((), ())), preferred_...  9.58 us
    pallas_call x1, Pallas kernels, attend(): pl.pallas_call(attend_kernel, grid=(heads,), in_specs=[head_spec(tokens,...  8.89 us
    unnamed x46, local copies, waits for them, and re-layouts  7.61 us

profile of v3, /device:TPU:8, one launch (start us, length us, event | category | flops | bytes accessed | tf_op | source)
XLA Modules:
  0.0 246.2 jit_solution(5274676260188642535)
XLA Ops:
  0.7 0.8 stack.27
  1.4 0.8 copy.58.par_ref
  2.2 1.5 copy.57
  3.7 24.3 %shard_map.305 = (bf16[768,1024]{1,0:T(8,128)(2,1)}, f32[8,1024]{1,0:T(8,128)}, bf16[768,768]{1,0:T(8,128)(2,1)}) custom-call(f32[192,1024]{1,0:T(8,128)} %x_ref.5, f32[192,6]{1,0:T(8,128)} %copy.58.par_ref, bf16[96,192]{1,0:T(8,128)(2,1)} %wq_ref.1, bf16[96,192]{1,0:T(8,128)(2,1)} %wk_ref.1, bf16[96,192]{1,0:T(8,128)(2,1)} %wv_ref.1, bf16[96,192]{1,0:T(8,128)(2,1)} %bitcast.44), custom_call_target="tpu_custom_call" | custom-call | tf_op jit(solution)/shard_map/pallas_call | solution.py:1010
  28.1 0.8 pad_maximum_fusion.1
  28.9 3.9 %multiply_convert_fusion.1.q_ref.k_ref.v_ref = bf16[576,1024]{1,0:T(8,128)(2,1)} fusion(bf16[768,1024]{1,0:T(8,128)(2,1)} %get-tuple-element.42, f32[576]{0:T(1024)S(1)} %get-tuple-element.149, f32[576]{0:T(1024)S(1)} %get-tuple-element.148, bf16[768,768]{1,0:T(8,128)(2,1)} %get-tuple-element.41), kind=kOutput, calls=%fused_computation.11 | convolution fusion | flops 907739136 | bytes 3740160 | tf_op jit(solution)/shard_map/dot_general | solution.py:311
  32.8 8.9 %shard_map.306 = (bf16[192,1024]{1,0:T(8,128)(2,1)}, f32[3,1,1024]{2,1,0:T(1,128)}) custom-call(bf16[576,1024]{1,0:T(8,128)(2,1)} %multiply_convert_fusion.1.q_ref.k_ref.v_ref, bf16[576,1024]{1,0:T(8,128)(2,1)} %multiply_convert_fusion.1.q_ref.k_ref.v_ref, bf16[576,1024]{1,0:T(8,128)(2,1)} %multiply_convert_fusion.1.q_ref.k_ref.v_ref, s32[1,3]{1,0:T(1,128)} %len_ref.3), custom_call_target="tpu_custom_call" | custom-call | tf_op jit(solution)/shard_map/pallas_call | solution.py:1100
  41.7 0.0 copy-done.10
  41.7 2.8 %convolution_convert_fusion.3.part_ref = bf16[768,1024]{1,0:T(8,128)(2,1)} fusion(bf16[192,1024]{1,0:T(8,128)(2,1)} %get-tuple-element.43, bf16[768,768]{1,0:T(8,128)(2,1)S(1)} %copy-done.10), kind=kOutput, calls=%fused_computation.15 | convolution fusion | flops 302776320 | bytes 2359296 | tf_op jit(solution)/shard_map/dot_general | solution.py:23
  44.5 44.2 %shard_map.307 = (f32[192,1024]{1,0:T(8,128)}, bf16[768,1024]{1,0:T(8,128)(2,1)}, bf16[768,1024]{1,0:T(8,128)(2,1)}, f32[8,1024]{1,0:T(8,128)}, bf16[768,768]{1,0:T(8,128)(2,1)}, /*index=5*/bf16[768,768]{1,0:T(8,128)(2,1)}) custom-call(bf16[768,1024]{1,0:T(8,128)(2,1)} %convolution_convert_fusion.3.part_ref, f32[192,1024]{1,0:T(8,128)} %x_ref.5, ...), custom_call_target="tpu_custom_call" | custom-call | tf_op jit(solution)/shard_map/pallas_call | solution.py:1010
  88.7 0.0 copy-start.15
  88.7 0.0 copy-start.17
  88.7 0.0 copy-start.18
  88.7 3.3 %fusion.15 = f32[768,1024]{1,0:T(8,128)S(1)} fusion(bf16[768,768]{1,0:T(8,128)(2,1)} %get-tuple-element.44, bf16[768,1024]{1,0:T(8,128)(2,1)} %get-tuple-element.47), kind=kOutput, calls=%fused_computation.39 | convolution fusion | flops 1207959552 | bytes 5898240 | tf_op jit(solution)/shard_map/dot_general | solution.py:311
  92.0 0.0 copy-done.15
  92.1 0.0 copy-done.17
  92.1 0.0 copy-done.18
  92.1 3.9 %convert_reduce_fusion = (f32[768]{0:T(1024)S(1)}, bf16[768,1024]{1,0:T(8,128)(2,1)S(1)}, bf16[768,1024]{1,0:T(8,128)(2,1)S(1)}) fusion(f32[768,1024]{1,0:T(8,128)S(1)} %fusion.15, f32[768]{0:T(1024)S(1)} %copy-done.18, bf16[768,768]{1,0:T(8,128)(2,1)S(1)} %copy-done.17, bf16[768,1024]{1,0:T(8,128)(2,1)S(1)} %copy-done.15), kind=kOutput, calls=%fused_computation.9 | convolution fusion | flops 1227619584 | bytes 9050112 | tf_op jit(solution)/shard_map/dot_general | solution.py:311
  96.0 0.0 copy-start.14
  96.0 2.5 %convolution_convert_fusion.4.second_ref = bf16[768,768]{1,0:T(8,128)(2,1)} fusion(bf16[768,1024]{1,0:T(8,128)(2,1)S(1)} %copy-done.15, bf16[768,1024]{1,0:T(8,128)(2,1)S(1)} %get-tuple-element.135), kind=kOutput, calls=%fused_computation.16 | convolution fusion | flops 1208549376 | bytes 4325376 | tf_op jit(solution)/shard_map/dot_general | solution.py:317
  98.5 0.0 copy-done.14
  98.5 2.5 convolution_convert_fusion.5.first_ref
  101.0 2.5 %convolution_convert_fusion.1.out_part_ref = bf16[768,1024]{1,0:T(8,128)(2,1)} fusion(bf16[768,768]{1,0:T(8,128)(2,1)S(1)} %copy-done.17, bf16[768,1024]{1,0:T(8,128)(2,1)S(1)} %get-tuple-element.135), kind=kOutput, calls=%fused_computation.13 | convolution fusion | flops 1208745984 | bytes 4325376 | tf_op jit(solution)/shard_map/dot_general | solution.py:23
  103.5 0.0 copy-done.16
  103.5 2.6 %convolution_convert_fusion.2.part_ref = bf16[768,1024]{1,0:T(8,128)(2,1)} fusion(bf16[768,768]{1,0:T(8,128)(2,1)S(1)} %copy-done.16, bf16[768,1024]{1,0:T(8,128)(2,1)S(1)} %get-tuple-element.134), kind=kOutput, calls=%fused_computation.14 | convolution fusion | flops 1208745984 | bytes 4325376 | tf_op jit(solution)/shard_map/dot_general | solution.py:23
  106.1 65.9 %shard_map.308 = (f32[192,1024]{1,0:T(8,128)}, bf16[768,1024]{1,0:T(8,128)(2,1)}, f32[192,1024]{1,0:T(8,128)}, f32[8,192]{1,0:T(8,128)}, f32[96,768]{1,0:T(8,128)}, /*index=5*/f32[96,768]{1,0:T(8,128)}) custom-call(bf16[768,1024]{1,0:T(8,128)(2,1)} %convolution_convert_fusion.2.part_ref, bf16[768,1024]{1,0:T(8,128)(2,1)} %convolution_convert_fusion.1.out_part_ref, ...), custom_call_target="tpu_custom_call" | custom-call | tf_op jit(solution)/shard_map/pallas_call | solution.py:1010
  172.0 2.7 %convolution_convert_fusion.7.go_ref = bf16[192,1024]{1,0:T(8,128)(2,1)} fusion(bf16[768,1024]{1,0:T(8,128)(2,1)} %get-tuple-element.51, bf16[768,768]{1,0:T(8,128)(2,1)S(1)} %copy-done.10), kind=kOutput, calls=%fused_computation.19 | convolution fusion | flops 302186496 | bytes 2359296 | tf_op jit(solution)/shard_map/dot_general | solution.py:311
  174.8 10.5 %shard_map.309 = (bf16[192,1024]{1,0:T(8,128)(2,1)}, bf16[192,1024]{1,0:T(8,128)(2,1)}, bf16[192,1024]{1,0:T(8,128)(2,1)}) custom-call(bf16[576,1024]{1,0:T(8,128)(2,1)} %multiply_convert_fusion.1.q_ref.k_ref.v_ref, bf16[576,1024]{1,0:T(8,128)(2,1)} %multiply_convert_fusion.1.q_ref.k_ref.v_ref, bf16[576,1024]{1,0:T(8,128)(2,1)} %multiply_convert_fusion.1.q_ref.k_ref.v_ref, ...), custom_call_target="tpu_custom_call" | custom-call | tf_op jit(solution)/shard_map/pallas_call | solution.py:1118
  185.3 0.0 copy-start.7
  185.3 1.2 convert_reduce_fusion.4
  186.5 1.1 convert_reduce_fusion.3
  187.7 0.7 slice.60
  188.4 0.0 copy-done.1
  188.4 0.1 convert_reduce_fusion.2
  188.5 0.1 reshape.47
  188.6 0.0 copy-done
  188.6 0.1 convert_reduce_fusion.1
  188.7 0.1 concatenate.15
  188.9 0.6 pad.4.vec_ref
  189.5 0.0 copy-done.3
  189.5 0.0 copy-done.7
  189.5 0.0 copy-done.2
  189.6 0.0 copy-start.12
  189.6 1.0 copy-done.12
  190.6 2.5 %convolution_convert_fusion.6 = bf16[768,576]{0,1:T(8,128)(2,1)S(1)} fusion(bf16[768,1024]{1,0:T(8,128)(2,1)} %get-tuple-element.42, bf16[576,1024]{1,0:T(8,128)(2,1)S(1)} %constant_dynamic-update-slice_fusion), kind=kOutput, calls=%fused_computation.18 | convolution fusion | flops 906412032 | bytes 3637248 | tf_op jit(solution)/shard_map/dot_general | solution.py:317
  193.2 0.0 copy-start.6
  193.2 0.6 copy.61
  193.8 0.3 copy-done.6
  194.2 2.1 convolution_convert_fusion.8
  196.2 0.2 copy.62
  196.4 1.2 pad_maximum_fusion.grads_ref
  197.6 0.7 copy-done.13
  198.3 2.6 %convolution_convert_fusion.part_ref = bf16[768,1024]{1,0:T(8,128)(2,1)} fusion(bf16[576,1024]{1,0:T(8,128)(2,1)S(1)} %copy-done.13, bf16[768,768]{1,0:T(8,128)(2,1)S(1)} %copy-done.11), kind=kOutput, calls=%fused_computation.12 | convolution fusion | flops 906756096 | bytes 3735552 | tf_op jit(solution)/shard_map/dot_general | solution.py:23
  200.9 35.0 %shard_map.310 = (f32[192,1024]{1,0:T(8,128)}, f32[96,384]{1,0:T(8,128)}, f32[96,384]{1,0:T(8,128)}, f32[16,256]{1,0:T(8,128)}) custom-call(bf16[768,1024]{1,0:T(8,128)(2,1)} %convolution_convert_fusion.part_ref, f32[192,1024]{1,0:T(8,128)} %x_ref.5, f32[8,1024]{1,0:T(8,128)} %get-tuple-element.56.stats_ref, f32[192,6]{1,0:T(8,128)} %copy.58.par_ref, ...), custom_call_target="tpu_custom_call" | custom-call | tf_op jit(solution)/shard_map/pallas_call | solution.py:1010
  235.9 1.7 slice_bitcast_fusion
  237.7 0.7 copy.64
  238.4 1.7 fusion.13
  240.1 1.5 fusion.14
  241.6 0.7 slice.72
  242.3 0.7 reshape.48
  243.0 0.9 copy.71
  243.9 0.9 copy.72
  244.8 0.7 copy.73
  245.5 0.7 copy.74
  (22 shorter events, 0.1 us)
Async XLA Ops:
  32.8 8.9 %copy-start.10 = (bf16[768,768]{1,0:T(8,128)(2,1)S(1)}, bf16[768,768]{1,0:T(8,128)(2,1)}, u32[]{:S(2)}) copy-start(bf16[768,768]{1,0:T(8,128)(2,1)} %get-tuple-element.41) | copy-start | bytes 3538948
  88.7 3.4 %copy-start.15 = (bf16[768,1024]{1,0:T(8,128)(2,1)S(1)}, bf16[768,1024]{1,0:T(8,128)(2,1)}, u32[]{:S(2)}) copy-start(bf16[768,1024]{1,0:T(8,128)(2,1)} %get-tuple-element.46) | copy-start | bytes 4718596
  88.7 3.4 %copy-start.17 = (bf16[768,768]{1,0:T(8,128)(2,1)S(1)}, bf16[768,768]{1,0:T(8,128)(2,1)}, u32[]{:S(2)}) copy-start(bf16[768,768]{1,0:T(8,128)(2,1)} %get-tuple-element.45) | copy-start | bytes 3538948
  88.7 3.4 %copy-start.18 = (f32[768]{0:T(1024)S(1)}, f32[768]{0:T(1024)}, u32[]{:S(2)}) copy-start(f32[768]{0:T(1024)} %param.31) | copy-start | bytes 9220
  96.0 2.5 %copy-start.14 = (bf16[768,1024]{1,0:T(8,128)(2,1)S(1)}, bf16[768,1024]{1,0:T(8,128)(2,1)}, u32[]{:S(2)}) copy-start(bf16[768,1024]{1,0:T(8,128)(2,1)} %get-tuple-element.47) | copy-start | bytes 4718596
  101.0 2.5 %copy-start.16 = (bf16[768,768]{1,0:T(8,128)(2,1)S(1)}, bf16[768,768]{1,0:T(8,128)(2,1)}, u32[]{:S(2)}) copy-start(bf16[768,768]{1,0:T(8,128)(2,1)} %get-tuple-element.44) | copy-start | bytes 3538948
  174.8 13.6 %copy-start.1 = (f32[192,1024]{1,0:T(8,128)S(1)}, f32[192,1024]{1,0:T(8,128)}, u32[]{:S(2)}) copy-start(f32[192,1024]{1,0:T(8,128)} %get-tuple-element.57.gx_ref) | copy-start | bytes 2359300
  185.3 3.3 %copy-start = (f32[192,1024]{1,0:T(8,128)S(1)}, f32[192,1024]{1,0:T(8,128)}, u32[]{:S(2)}) copy-start(f32[192,1024]{1,0:T(8,128)} %cot_ref.3) | copy-start | bytes 2359300
  185.3 4.2 %copy-start.3 = (bf16[192,1024]{1,0:T(8,128)(2,1)S(1)}, bf16[192,1024]{1,0:T(8,128)(2,1)}, u32[]{:S(2)}) copy-start(bf16[192,1024]{1,0:T(8,128)(2,1)} %get-tuple-element.53) | copy-start | bytes 1179652
  185.3 4.2 %copy-start.7 = (bf16[192,1024]{1,0:T(8,128)(2,1)S(1)}, bf16[192,1024]{1,0:T(8,128)(2,1)}, u32[]{:S(2)}) copy-start(bf16[192,1024]{1,0:T(8,128)(2,1)} %get-tuple-element.54) | copy-start | bytes 1179652
  188.4 1.2 copy-start.2
  189.6 1.0 copy-start.12
  193.2 1.0 copy-start.6
  196.2 1.4 copy-start.11
  196.4 1.9 copy-start.13
  235.9 7.1 %copy-start.4 = (f32[192,1024]{1,0:T(8,128)S(1)}, f32[192,1024]{1,0:T(8,128)}, u32[]{:S(2)}) copy-start(f32[192,1024]{1,0:T(8,128)} %get-tuple-element.167) | copy-start | bytes 2359300
  235.9 8.0 %copy-start.5 = (f32[192,1024]{1,0:T(8,128)S(1)}, f32[192,1024]{1,0:T(8,128)}, u32[]{:S(2)}) copy-start(f32[192,1024]{1,0:T(8,128)} %get-tuple-element.168) | copy-start | bytes 2359300
  243.0 1.8 copy-start.9
  243.0 2.5 %copy-start.8 = (f32[96,768]{1,0:T(8,128)S(1)}, f32[96,768]{1,0:T(8,128)}, u32[]{:S(2)}) copy-start(f32[96,768]{1,0:T(8,128)} %get-tuple-element.64) | copy-start | bytes 884740

commit v4 on v3

--- a/solution.py
+++ b/solution.py
@@ -868,16 +868,18 @@
         gathers.append(ColGather(place, h_ref, cols, h_send, h_recv, 3 * index))
         gathers[-1].start()
 
+    gather.line_a.step(1)
     begin(0)
+    begin(1)
+    gather.line_b.step(1)
     end(0)
-    gather.step(1)
-    begin(1)
+    gather.line_a.step(2)
     end(1)
     everywhere = pl.ds(0, x_ref.shape[1])
     gathers.append(ColGather(place, gm_ref, everywhere, gm_send, gm_recv, 0))
     gathers[2].start()
+    gather.line_b.step(2)
     gathers[0].forward()
-    gather.step(2)
     gathers[1].forward()
     gather.step(3)
     gathers[2].forward()
@@ -917,34 +919,41 @@
     for item in scatters:
         item.forward()
     summer.second_start()
-    gathers = []
+    sums, gathers = [], []
 
     def scaled(cols):
         return (mid_ref[:, cols] - stats_ref[0:1, cols]) * stats_ref[1:2, cols]
 
-    def turn(index):
+    def begin(index):
         cols = chunks[index]
         upstream = scatters[index].finish()
         up_keep[:, cols] = upstream
         xhat = scaled(cols)
-        sums = begin_back(
-            place, upstream, xhat, gain, stat, cols, sums_send, sums_recv, 3 * index
+        sums.append(
+            begin_back(place, upstream, xhat, gain, stat, cols, sums_send, sums_recv, 3 * index)
         )
-        back = end_back(sums, upstream, xhat, stats_ref[1:2, cols], gain, 4.0 * size)
+
+    def end(index):
+        cols = chunks[index]
+        back = end_back(
+            sums[index], up_keep[:, cols], scaled(cols), stats_ref[1:2, cols], gain, 4.0 * size
+        )
         gx = cot_ref[:, cols] + back
         gx_ref[:, cols] = gx
         ga_ref[own, cols] = gx.astype(ga_ref.dtype)
         gathers.append(ColGather(place, ga_ref, cols, ga_send, ga_recv, 3 * index))
         gathers[-1].start()
 
-    turn(0)
     summer.third()
-    turn(1)
+    begin(0)
+    begin(1)
+    end(0)
+    end(1)
+    summer.fourth()
     out_scatter.forward()
-    summer.fourth()
     gathers[0].forward()
+    gathers[1].forward()
     summer.fifth()
-    gathers[1].forward()
     vec_ref[0:1, :] = token_sum(up_keep[...] * scaled(pl.ds(0, mid_ref.shape[1])))
     vec_ref[1:2, :] = token_sum(up_keep[...])
     for item in gathers:
@@ -972,8 +981,9 @@
         place, (grads_ref, pl.ds(0, half)), (grads_ref, pl.ds(half, half)), rows, *row_scratch
     )
     summer.start()
+    summer.second_start()
     scatter.forward()
-    summer.second_start()
+    summer.third()
     scale = stats_ref[1:2, :]
     upstream = scatter.finish()
     scaled = (x_ref[...] - stats_ref[0:1, :]) * scale
@@ -993,9 +1003,8 @@
         )
         copy.start()
         vec_copies.append(copy)
-    summer.third()
+    summer.fourth()
     gin_ref[...] = gx_ref[...] + end_back(sums, upstream, scaled, scale, gain, 4.0 * size)
-    summer.fourth()
     summer.fifth()
     summer.finish(first_out, second_out)
     for copy in vec_copies:

time: 247 us -> 250 us (1.012)
  Pallas kernels: 189 us -> 192 us
    pallas_call x4, Pallas kernels: 170 us -> 173 us  [communicate(): pl.pallas_call(kernel, out_shape=[jax.ShapeDtypeStruct(*shape) for shape...]
where the time goes in v4:
time: 250 us; the launch traced here: 249 us
  Pallas kernels  192 us (77%)
  matrix products  33.9 us (14%)
  local copies, waits for them, and re-layouts  17.8 us (7%)
  other arithmetic  4.61 us (2%)
    pallas_call x4, Pallas kernels, communicate(): pl.pallas_call(kernel, out_shape=[jax.ShapeDtypeStruct(*shape) for shape...  173 us
    dot_general x4, matrix products, left_product(): lax.dot_general(first_op, second_op, (((0,), (0,)), ((), ())), preferred_...  13.9 us
    pallas_call x1, Pallas kernels, attend_back(): pl.pallas_call(attend_back_kernel, grid=(heads,), in_specs=[head_spec(tok...  10.5 us
    dot_general x4, matrix products, product(): return jnp.dot(first_op, second_op, preferred_element_type=jnp.float32)  10.4 us
    dot_general x4, matrix products, right_product(): lax.dot_general(first_op, second_op, (((1,), (1,)), ((), ())), preferred_...  9.58 us
    pallas_call x1, Pallas kernels, attend(): pl.pallas_call(attend_kernel, grid=(heads,), in_specs=[head_spec(tokens,...  8.89 us
    unnamed x46, local copies, waits for them, and re-layouts  7.61 us

profile of v4, /device:TPU:8, one launch (start us, length us, event | category | flops | bytes accessed | tf_op | source)
XLA Modules:
  0.0 249.4 jit_solution(9163170221655159145)
XLA Ops:
  0.7 0.8 stack.27
  1.4 0.8 copy.58.par_ref
  2.2 1.5 copy.57
  3.7 24.3 %shard_map.305 = (bf16[768,1024]{1,0:T(8,128)(2,1)}, f32[8,1024]{1,0:T(8,128)}, bf16[768,768]{1,0:T(8,128)(2,1)}) custom-call(f32[192,1024]{1,0:T(8,128)} %x_ref.5, f32[192,6]{1,0:T(8,128)} %copy.58.par_ref, bf16[96,192]{1,0:T(8,128)(2,1)} %wq_ref.1, bf16[96,192]{1,0:T(8,128)(2,1)} %wk_ref.1, bf16[96,192]{1,0:T(8,128)(2,1)} %wv_ref.1, bf16[96,192]{1,0:T(8,128)(2,1)} %bitcast.44), custom_call_target="tpu_custom_call" | custom-call | tf_op jit(solution)/shard_map/pallas_call | solution.py:1019
  28.1 0.8 pad_maximum_fusion.1
  28.9 3.9 %multiply_convert_fusion.1.q_ref.k_ref.v_ref = bf16[576,1024]{1,0:T(8,128)(2,1)} fusion(bf16[768,1024]{1,0:T(8,128)(2,1)} %get-tuple-element.42, f32[576]{0:T(1024)S(1)} %get-tuple-element.149, f32[576]{0:T(1024)S(1)} %get-tuple-element.148, bf16[768,768]{1,0:T(8,128)(2,1)} %get-tuple-element.41), kind=kOutput, calls=%fused_computation.11 | convolution fusion | flops 907739136 | bytes 3740160 | tf_op jit(solution)/shard_map/dot_general | solution.py:311
  32.8 8.9 %shard_map.306 = (bf16[192,1024]{1,0:T(8,128)(2,1)}, f32[3,1,1024]{2,1,0:T(1,128)}) custom-call(bf16[576,1024]{1,0:T(8,128)(2,1)} %multiply_convert_fusion.1.q_ref.k_ref.v_ref, bf16[576,1024]{1,0:T(8,128)(2,1)} %multiply_convert_fusion.1.q_ref.k_ref.v_ref, bf16[576,1024]{1,0:T(8,128)(2,1)} %multiply_convert_fusion.1.q_ref.k_ref.v_ref, s32[1,3]{1,0:T(1,128)} %len_ref.3), custom_call_target="tpu_custom_call" | custom-call | tf_op jit(solution)/shard_map/pallas_call | solution.py:1109
  41.7 0.0 copy-done.10
  41.7 2.8 %convolution_convert_fusion.3.part_ref = bf16[768,1024]{1,0:T(8,128)(2,1)} fusion(bf16[192,1024]{1,0:T(8,128)(2,1)} %get-tuple-element.43, bf16[768,768]{1,0:T(8,128)(2,1)S(1)} %copy-done.10), kind=kOutput, calls=%fused_computation.15 | convolution fusion | flops 302776320 | bytes 2359296 | tf_op jit(solution)/shard_map/dot_general | solution.py:23
  44.5 41.5 %shard_map.307 = (f32[192,1024]{1,0:T(8,128)}, bf16[768,1024]{1,0:T(8,128)(2,1)}, bf16[768,1024]{1,0:T(8,128)(2,1)}, f32[8,1024]{1,0:T(8,128)}, bf16[768,768]{1,0:T(8,128)(2,1)}, /*index=5*/bf16[768,768]{1,0:T(8,128)(2,1)}) custom-call(bf16[768,1024]{1,0:T(8,128)(2,1)} %convolution_convert_fusion.3.part_ref, f32[192,1024]{1,0:T(8,128)} %x_ref.5, ...), custom_call_target="tpu_custom_call" | custom-call | tf_op jit(solution)/shard_map/pallas_call | solution.py:1019
  86.0 0.0 copy-start.15
  86.0 0.0 copy-start.17
  86.0 0.0 copy-start.18
  86.0 3.3 %fusion.15 = f32[768,1024]{1,0:T(8,128)S(1)} fusion(bf16[768,768]{1,0:T(8,128)(2,1)} %get-tuple-element.44, bf16[768,1024]{1,0:T(8,128)(2,1)} %get-tuple-element.47), kind=kOutput, calls=%fused_computation.39 | convolution fusion | flops 1207959552 | bytes 5898240 | tf_op jit(solution)/shard_map/dot_general | solution.py:311
  89.4 0.0 copy-done.15
  89.4 0.0 copy-done.17
  89.4 0.0 copy-done.18
  89.4 3.9 %convert_reduce_fusion = (f32[768]{0:T(1024)S(1)}, bf16[768,1024]{1,0:T(8,128)(2,1)S(1)}, bf16[768,1024]{1,0:T(8,128)(2,1)S(1)}) fusion(f32[768,1024]{1,0:T(8,128)S(1)} %fusion.15, f32[768]{0:T(1024)S(1)} %copy-done.18, bf16[768,768]{1,0:T(8,128)(2,1)S(1)} %copy-done.17, bf16[768,1024]{1,0:T(8,128)(2,1)S(1)} %copy-done.15), kind=kOutput, calls=%fused_computation.9 | convolution fusion | flops 1227619584 | bytes 9050112 | tf_op jit(solution)/shard_map/dot_general | solution.py:311
  93.3 0.0 copy-start.14
  93.3 2.5 %convolution_convert_fusion.4.second_ref = bf16[768,768]{1,0:T(8,128)(2,1)} fusion(bf16[768,1024]{1,0:T(8,128)(2,1)S(1)} %copy-done.15, bf16[768,1024]{1,0:T(8,128)(2,1)S(1)} %get-tuple-element.135), kind=kOutput, calls=%fused_computation.16 | convolution fusion | flops 1208549376 | bytes 4325376 | tf_op jit(solution)/shard_map/dot_general | solution.py:317
  95.8 0.0 copy-done.14
  95.8 2.5 convolution_convert_fusion.5.first_ref
  98.3 2.5 %convolution_convert_fusion.1.out_part_ref = bf16[768,1024]{1,0:T(8,128)(2,1)} fusion(bf16[768,768]{1,0:T(8,128)(2,1)S(1)} %copy-done.17, bf16[768,1024]{1,0:T(8,128)(2,1)S(1)} %get-tuple-element.135), kind=kOutput, calls=%fused_computation.13 | convolution fusion | flops 1208745984 | bytes 4325376 | tf_op jit(solution)/shard_map/dot_general | solution.py:23
  100.8 0.0 copy-done.16
  100.8 2.6 %convolution_convert_fusion.2.part_ref = bf16[768,1024]{1,0:T(8,128)(2,1)} fusion(bf16[768,768]{1,0:T(8,128)(2,1)S(1)} %copy-done.16, bf16[768,1024]{1,0:T(8,128)(2,1)S(1)} %get-tuple-element.134), kind=kOutput, calls=%fused_computation.14 | convolution fusion | flops 1208745984 | bytes 4325376 | tf_op jit(solution)/shard_map/dot_general | solution.py:23
  103.4 65.2 %shard_map.308 = (f32[192,1024]{1,0:T(8,128)}, bf16[768,1024]{1,0:T(8,128)(2,1)}, f32[192,1024]{1,0:T(8,128)}, f32[8,192]{1,0:T(8,128)}, f32[96,768]{1,0:T(8,128)}, /*index=5*/f32[96,768]{1,0:T(8,128)}) custom-call(bf16[768,1024]{1,0:T(8,128)(2,1)} %convolution_convert_fusion.2.part_ref, bf16[768,1024]{1,0:T(8,128)(2,1)} %convolution_convert_fusion.1.out_part_ref, ...), custom_call_target="tpu_custom_call" | custom-call | tf_op jit(solution)/shard_map/pallas_call | solution.py:1019
  168.6 2.7 %convolution_convert_fusion.7.go_ref = bf16[192,1024]{1,0:T(8,128)(2,1)} fusion(bf16[768,1024]{1,0:T(8,128)(2,1)} %get-tuple-element.51, bf16[768,768]{1,0:T(8,128)(2,1)S(1)} %copy-done.10), kind=kOutput, calls=%fused_computation.19 | convolution fusion | flops 302186496 | bytes 2359296 | tf_op jit(solution)/shard_map/dot_general | solution.py:311
  171.3 10.5 %shard_map.309 = (bf16[192,1024]{1,0:T(8,128)(2,1)}, bf16[192,1024]{1,0:T(8,128)(2,1)}, bf16[192,1024]{1,0:T(8,128)(2,1)}) custom-call(bf16[576,1024]{1,0:T(8,128)(2,1)} %multiply_convert_fusion.1.q_ref.k_ref.v_ref, bf16[576,1024]{1,0:T(8,128)(2,1)} %multiply_convert_fusion.1.q_ref.k_ref.v_ref, bf16[576,1024]{1,0:T(8,128)(2,1)} %multiply_convert_fusion.1.q_ref.k_ref.v_ref, ...), custom_call_target="tpu_custom_call" | custom-call | tf_op jit(solution)/shard_map/pallas_call | solution.py:1127
  181.9 0.0 copy-start.7
  181.9 1.2 convert_reduce_fusion.4
  183.1 1.1 convert_reduce_fusion.3
  184.2 0.7 slice.60
  184.9 0.0 copy-done.1
  184.9 0.1 convert_reduce_fusion.2
  185.1 0.1 reshape.47
  185.2 0.0 copy-done
  185.2 0.1 convert_reduce_fusion.1
  185.3 0.1 concatenate.15
  185.4 0.6 pad.4.vec_ref
  186.0 0.0 copy-done.3
  186.1 0.0 copy-done.2
  186.2 1.0 copy-done.12
  187.2 2.5 %convolution_convert_fusion.6 = bf16[768,576]{0,1:T(8,128)(2,1)S(1)} fusion(bf16[768,1024]{1,0:T(8,128)(2,1)} %get-tuple-element.42, bf16[576,1024]{1,0:T(8,128)(2,1)S(1)} %constant_dynamic-update-slice_fusion), kind=kOutput, calls=%fused_computation.18 | convolution fusion | flops 906412032 | bytes 3637248 | tf_op jit(solution)/shard_map/dot_general | solution.py:317
  189.7 0.0 copy-start.6
  189.7 0.6 copy.61
  190.4 0.3 copy-done.6
  190.7 2.1 convolution_convert_fusion.8
  192.8 0.2 copy.62
  193.0 0.0 copy-start.13
  193.0 1.2 pad_maximum_fusion.grads_ref
  194.2 0.7 copy-done.13
  194.9 2.6 %convolution_convert_fusion.part_ref = bf16[768,1024]{1,0:T(8,128)(2,1)} fusion(bf16[576,1024]{1,0:T(8,128)(2,1)S(1)} %copy-done.13, bf16[768,768]{1,0:T(8,128)(2,1)S(1)} %copy-done.11), kind=kOutput, calls=%fused_computation.12 | convolution fusion | flops 906756096 | bytes 3735552 | tf_op jit(solution)/shard_map/dot_general | solution.py:23
  197.5 41.6 %shard_map.310 = (f32[192,1024]{1,0:T(8,128)}, f32[96,384]{1,0:T(8,128)}, f32[96,384]{1,0:T(8,128)}, f32[16,256]{1,0:T(8,128)}) custom-call(bf16[768,1024]{1,0:T(8,128)(2,1)} %convolution_convert_fusion.part_ref, f32[192,1024]{1,0:T(8,128)} %x_ref.5, f32[8,1024]{1,0:T(8,128)} %get-tuple-element.56.stats_ref, f32[192,6]{1,0:T(8,128)} %copy.58.par_ref, ...), custom_call_target="tpu_custom_call" | custom-call | tf_op jit(solution)/shard_map/pallas_call | solution.py:1019
  239.1 1.7 slice_bitcast_fusion
  240.8 0.7 copy.64
  241.5 1.7 fusion.13
  243.2 1.5 fusion.14
  244.8 0.7 slice.72
  245.5 0.7 reshape.48
  246.2 0.9 copy.71
  247.0 0.0 copy-done.5
  247.0 0.9 copy.72
  247.9 0.7 copy.73
  248.6 0.7 copy.74
  (22 shorter events, 0.1 us)
Async XLA Ops:
  32.8 8.9 %copy-start.10 = (bf16[768,768]{1,0:T(8,128)(2,1)S(1)}, bf16[768,768]{1,0:T(8,128)(2,1)}, u32[]{:S(2)}) copy-start(bf16[768,768]{1,0:T(8,128)(2,1)} %get-tuple-element.41) | copy-start | bytes 3538948
  86.0 3.4 %copy-start.15 = (bf16[768,1024]{1,0:T(8,128)(2,1)S(1)}, bf16[768,1024]{1,0:T(8,128)(2,1)}, u32[]{:S(2)}) copy-start(bf16[768,1024]{1,0:T(8,128)(2,1)} %get-tuple-element.46) | copy-start | bytes 4718596
  86.0 3.4 %copy-start.17 = (bf16[768,768]{1,0:T(8,128)(2,1)S(1)}, bf16[768,768]{1,0:T(8,128)(2,1)}, u32[]{:S(2)}) copy-start(bf16[768,768]{1,0:T(8,128)(2,1)} %get-tuple-element.45) | copy-start | bytes 3538948
  86.0 3.4 %copy-start.18 = (f32[768]{0:T(1024)S(1)}, f32[768]{0:T(1024)}, u32[]{:S(2)}) copy-start(f32[768]{0:T(1024)} %param.31) | copy-start | bytes 9220
  93.3 2.5 %copy-start.14 = (bf16[768,1024]{1,0:T(8,128)(2,1)S(1)}, bf16[768,1024]{1,0:T(8,128)(2,1)}, u32[]{:S(2)}) copy-start(bf16[768,1024]{1,0:T(8,128)(2,1)} %get-tuple-element.47) | copy-start | bytes 4718596
  98.3 2.5 %copy-start.16 = (bf16[768,768]{1,0:T(8,128)(2,1)S(1)}, bf16[768,768]{1,0:T(8,128)(2,1)}, u32[]{:S(2)}) copy-start(bf16[768,768]{1,0:T(8,128)(2,1)} %get-tuple-element.44) | copy-start | bytes 3538948
  171.3 13.6 %copy-start.1 = (f32[192,1024]{1,0:T(8,128)S(1)}, f32[192,1024]{1,0:T(8,128)}, u32[]{:S(2)}) copy-start(f32[192,1024]{1,0:T(8,128)} %get-tuple-element.57.gx_ref) | copy-start | bytes 2359300
  181.9 3.3 %copy-start = (f32[192,1024]{1,0:T(8,128)S(1)}, f32[192,1024]{1,0:T(8,128)}, u32[]{:S(2)}) copy-start(f32[192,1024]{1,0:T(8,128)} %cot_ref.3) | copy-start | bytes 2359300
  181.9 4.2 %copy-start.3 = (bf16[192,1024]{1,0:T(8,128)(2,1)S(1)}, bf16[192,1024]{1,0:T(8,128)(2,1)}, u32[]{:S(2)}) copy-start(bf16[192,1024]{1,0:T(8,128)(2,1)} %get-tuple-element.53) | copy-start | bytes 1179652
  181.9 4.2 %copy-start.7 = (bf16[192,1024]{1,0:T(8,128)(2,1)S(1)}, bf16[192,1024]{1,0:T(8,128)(2,1)}, u32[]{:S(2)}) copy-start(bf16[192,1024]{1,0:T(8,128)(2,1)} %get-tuple-element.54) | copy-start | bytes 1179652
  184.9 1.2 copy-start.2
  186.2 1.0 copy-start.12
  189.7 1.0 copy-start.6
  192.8 1.4 copy-start.11
  193.0 1.9 copy-start.13
  239.1 7.1 %copy-start.4 = (f32[192,1024]{1,0:T(8,128)S(1)}, f32[192,1024]{1,0:T(8,128)}, u32[]{:S(2)}) copy-start(f32[192,1024]{1,0:T(8,128)} %get-tuple-element.167) | copy-start | bytes 2359300
  239.1 8.0 %copy-start.5 = (f32[192,1024]{1,0:T(8,128)S(1)}, f32[192,1024]{1,0:T(8,128)}, u32[]{:S(2)}) copy-start(f32[192,1024]{1,0:T(8,128)} %get-tuple-element.168) | copy-start | bytes 2359300
  246.2 1.8 copy-start.9
  246.2 2.5 copy-start.8
